TPU v7x, 512 devices: a whole 4x8x8 slice. The times are simulated.
512 devices in a mesh: replica: 64 (over z_hi, y, core), tensor: 8 (over x, z_lo).
Axes of the slice: x: 4, y: 8, z: 8 (z_hi: 4, z_lo: 2; z = z_hi * 2 + z_lo), core: 2. Of those that a mesh axis runs over, the one named last changes fastest.
Arguments:
- weights: bfloat16 [3, 64, 224, 13824], P(None, 'replica', None, 'tensor'), may hold values from -6 to 6
- vectors: float32 [3, 64, 8, 13824], P(None, 'replica', None, 'tensor'), may hold values from -6 to 6
Outputs:
- new_weights: bfloat16 [3, 64, 224, 13824], P(None, 'replica', None, 'tensor')
- new_vectors: float32 [3, 64, 8, 13824], P(None, 'replica', None, 'tensor')
All inputs are finite; a program needn't handle non-finite values.
Results may differ from a plain program's by a relative error of at most 0.0049.
Values may be sent and summed in bfloat16 or wider, within the bound.
No kernel may reach another device: no remote copies, remote signals or barrier semaphores. Data moves between devices by JAX's collectives and lax.ppermute only.
A program may use at most 64 MiB of HBM per device.

v0:
```python
import jax
import jax.numpy as jnp
from jax import lax
from jax.sharding import PartitionSpec as P


def shifted(value, axis, steps):
    count = lax.axis_size(axis)
    pairs = [(source, (source + steps) % count) for source in range(count)]
    return lax.ppermute(value, axis, pairs)


def edge_differences(summed, rank_count):
    upper_half = summed[:, :rank_count]
    lower_half = summed[:, rank_count:]
    from_right = shifted(lower_half, "replica", -1)
    from_left = shifted(upper_half, "replica", 1)
    return jnp.stack([upper_half - from_right, from_left - lower_half], 1)


def orthonormal(gram_block, differences):
    lower = jnp.linalg.cholesky(gram_block)
    return lax.linalg.triangular_solve(lower, differences, left_side=True, lower=True)


def shards(weights, vectors):
    highest = lax.Precision.HIGHEST
    window = weights[:, 0]
    rank_count = vectors.shape[2]
    mat_count = window.shape[0]
    row_count = window.shape[1]
    own_vectors = vectors[:, 0].astype(jnp.bfloat16)
    left_vectors = shifted(own_vectors, "replica", 1)
    both_vectors = jnp.concatenate([own_vectors, left_vectors], 1)
    partial_value = jnp.einsum(
        "mkc,mrc->mkr", both_vectors, window, preferred_element_type=jnp.float32
    )
    summed = lax.psum(partial_value, "tensor")
    differences = edge_differences(summed, rank_count)
    gram_block = jnp.einsum("mekn,mejn->mekj", differences, differences, precision=highest)
    bases_full = orthonormal(gram_block, differences)
    bases_b = bases_full.astype(jnp.bfloat16).reshape(mat_count, 2 * rank_count, row_count)
    products = jnp.einsum("mkr,mrc->mkc", bases_b, window, preferred_element_type=jnp.float32)
    from_right = shifted(products[:, rank_count:].astype(jnp.bfloat16), "replica", -1).astype(
        jnp.float32
    )
    new_right = products[:, :rank_count] - from_right
    from_left = shifted(products[:, :rank_count].astype(jnp.bfloat16), "replica", 1).astype(
        jnp.float32
    )
    new_left = from_left - products[:, rank_count:]
    signed_bases = jnp.concatenate([bases_full[:, 0], -bases_full[:, 1]], 1)
    factors = jnp.concatenate([new_right, new_left], 1)
    correction = jnp.einsum("mkr,mkc->mrc", signed_bases, factors, precision=highest)
    updated = (window.astype(jnp.float32) - 0.5 * correction).astype(jnp.bfloat16)
    return (updated[:, None], new_right[:, None])


def solution(mesh):
    placed = (P(None, "replica", None, "tensor"), P(None, "replica", None, "tensor"))
    return jax.shard_map(
        shards,
        mesh=mesh,
        in_specs=placed,
        out_specs=(P(None, "replica", None, "tensor"), P(None, "replica", None, "tensor")),
        check_vma=False,
    )
```

profile of v0, /device:TPU:6, one launch (start us, length us, event | category | flops | bytes accessed | tf_op | source)
XLA Modules:
  0.0 91.5 jit_solution(10401001419555073672)
XLA Ops:
  0.6 0.0 copy-start
  0.6 1.1 %fusion.11 = bf16[3,8,1728]{2,1,0:T(8,128)(2,1)S(1)} fusion(f32[3,1,8,1728]{3,2,1,0:T(8,128)} %param.3), kind=kLoop, calls=%fused_computation.17 | loop fusion | flops 41472 | bytes 248832 | tf_op jit(solution)/shard_map/convert_element_type | solution.py:32
  1.7 1.9 %collective-permute-start = (bf16[3,8,1728]{2,1,0:T(8,128)(2,1)S(1)}, bf16[3,8,1728]{2,1,0:T(8,128)(2,1)S(1)}, u32[]{:S(2)}, u32[]{:S(2)}) collective-permute-start(bf16[3,8,1728]{2,1,0:T(8,128)(2,1)S(1)} %fusion.11), channel_id=1, source_target_pairs={{0,8},{8,16},{16,24},{24,32},{32,40},{40,48},{48,56},{56,64},{64,7... | collective-permute-start | bytes 248840 | tf_op jit(solution)/shard_map/ppermute | solution.py:10
  3.7 14.4 %collective-permute-done = bf16[3,8,1728]{2,1,0:T(8,128)(2,1)S(1)} collective-permute-done((bf16[3,8,1728]{2,1,0:T(8,128)(2,1)S(1)}, bf16[3,8,1728]{2,1,0:T(8,128)(2,1)S(1)}, u32[]{:S(2)}, u32[]{:S(2)}) %collective-permute-start) | collective-permute-done | bytes 82976 | tf_op jit(solution)/shard_map/ppermute | solution.py:10
  18.1 2.4 %fusion.3 = f32[3,16,224]{2,1,0:T(8,128)S(1)} fusion(bf16[3,1,224,1728]{3,2,1,0:T(8,128)(2,1)} %param.2, bf16[3,8,1728]{2,1,0:T(8,128)(2,1)S(1)} %collective-permute-done, bf16[3,8,1728]{2,1,0:T(8,128)(2,1)S(1)} %fusion.11), kind=kOutput, calls=%fused_computation.4 | convolution fusion | flops 37490688 | bytes 2531328 | tf_op jit(solution)/shard_map/mkc,mrc->mkr/dot_general | solution.py:35
  20.5 32.9 %psum.7 = f32[3,16,224]{2,1,0:T(8,128)S(1)} all-reduce(f32[3,16,224]{2,1,0:T(8,128)S(1)} %fusion.3), channel_id=1, replica_groups=mesh['replica'=64,'tensor'=8] {'tensor'}, use_global_device_ids=true, to_apply=%region_0.0 | all-reduce | flops 10752 | bytes 86016 | tf_op jit(solution)/shard_map/psum | solution.py:38
  53.4 1.9 %collective-permute-start.1 = (f32[3,8,224]{2,1,0:T(8,128)S(1)}, f32[3,8,224]{2,1,0:T(8,128)S(1)}, u32[]{:S(2)}, u32[]{:S(2)}) collective-permute-start(f32[3,8,224]{2,1,0:T(8,128)S(1)} %get-tuple-element.16), channel_id=1, source_target_pairs={{0,504},{8,0},{16,8},{24,16},{32,24},{40,32},{48,40},{56,48},{64,5... | collective-permute-start | bytes 64520 | tf_op jit(solution)/shard_map/ppermute | solution.py:10
  55.3 2.4 %collective-permute-start.2 = (f32[3,8,224]{2,1,0:T(8,128)S(1)}, f32[3,8,224]{2,1,0:T(8,128)S(1)}, u32[]{:S(2)}, u32[]{:S(2)}) collective-permute-start(f32[3,8,224]{2,1,0:T(8,128)S(1)} %get-tuple-element.17), channel_id=1, source_target_pairs={{0,8},{8,16},{16,24},{24,32},{32,40},{40,48},{48,56},{56,64},{64,7... | collective-permute-start | bytes 64520 | tf_op jit(solution)/shard_map/ppermute | solution.py:10
  57.7 0.0 collective-permute-done.1
  57.7 6.9 %collective-permute-done.2 = f32[3,8,224]{2,1,0:T(8,128)S(1)} collective-permute-done((f32[3,8,224]{2,1,0:T(8,128)S(1)}, f32[3,8,224]{2,1,0:T(8,128)S(1)}, u32[]{:S(2)}, u32[]{:S(2)}) %collective-permute-start.2) | collective-permute-done | bytes 21536 | tf_op jit(solution)/shard_map/ppermute | solution.py:10
  64.7 0.2 fusion.17
  64.8 0.1 copy.26
  64.9 4.4 %custom-call.7 = f32[3,2,8,8]{3,2,1,0:T(8,128)S(1)} custom-call(f32[3,2,8,8]{3,2,1,0:T(8,128)S(1)} %fusion.22), custom_call_target="Cholesky" | custom-call | tf_op jit(solution)/shard_map/jit(cholesky)/cholesky | solution.py:22
  69.3 0.1 select_reduce_fusion
  69.4 0.1 compare_reduce_fusion
  69.5 0.1 select_bitcast_fusion
  69.6 3.8 %custom-call.8 = f32[3,2,1,8,8]{3,4,2,1,0:T(8,128)S(1)} custom-call(f32[3,2,1,8,8]{4,3,2,1,0:T(8,128)S(1)} %select_bitcast_fusion), custom_call_target="InvertDiagBlocksLowerTriangular" | custom-call | tf_op jit(solution)/shard_map/triangular_solve | solution.py:23
  73.4 0.3 fusion.15
  73.7 0.4 fusion.1
  74.1 1.9 %collective-permute-start.3 = (bf16[3,8,1728]{2,1,0:T(8,128)(2,1)S(1)}, bf16[3,8,1728]{2,1,0:T(8,128)(2,1)S(1)}, u32[]{:S(2)}, u32[]{:S(2)}) collective-permute-start(bf16[3,8,1728]{2,1,0:T(8,128)(2,1)S(1)} %get-tuple-element.10), channel_id=1, source_target_pairs={{0,504},{8,0},{16,8},{24,16},{32,24},{40,32},{48,40},{56,48},{64,5... | collective-permute-start | bytes 248840 | tf_op jit(solution)/shard_map/ppermute | solution.py:10
  76.0 2.4 %collective-permute-start.4 = (bf16[3,8,1728]{2,1,0:T(8,128)(2,1)S(1)}, bf16[3,8,1728]{2,1,0:T(8,128)(2,1)S(1)}, u32[]{:S(2)}, u32[]{:S(2)}) collective-permute-start(bf16[3,8,1728]{2,1,0:T(8,128)(2,1)S(1)} %get-tuple-element.11), channel_id=1, source_target_pairs={{0,8},{8,16},{16,24},{24,32},{32,40},{40,48},{48,56},{56,64},{64,7... | collective-permute-start | bytes 248840 | tf_op jit(solution)/shard_map/ppermute | solution.py:10
  78.5 7.6 %collective-permute-done.4 = bf16[3,8,1728]{2,1,0:T(8,128)(2,1)S(1)} collective-permute-done((bf16[3,8,1728]{2,1,0:T(8,128)(2,1)S(1)}, bf16[3,8,1728]{2,1,0:T(8,128)(2,1)S(1)}, u32[]{:S(2)}, u32[]{:S(2)}) %collective-permute-start.4) | collective-permute-done | bytes 82976 | tf_op jit(solution)/shard_map/ppermute | solution.py:10
  86.1 0.0 copy-start.1
  86.1 5.4 %fusion = bf16[3,1,224,1728]{3,2,1,0:T(8,128)(2,1)} fusion(bf16[3,1,224,1728]{3,2,1,0:T(8,128)(2,1)S(1)} %copy-done, f32[3,8,1728]{2,1,0:T(8,128)S(1)} %get-tuple-element.9, f32[3,8,1728]{2,1,0:T(8,128)S(1)} %get-tuple-element.8, f32[3,8,224]{2,1,0:T(8,128)S(1)} %get-tuple-element.13, f32[3,8,224]{2,1,0:T(8,128)S(1)} %get-tuple-element.12), kind=kOutput, calls=%fused_computation.1 | convolution fusion | flops 227692032 | bytes 5019648 | tf_op jit(solution)/shard_map/mkr,mkc->mrc/dot_general | solution.py:54
  (11 shorter events, 0.1 us)
Async XLA Ops:
  0.6 73.0 %copy-start = (bf16[3,1,224,1728]{3,2,1,0:T(8,128)(2,1)S(1)}, bf16[3,1,224,1728]{3,2,1,0:T(8,128)(2,1)}, u32[]{:S(2)}) copy-start(bf16[3,1,224,1728]{3,2,1,0:T(8,128)(2,1)} %param.2) | copy-start | bytes 6967300
  1.7 16.4 %collective-permute-start = (bf16[3,8,1728]{2,1,0:T(8,128)(2,1)S(1)}, bf16[3,8,1728]{2,1,0:T(8,128)(2,1)S(1)}, u32[]{:S(2)}, u32[]{:S(2)}) collective-permute-start(bf16[3,8,1728]{2,1,0:T(8,128)(2,1)S(1)} %fusion.11), channel_id=1, source_target_pairs={{0,8},{8,16},{16,24},{24,32},{32,40},{40,48},{48,56},{56,64},{64,7... | collective-permute-start | bytes 248840 | tf_op jit(solution)/shard_map/ppermute | solution.py:10
  53.4 4.4 %collective-permute-start.1 = (f32[3,8,224]{2,1,0:T(8,128)S(1)}, f32[3,8,224]{2,1,0:T(8,128)S(1)}, u32[]{:S(2)}, u32[]{:S(2)}) collective-permute-start(f32[3,8,224]{2,1,0:T(8,128)S(1)} %get-tuple-element.16), channel_id=1, source_target_pairs={{0,504},{8,0},{16,8},{24,16},{32,24},{40,32},{48,40},{56,48},{64,5... | collective-permute-start | bytes 64520 | tf_op jit(solution)/shard_map/ppermute | solution.py:10
  55.3 9.4 %collective-permute-start.2 = (f32[3,8,224]{2,1,0:T(8,128)S(1)}, f32[3,8,224]{2,1,0:T(8,128)S(1)}, u32[]{:S(2)}, u32[]{:S(2)}) collective-permute-start(f32[3,8,224]{2,1,0:T(8,128)S(1)} %get-tuple-element.17), channel_id=1, source_target_pairs={{0,8},{8,16},{16,24},{24,32},{32,40},{40,48},{48,56},{56,64},{64,7... | collective-permute-start | bytes 64520 | tf_op jit(solution)/shard_map/ppermute | solution.py:10
  74.1 4.4 %collective-permute-start.3 = (bf16[3,8,1728]{2,1,0:T(8,128)(2,1)S(1)}, bf16[3,8,1728]{2,1,0:T(8,128)(2,1)S(1)}, u32[]{:S(2)}, u32[]{:S(2)}) collective-permute-start(bf16[3,8,1728]{2,1,0:T(8,128)(2,1)S(1)} %get-tuple-element.10), channel_id=1, source_target_pairs={{0,504},{8,0},{16,8},{24,16},{32,24},{40,32},{48,40},{56,48},{64,5... | collective-permute-start | bytes 248840 | tf_op jit(solution)/shard_map/ppermute | solution.py:10
  76.0 10.0 %collective-permute-start.4 = (bf16[3,8,1728]{2,1,0:T(8,128)(2,1)S(1)}, bf16[3,8,1728]{2,1,0:T(8,128)(2,1)S(1)}, u32[]{:S(2)}, u32[]{:S(2)}) collective-permute-start(bf16[3,8,1728]{2,1,0:T(8,128)(2,1)S(1)} %get-tuple-element.11), channel_id=1, source_target_pairs={{0,8},{8,16},{16,24},{24,32},{32,40},{40,48},{48,56},{56,64},{64,7... | collective-permute-start | bytes 248840 | tf_op jit(solution)/shard_map/ppermute | solution.py:10
  86.1 5.4 %copy-start.1 = (f32[3,8,1728]{2,1,0:T(8,128)}, f32[3,8,1728]{2,1,0:T(8,128)S(1)}, u32[]{:S(2)}) copy-start(f32[3,8,1728]{2,1,0:T(8,128)S(1)} %get-tuple-element.8) | copy-start | bytes 497668
where the time goes:
time: 91.8 us; the launch traced here: 91.5 us
  blocking collectives  32.9 us (36%)
  waiting for transfers between devices  28.9 us (31%)
  starting transfers between devices  10.6 us (12%)
  other arithmetic  9.59 us (10%)
  matrix products  8.71 us (9%)
    psum x1, blocking collectives, shards(): summed = lax.psum(partial_value, 'tensor')  32.9 us
    ppermute x5, waiting for transfers between devices, shifted(): return lax.ppermute(value, axis, pairs)  28.9 us
    ppermute x5, starting transfers between devices, shifted(): return lax.ppermute(value, axis, pairs)  10.6 us
    dot_general x1, matrix products, shards(): jnp.einsum('mkr,mkc->mrc', signed_bases, factors, precision=highest)  5.4 us
    another operation x4, other arithmetic, orthonormal(): lower = jnp.linalg.cholesky(gram_block)  4.6 us
    another operation x3, other arithmetic, orthonormal(): lax.linalg.triangular_solve(lower, differences, left_side=True, lower=True)  3.84 us
    dot_general x1, matrix products, shards(): jnp.einsum('mkc,mrc->mkr', both_vectors, window, preferred_element_type=j...  2.42 us
  transfers between devices with their start and end apart: 5, of which 3 were waited for; matrix products, arithmetic and copies ran while one was open for 0% of the time, Pallas kernels for 0%

commit v1 on v0

v1 whole, which is shorter than its diff:
```python
import functools

import jax
import jax.numpy as jnp
from jax import lax
from jax.experimental import pallas as pl
from jax.experimental.pallas import tpu as pltpu
from jax.sharding import PartitionSpec as P

LANES = 128
ROWS_BY_ROWS = (((1,), (1,)), ((), ()))
IN_VMEM = pl.BlockSpec(memory_space=pltpu.VMEM)


def shifted(value, axis, steps):
    count = lax.axis_size(axis)
    pairs = [(source, (source + steps) % count) for source in range(count)]
    return lax.ppermute(value, axis, pairs)


def padded(size):
    return -(-size // LANES) * LANES


def images_of(vectors_ref, window_ref, mat):
    return lax.dot_general(
        vectors_ref[mat].astype(jnp.bfloat16),
        window_ref[mat],
        ROWS_BY_ROWS,
        preferred_element_type=jnp.float32,
    )


def own_images_kernel(vectors_ref, window_ref, images_ref):
    mats, rank, _ = vectors_ref.shape
    for mat in range(mats):
        images_ref[mat * rank : (mat + 1) * rank] = images_of(vectors_ref, window_ref, mat)


def differences_kernel(vectors_ref, images_ref, window_ref, differences_ref):
    mats, rank, _ = vectors_ref.shape
    for mat in range(mats):
        rows = slice(mat * rank, (mat + 1) * rank)
        differences_ref[rows] = images_ref[rows] - images_of(vectors_ref, window_ref, mat)


def orthonormal_rows(gram, images, rank):
    mats = gram.shape[0] // rank
    grams = [gram[mat * rank : (mat + 1) * rank] for mat in range(mats)]
    rows = [images[mat * rank : (mat + 1) * rank] for mat in range(mats)]
    place = lax.broadcasted_iota(jnp.int32, (rank, 1), 0)
    pivots = [jnp.ones((rank, 1), jnp.float32) for _ in range(mats)]
    for step in range(rank):
        for mat in range(mats):
            column = grams[mat][:, mat * rank + step : mat * rank + step + 1]
            pivot = column[step : step + 1]
            pivots[mat] = jnp.where(place == step, pivot, pivots[mat])
            if step < rank - 1:
                factor = jnp.where(place > step, column / pivot, 0.0)
                rows[mat] = rows[mat] - factor * rows[mat][step : step + 1]
                grams[mat] = grams[mat] - factor * grams[mat][step : step + 1]
    return jnp.concatenate([row / jnp.sqrt(pivot) for row, pivot in zip(rows, pivots)], 0)


def column_products(basis, window_ref, mats):
    rank = basis.shape[0] // mats
    return [
        jnp.dot(
            basis[mat * rank : (mat + 1) * rank].astype(jnp.bfloat16),
            window_ref[mat],
            preferred_element_type=jnp.float32,
        )
        for mat in range(mats)
    ]


def basis_kernel(parts_ref, window_ref, message_ref, basis_ref):
    mats, row_count, columns = window_ref.shape
    images = jnp.sum(parts_ref[...], 0)
    gram = lax.dot_general(
        images, images, ROWS_BY_ROWS, precision=lax.Precision.HIGHEST, preferred_element_type=jnp.float32
    )
    basis = orthonormal_rows(gram, images, images.shape[0] // mats)
    basis_ref[...] = basis
    high = basis.astype(jnp.bfloat16)
    low = (basis - high.astype(jnp.float32)).astype(jnp.bfloat16)
    start = padded(columns)
    message_ref[:, start : start + row_count] = high
    start += padded(row_count)
    message_ref[:, start : start + row_count] = low
    products = jnp.concatenate(column_products(basis, window_ref, mats), 0)
    message_ref[:, :columns] = products.astype(jnp.bfloat16)


def factors_kernel(message_ref, window_ref, factors_ref, rounded_ref):
    mats, row_count, columns = window_ref.shape
    start = padded(columns)
    high = message_ref[:, start : start + row_count].astype(jnp.float32)
    products = jnp.concatenate(column_products(high, window_ref, mats), 0)
    factors = products - message_ref[:, :columns].astype(jnp.float32)
    factors_ref[...] = factors
    rounded_ref[...] = factors.astype(jnp.bfloat16)


def split(value):
    high = value.astype(jnp.bfloat16).astype(jnp.float32)
    return high, value - high


def left_kernel(message_ref, basis_ref, left_ref):
    mats, row_count, _ = left_ref.shape
    rank = basis_ref.shape[0] // mats
    start = message_ref.shape[1] - 2 * padded(row_count)
    upper_high = -0.5 * message_ref[:, start : start + row_count].astype(jnp.float32)
    start += padded(row_count)
    upper_low = -0.5 * message_ref[:, start : start + row_count].astype(jnp.float32)
    lower_high, lower_low = split(0.5 * basis_ref[...])
    for mat in range(mats):
        rows = slice(mat * rank, (mat + 1) * rank)
        parts = [upper_high[rows], upper_low[rows], upper_high[rows], lower_high[rows], lower_low[rows]]
        left_ref[mat] = jnp.concatenate(parts, 0).T.astype(jnp.bfloat16)


def update_kernel(left_ref, factors_ref, lower_ref, window_ref, updated_ref, held_ref, sems):
    mats, _, columns = window_ref.shape
    rank = factors_ref.shape[0] // mats
    width = 2 * LANES
    copies = []
    for mat in range(mats):
        rows = slice(mat * rank, (mat + 1) * rank)
        for start in range(0, columns, width):
            stop = min(start + width, columns)
            high, low = split(factors_ref[rows, start:stop])
            lower = lower_ref[:, start:stop].astype(jnp.float32)[rows]
            right = jnp.concatenate([high, high, low, lower, lower], 0).astype(jnp.bfloat16)
            change = jnp.dot(left_ref[mat], right, preferred_element_type=jnp.float32)
            held_ref[mat, :, start:stop] = (
                window_ref[mat, :, start:stop].astype(jnp.float32) + change
            ).astype(jnp.bfloat16)
        copies.append(pltpu.make_async_copy(held_ref.at[mat], updated_ref.at[mat, 0], sems.at[mat]))
        copies[-1].start()
    for copy in copies:
        copy.wait()


def call(kernel, outs, in_count, flops, **more):
    return pl.pallas_call(
        kernel,
        out_shape=outs,
        in_specs=[IN_VMEM] * in_count,
        cost_estimate=pl.CostEstimate(flops=flops, bytes_accessed=1 << 20, transcendentals=0),
        compiler_params=pltpu.CompilerParams(vmem_limit_bytes=24 << 20),
        **more,
    )


def shards(weights, vectors):
    window = weights[:, 0]
    own_vectors = vectors[:, 0]
    mats, rank, columns = own_vectors.shape
    row_count = window.shape[1]
    stacked = mats * rank
    product_flops = 2 * stacked * row_count * columns
    f32, bf16 = jnp.float32, jnp.bfloat16
    shape = jax.ShapeDtypeStruct
    out = IN_VMEM

    left_vectors = shifted(own_vectors, "replica", 1)
    own_images = call(own_images_kernel, shape((stacked, row_count), f32), 2, product_flops, out_specs=out)(
        own_vectors, window
    )
    left_images = shifted(own_images, "replica", 1)
    partial_differences = call(
        differences_kernel, shape((stacked, row_count), f32), 3, product_flops, out_specs=out
    )(left_vectors, left_images, window)
    group = lax.axis_size("tensor")
    parts = lax.all_to_all(
        jnp.broadcast_to(partial_differences[None], (group, stacked, row_count)), "tensor", 0, 0
    )
    message_width = padded(columns) + 2 * padded(row_count)
    message, lower_basis = call(
        basis_kernel,
        (shape((stacked, message_width), bf16), shape((stacked, row_count), f32)),
        2,
        product_flops,
        out_specs=(out, out),
    )(parts, window)
    message = shifted(message, "replica", -1)
    factors, rounded = call(
        factors_kernel,
        (shape((stacked, columns), f32), shape((stacked, columns), bf16)),
        2,
        product_flops,
        out_specs=(out, out),
    )(message, window)
    lower_factors = shifted(rounded, "replica", 1)
    left = call(left_kernel, shape((mats, row_count, 5 * rank), bf16), 2, product_flops // 4, out_specs=out)(
        message, lower_basis
    )
    updated = call(
        update_kernel,
        shape((mats, 1, row_count, columns), bf16),
        4,
        5 * product_flops,
        out_specs=pl.BlockSpec(memory_space=pl.ANY),
        scratch_shapes=[pltpu.VMEM((mats, row_count, columns), bf16), pltpu.SemaphoreType.DMA((mats,))],
    )(left, factors, lower_factors, window)
    return (updated, factors.reshape(mats, 1, rank, columns))


def solution(mesh):
    placed = (P(None, "replica", None, "tensor"), P(None, "replica", None, "tensor"))
    return jax.shard_map(
        shards,
        mesh=mesh,
        in_specs=placed,
        out_specs=(P(None, "replica", None, "tensor"), P(None, "replica", None, "tensor")),
        check_vma=False,
    )
```

time: 91.8 us -> 53.7 us (0.58)
  the two profiles are of different devices: /device:TPU:6 before, /device:TPU:2 now
where the time goes in v1:
time: 53.7 us; the launch traced here: 53.3 us
  waiting for transfers between devices  23.1 us (43%)
  blocking collectives  10.7 us (20%)
  starting transfers between devices  9.37 us (17%)
  Pallas kernels  5.87 us (11%)
  local copies, waits for them, and re-layouts  3.56 us (7%)
  between operations  0.69 us (1%)
    ppermute x4, waiting for transfers between devices, shifted(): return lax.ppermute(value, axis, pairs)  23.1 us
    all_to_all x1, blocking collectives, shards(): lax.all_to_all(jnp.broadcast_to(partial_differences[None], (group, stacke...  10.7 us
    ppermute x4, starting transfers between devices, shifted(): return lax.ppermute(value, axis, pairs)  9.37 us
    unnamed x8, local copies, waits for them, and re-layouts  3.51 us
    pallas_call x1, Pallas kernels, shards(): call(update_kernel, shape((mats, 1, row_count, columns), bf16), 4, 5 * pr...  1.78 us
    pallas_call x1, Pallas kernels, shards(): call(basis_kernel, (shape((stacked, message_width), bf16), shape((stacked...  1.37 us
    pallas_call x1, Pallas kernels, shards(): call(factors_kernel, (shape((stacked, columns), f32), shape((stacked, col...  1.11 us
  transfers between devices with their start and end apart: 4, of which 3 were waited for; matrix products, arithmetic and copies ran while one was open for 0% of the time, Pallas kernels for 2%

profile of v1, /device:TPU:2, one launch (start us, length us, event | category | flops | bytes accessed | tf_op | source)
XLA Modules:
  0.0 53.3 jit_solution(16561733345814834602)
XLA Ops:
  0.6 1.9 %collective-permute-start = (f32[3,8,1728]{2,1,0:T(8,128)}, f32[3,8,1728]{2,1,0:T(8,128)S(1)}, u32[]{:S(2)}, u32[]{:S(2)}) collective-permute-start(f32[3,8,1728]{2,1,0:T(8,128)} %bitcast.11), channel_id=1, source_target_pairs={{0,8},{8,16},{16,24},{24,32},{32,40},{40,48},{48,56},{56,64},{64,7... | collective-permute-start | bytes 497672 | tf_op jit(solution)/shard_map/ppermute | solution.py:18
  2.6 0.0 copy-start
  2.6 1.7 %copy-done = bf16[3,1,224,1728]{3,2,1,0:T(8,128)(2,1)S(1)} copy-done((bf16[3,1,224,1728]{3,2,1,0:T(8,128)(2,1)S(1)}, bf16[3,1,224,1728]{3,2,1,0:T(8,128)(2,1)}, u32[]{:S(2)}) %copy-start) | copy-done | bytes 2322456
  4.2 0.0 copy-start.3
  4.2 0.9 %copy-done.3 = f32[3,1,8,1728]{3,2,1,0:T(8,128)S(1)} copy-done((f32[3,1,8,1728]{3,2,1,0:T(8,128)S(1)}, f32[3,1,8,1728]{3,2,1,0:T(8,128)}, u32[]{:S(2)}) %copy-start.3) | copy-done | bytes 165912
  5.2 0.0 copy-start.1
  5.2 0.7 %shard_map.41 = f32[24,224]{1,0:T(8,128)S(1)} custom-call(f32[3,8,1728]{2,1,0:T(8,128)S(1)} %bitcast.12, bf16[3,224,1728]{2,1,0:T(8,128)(2,1)S(1)} %bitcast.5), custom_call_target="tpu_custom_call" | custom-call | flops 18579456 | bytes 1048576 | tf_op jit(solution)/shard_map/pallas_call | solution.py:169
  5.9 3.6 %collective-permute-start.1 = (f32[24,224]{1,0:T(8,128)S(1)}, f32[24,224]{1,0:T(8,128)S(1)}, u32[]{:S(2)}, u32[]{:S(2)}) collective-permute-start(f32[24,224]{1,0:T(8,128)S(1)} %shard_map.41), channel_id=1, source_target_pairs={{0,8},{8,16},{16,24},{24,32},{32,40},{40,48},{48,56},{56,64},{64,7... | collective-permute-start | bytes 64520 | tf_op jit(solution)/shard_map/ppermute | solution.py:18
  9.5 11.5 %collective-permute-done.1.images_ref = f32[24,224]{1,0:T(8,128)S(1)} collective-permute-done((f32[24,224]{1,0:T(8,128)S(1)}, f32[24,224]{1,0:T(8,128)S(1)}, u32[]{:S(2)}, u32[]{:S(2)}) %collective-permute-start.1) | collective-permute-done | bytes 21536 | tf_op jit(solution)/shard_map/ppermute | solution.py:18
  21.0 0.0 collective-permute-done.vectors_ref
  21.0 0.0 copy-done.1
  21.0 0.7 %shard_map.42 = f32[24,224]{1,0:T(8,128)S(1)} custom-call(f32[3,8,1728]{2,1,0:T(8,128)S(1)} %collective-permute-done.vectors_ref, f32[24,224]{1,0:T(8,128)S(1)} %collective-permute-done.1.images_ref, bf16[3,224,1728]{2,1,0:T(8,128)(2,1)S(1)} %bitcast.6), custom_call_target="tpu_custom_call" | custom-call | flops 18579456 | bytes 1048576 | tf_op jit(solution)/shard_map/pallas_call | solution.py:173
  21.8 10.7 %all_to_all.5.parts_ref = f32[8,24,224]{2,1,0:T(8,128)S(1)} all-to-all(f32[8,24,224]{2,1,0:T(8,128)S(1)} %broadcast_in_dim.2), channel_id=1, replica_groups=mesh['replica'=64,'tensor'=8] {'tensor'}, dimensions={0} | all-to-all | bytes 344064 | tf_op jit(solution)/shard_map/all_to_all | solution.py:177
  32.5 1.4 %shard_map.43 = (bf16[24,2304]{1,0:T(8,128)(2,1)S(1)}, f32[24,224]{1,0:T(8,128)S(1)}) custom-call(f32[8,24,224]{2,1,0:T(8,128)S(1)} %all_to_all.5.parts_ref, bf16[3,224,1728]{2,1,0:T(8,128)(2,1)S(1)} %bitcast.7), custom_call_target="tpu_custom_call" | custom-call | flops 18579456 | bytes 1048576 | tf_op jit(solution)/shard_map/pallas_call | solution.py:181
  33.9 1.9 %collective-permute-start.2 = (bf16[24,2304]{1,0:T(8,128)(2,1)S(1)}, bf16[24,2304]{1,0:T(8,128)(2,1)S(1)}, u32[]{:S(2)}, u32[]{:S(2)}) collective-permute-start(bf16[24,2304]{1,0:T(8,128)(2,1)S(1)} %get-tuple-element.6), channel_id=1, source_target_pairs={{0,504},{8,0},{16,8},{24,16},{32,24},{40,32},{48,40},{56,48},{64,5... | collective-permute-start | bytes 331784 | tf_op jit(solution)/shard_map/ppermute | solution.py:18
  35.8 2.3 %collective-permute-done.2.message_ref = bf16[24,2304]{1,0:T(8,128)(2,1)S(1)} collective-permute-done((bf16[24,2304]{1,0:T(8,128)(2,1)S(1)}, bf16[24,2304]{1,0:T(8,128)(2,1)S(1)}, u32[]{:S(2)}, u32[]{:S(2)}) %collective-permute-start.2) | collective-permute-done | bytes 110624 | tf_op jit(solution)/shard_map/ppermute | solution.py:18
  38.1 1.1 %shard_map.45 = (f32[24,1728]{1,0:T(8,128)}, bf16[24,1728]{1,0:T(8,128)(2,1)S(1)}) custom-call(bf16[24,2304]{1,0:T(8,128)(2,1)S(1)} %collective-permute-done.2.message_ref, bf16[3,224,1728]{2,1,0:T(8,128)(2,1)S(1)} %bitcast.8), custom_call_target="tpu_custom_call" | custom-call | flops 18579456 | bytes 1048576 | tf_op jit(solution)/shard_map/pallas_call | solution.py:189
  39.2 1.9 %collective-permute-start.3 = (bf16[24,1728]{1,0:T(8,128)(2,1)S(1)}, bf16[24,1728]{1,0:T(8,128)(2,1)S(1)}, u32[]{:S(2)}, u32[]{:S(2)}) collective-permute-start(bf16[24,1728]{1,0:T(8,128)(2,1)S(1)} %get-tuple-element.9), channel_id=1, source_target_pairs={{0,8},{8,16},{16,24},{24,32},{32,40},{40,48},{48,56},{56,64},{64,7... | collective-permute-start | bytes 248840 | tf_op jit(solution)/shard_map/ppermute | solution.py:18
  41.1 0.1 shard_map.44.left_ref
  41.3 9.3 %collective-permute-done.3.lower_ref = bf16[24,1728]{1,0:T(8,128)(2,1)S(1)} collective-permute-done((bf16[24,1728]{1,0:T(8,128)(2,1)S(1)}, bf16[24,1728]{1,0:T(8,128)(2,1)S(1)}, u32[]{:S(2)}, u32[]{:S(2)}) %collective-permute-start.3) | collective-permute-done | bytes 82976 | tf_op jit(solution)/shard_map/ppermute | solution.py:18
  50.6 0.0 copy-start.2
  50.6 0.9 %copy-done.2 = f32[24,1728]{1,0:T(8,128)S(1)} copy-done((f32[24,1728]{1,0:T(8,128)S(1)}, f32[24,1728]{1,0:T(8,128)}, u32[]{:S(2)}) %copy-start.2) | copy-done | bytes 165912
  51.5 1.8 %shard_map.46 = bf16[3,1,224,1728]{3,2,1,0:T(8,128)(2,1)} custom-call(bf16[3,224,40]{2,1,0:T(8,128)(2,1)S(1)} %shard_map.44.left_ref, f32[24,1728]{1,0:T(8,128)S(1)} %copy-done.2, bf16[24,1728]{1,0:T(8,128)(2,1)S(1)} %collective-permute-done.3.lower_ref, bf16[3,224,1728]{2,1,0:T(8,128)(2,1)S(1)} %bitcast.9), custom_call_target="tpu_custom_call" | custom-call | flops 92897280 | bytes 1048576 | tf_op jit(solution)/shard_map/pallas_call | solution.py:200
  (1 shorter events, 0.0 us)
Async XLA Ops:
  0.6 20.3 %collective-permute-start = (f32[3,8,1728]{2,1,0:T(8,128)}, f32[3,8,1728]{2,1,0:T(8,128)S(1)}, u32[]{:S(2)}, u32[]{:S(2)}) collective-permute-start(f32[3,8,1728]{2,1,0:T(8,128)} %bitcast.11), channel_id=1, source_target_pairs={{0,8},{8,16},{16,24},{24,32},{32,40},{40,48},{48,56},{56,64},{64,7... | collective-permute-start | bytes 497672 | tf_op jit(solution)/shard_map/ppermute | solution.py:18
  2.6 1.7 %copy-start = (bf16[3,1,224,1728]{3,2,1,0:T(8,128)(2,1)S(1)}, bf16[3,1,224,1728]{3,2,1,0:T(8,128)(2,1)}, u32[]{:S(2)}) copy-start(bf16[3,1,224,1728]{3,2,1,0:T(8,128)(2,1)} %param.2) | copy-start | bytes 6967300
  4.2 0.9 %copy-start.3 = (f32[3,1,8,1728]{3,2,1,0:T(8,128)S(1)}, f32[3,1,8,1728]{3,2,1,0:T(8,128)}, u32[]{:S(2)}) copy-start(f32[3,1,8,1728]{3,2,1,0:T(8,128)} %param.3) | copy-start | bytes 497668
  5.2 15.8 %copy-start.1 = (bf16[3,1,224,1728]{3,2,1,0:T(8,128)(2,1)S(1)}, bf16[3,1,224,1728]{3,2,1,0:T(8,128)(2,1)}, u32[]{:S(2)}) copy-start(bf16[3,1,224,1728]{3,2,1,0:T(8,128)(2,1)} %param.2) | copy-start | bytes 6967300
  5.9 15.1 %collective-permute-start.1 = (f32[24,224]{1,0:T(8,128)S(1)}, f32[24,224]{1,0:T(8,128)S(1)}, u32[]{:S(2)}, u32[]{:S(2)}) collective-permute-start(f32[24,224]{1,0:T(8,128)S(1)} %shard_map.41), channel_id=1, source_target_pairs={{0,8},{8,16},{16,24},{24,32},{32,40},{40,48},{48,56},{56,64},{64,7... | collective-permute-start | bytes 64520 | tf_op jit(solution)/shard_map/ppermute | solution.py:18
  33.9 4.2 %collective-permute-start.2 = (bf16[24,2304]{1,0:T(8,128)(2,1)S(1)}, bf16[24,2304]{1,0:T(8,128)(2,1)S(1)}, u32[]{:S(2)}, u32[]{:S(2)}) collective-permute-start(bf16[24,2304]{1,0:T(8,128)(2,1)S(1)} %get-tuple-element.6), channel_id=1, source_target_pairs={{0,504},{8,0},{16,8},{24,16},{32,24},{40,32},{48,40},{56,48},{64,5... | collective-permute-start | bytes 331784 | tf_op jit(solution)/shard_map/ppermute | solution.py:18
  39.2 11.4 %collective-permute-start.3 = (bf16[24,1728]{1,0:T(8,128)(2,1)S(1)}, bf16[24,1728]{1,0:T(8,128)(2,1)S(1)}, u32[]{:S(2)}, u32[]{:S(2)}) collective-permute-start(bf16[24,1728]{1,0:T(8,128)(2,1)S(1)} %get-tuple-element.9), channel_id=1, source_target_pairs={{0,8},{8,16},{16,24},{24,32},{32,40},{40,48},{48,56},{56,64},{64,7... | collective-permute-start | bytes 248840 | tf_op jit(solution)/shard_map/ppermute | solution.py:18
  50.6 0.9 %copy-start.2 = (f32[24,1728]{1,0:T(8,128)S(1)}, f32[24,1728]{1,0:T(8,128)}, u32[]{:S(2)}) copy-start(f32[24,1728]{1,0:T(8,128)} %get-tuple-element.8.factors_ref) | copy-start | bytes 497668

commit v2 on v0

v2 whole, which is shorter than its diff:
```python
import functools

import jax
import jax.numpy as jnp
from jax import lax
from jax.experimental import pallas as pl
from jax.experimental.pallas import tpu as pltpu
from jax.sharding import PartitionSpec as P

LANES = 128
ROWS_BY_ROWS = (((1,), (1,)), ((), ()))
IN_VMEM = pl.BlockSpec(memory_space=pltpu.VMEM)


def shifted(value, axis, steps):
    count = lax.axis_size(axis)
    pairs = [(source, (source + steps) % count) for source in range(count)]
    return lax.ppermute(value, axis, pairs)


def padded(size):
    return -(-size // LANES) * LANES


def images_of(vectors_ref, window_ref, mat):
    return lax.dot_general(
        vectors_ref[mat], window_ref[mat], ROWS_BY_ROWS, preferred_element_type=jnp.float32
    )


def staging_kernel(vectors_hbm, window_hbm, vectors_ref, images_ref, window_ref, held_ref, sems):
    mats, rank, _ = vectors_ref.shape
    vectors_copy = pltpu.make_async_copy(vectors_hbm, held_ref, sems.at[mats])
    vectors_copy.start()
    copies = [
        pltpu.make_async_copy(window_hbm.at[mat], window_ref.at[mat], sems.at[mat]) for mat in range(mats)
    ]
    for copy in copies:
        copy.start()
    vectors_copy.wait()
    vectors_ref[...] = held_ref[...].astype(jnp.bfloat16)
    for mat, copy in enumerate(copies):
        copy.wait()
        images_ref[mat * rank : (mat + 1) * rank] = images_of(vectors_ref, window_ref, mat)


def images_kernel(vectors_ref, window_ref, images_ref):
    mats, rank, _ = vectors_ref.shape
    for mat in range(mats):
        images_ref[mat * rank : (mat + 1) * rank] = images_of(vectors_ref, window_ref, mat)


def orthonormal_rows(gram, images, rank):
    mats = gram.shape[0] // rank
    grams = [gram[mat * rank : (mat + 1) * rank] for mat in range(mats)]
    rows = [images[mat * rank : (mat + 1) * rank] for mat in range(mats)]
    place = lax.broadcasted_iota(jnp.int32, (rank, 1), 0)
    pivots = [jnp.ones((rank, 1), jnp.float32) for _ in range(mats)]
    for step in range(rank):
        for mat in range(mats):
            column = grams[mat][:, mat * rank + step : mat * rank + step + 1]
            pivot = column[step : step + 1]
            pivots[mat] = jnp.where(place == step, pivot, pivots[mat])
            if step < rank - 1:
                factor = jnp.where(place > step, column / pivot, 0.0)
                rows[mat] = rows[mat] - factor * rows[mat][step : step + 1]
                grams[mat] = grams[mat] - factor * grams[mat][step : step + 1]
    return jnp.concatenate([row / jnp.sqrt(pivot) for row, pivot in zip(rows, pivots)], 0)


def split(value):
    high = value.astype(jnp.bfloat16).astype(jnp.float32)
    return high, value - high


def basis_kernel(mats, parts_ref, basis_ref, message_ref):
    rank = parts_ref.shape[1] // mats
    row_count = parts_ref.shape[2]
    images = jnp.sum(parts_ref[...], 0)
    gram = lax.dot_general(
        images, images, ROWS_BY_ROWS, precision=lax.Precision.HIGHEST, preferred_element_type=jnp.float32
    )
    basis = orthonormal_rows(gram, images, rank)
    basis_ref[...] = basis
    high, low = split(basis)
    message_ref[:, :row_count] = high.astype(jnp.bfloat16)
    start = padded(row_count)
    message_ref[:, start : start + row_count] = low.astype(jnp.bfloat16)


def products_kernel(message_ref, window_ref, products_ref, rounded_ref):
    mats, row_count, _ = window_ref.shape
    rank = message_ref.shape[0] // mats
    basis = message_ref[:, :row_count].astype(jnp.float32)
    for mat in range(mats):
        rows = slice(mat * rank, (mat + 1) * rank)
        products_ref[rows] = jnp.dot(
            basis[rows].astype(jnp.bfloat16), window_ref[mat], preferred_element_type=jnp.float32
        )
    rounded_ref[...] = products_ref[...].astype(jnp.bfloat16)


def left_kernel(message_ref, basis_ref, left_ref):
    mats, row_count, _ = left_ref.shape
    rank = basis_ref.shape[0] // mats
    start = padded(row_count)
    upper_high = -0.5 * message_ref[:, :row_count].astype(jnp.float32)
    upper_low = -0.5 * message_ref[:, start : start + row_count].astype(jnp.float32)
    lower_high, lower_low = split(0.5 * basis_ref[...])
    for mat in range(mats):
        rows = slice(mat * rank, (mat + 1) * rank)
        parts = [upper_high[rows], upper_low[rows], upper_high[rows], lower_high[rows], lower_low[rows], lower_high[rows]]
        left_ref[mat] = jnp.concatenate(parts, 0).T.astype(jnp.bfloat16)


def update_kernel(
    left_ref, upper_ref, next_ref, lower_ref, previous_ref, window_ref, updated_ref, factors_ref, held_ref, sums_ref, sems
):
    mats, row_count, columns = window_ref.shape
    rank = upper_ref.shape[0] // mats
    width = 2 * LANES
    pieces = sems.shape[1] - 1
    piece = row_count // pieces
    copies = []
    for mat in range(mats):
        rows = slice(mat * rank, (mat + 1) * rank)
        rights = []
        for start in range(0, columns, width):
            stop = min(start + width, columns)
            upper = upper_ref[rows, start:stop] - next_ref[:, start:stop].astype(jnp.float32)[rows]
            sums_ref[mat, 0, :, start:stop] = upper
            upper_high, upper_low = split(upper)
            lower = previous_ref[:, start:stop].astype(jnp.float32)[rows] - lower_ref[rows, start:stop]
            lower_high, lower_low = split(lower)
            parts = [upper_high, upper_high, upper_low, lower_high, lower_high, lower_low]
            rights.append((start, stop, jnp.concatenate(parts, 0).astype(jnp.bfloat16)))
        copies.append(pltpu.make_async_copy(sums_ref.at[mat], factors_ref.at[mat], sems.at[mat, pieces]))
        copies[-1].start()
        for index in range(pieces):
            own = slice(index * piece, (index + 1) * piece)
            left = left_ref[mat, own]
            for start, stop, right in rights:
                change = jnp.dot(left, right, preferred_element_type=jnp.float32)
                held_ref[mat, own, start:stop] = (
                    window_ref[mat, own, start:stop].astype(jnp.float32) + change
                ).astype(jnp.bfloat16)
            copies.append(
                pltpu.make_async_copy(held_ref.at[mat, own], updated_ref.at[mat, 0, own], sems.at[mat, index])
            )
            copies[-1].start()
    for copy in copies:
        copy.wait()


def call(kernel, outs, flops, in_specs=None, out_specs=None, **more):
    def run(*operands):
        return pl.pallas_call(
            kernel,
            out_shape=outs,
            in_specs=[IN_VMEM] * len(operands) if in_specs is None else in_specs,
            out_specs=jax.tree.map(lambda _: IN_VMEM, outs) if out_specs is None else out_specs,
            cost_estimate=pl.CostEstimate(flops=flops, bytes_accessed=1 << 20, transcendentals=0),
            compiler_params=pltpu.CompilerParams(vmem_limit_bytes=24 << 20),
            **more,
        )(*operands)

    return run


def shards(weights, vectors):
    window = weights[:, 0]
    own_vectors = vectors[:, 0]
    mats, rank, columns = own_vectors.shape
    row_count = window.shape[1]
    stacked = mats * rank
    flops = 2 * stacked * row_count * columns

    def whole(dtype, *dims):
        return jax.ShapeDtypeStruct(dims, dtype)

    f32, bf16 = jnp.float32, jnp.bfloat16
    images = whole(f32, stacked, row_count)
    rounded_images = whole(bf16, stacked, row_count)
    products = whole(f32, stacked, columns)
    rounded_products = whole(bf16, stacked, columns)

    vectors_b, own_images, window = call(
        staging_kernel,
        (whole(bf16, *own_vectors.shape), images, whole(bf16, *window.shape)),
        flops,
        in_specs=[pl.BlockSpec(memory_space=pltpu.HBM)] * 2,
        scratch_shapes=[pltpu.VMEM(own_vectors.shape, f32), pltpu.SemaphoreType.DMA((mats + 1,))],
    )(*(pltpu.with_memory_space_constraint(value, pltpu.HBM) for value in (own_vectors, window)))
    left_vectors = shifted(vectors_b, "replica", 1)
    left_images = shifted(own_images, "replica", 1)
    next_images = call(images_kernel, images, flops)(left_vectors, window)
    group = lax.axis_size("tensor")
    parts = lax.all_to_all(
        jnp.broadcast_to((left_images - next_images)[None], (group, stacked, row_count)), "tensor", 0, 0
    )
    lower_basis, message = call(
        functools.partial(basis_kernel, mats),
        (images, whole(bf16, stacked, padded(row_count) + row_count)),
        flops // 4,
    )(parts)
    upper_message = shifted(message, "replica", -1)
    column_products = call(products_kernel, (products, rounded_products), 400 * flops)
    upper_products, rounded_upper = column_products(upper_message, window)
    previous_products = shifted(rounded_upper, "replica", 1)
    message, _ = lax.optimization_barrier((message, rounded_upper))
    lower_products, rounded_lower = column_products(message, window)
    next_products = shifted(rounded_lower, "replica", -1)
    left = call(left_kernel, whole(bf16, mats, row_count, 6 * rank), flops // 4)(upper_message, lower_basis)
    pieces = 2 if row_count % 32 == 0 else 1
    updated, factors = call(
        update_kernel,
        (whole(bf16, mats, 1, row_count, columns), whole(f32, mats, 1, rank, columns)),
        4 * flops,
        out_specs=[pl.BlockSpec(memory_space=pl.ANY)] * 2,
        scratch_shapes=[
            pltpu.VMEM((mats, row_count, columns), bf16),
            pltpu.VMEM((mats, 1, rank, columns), f32),
            pltpu.SemaphoreType.DMA((mats, pieces + 1)),
        ],
    )(left, upper_products, next_products, lower_products, previous_products, window)
    return (updated, factors)


def solution(mesh):
    placed = (P(None, "replica", None, "tensor"), P(None, "replica", None, "tensor"))
    return jax.shard_map(
        shards,
        mesh=mesh,
        in_specs=placed,
        out_specs=(P(None, "replica", None, "tensor"), P(None, "replica", None, "tensor")),
        check_vma=False,
    )
```

time: 91.8 us -> 51.5 us (0.56)
  the two profiles are of different devices: /device:TPU:6 before, /device:TPU:185 now
where the time goes in v2:
time: 51.5 us; the launch traced here: 51.2 us
  starting transfers between devices  16.3 us (32%)
  waiting for transfers between devices  16.2 us (31%)
  blocking collectives  11 us (21%)
  Pallas kernels  7.04 us (14%)
  between operations  0.71 us (1%)
    ppermute x5, starting transfers between devices, shifted(): return lax.ppermute(value, axis, pairs)  16.3 us
    ppermute x5, waiting for transfers between devices, shifted(): return lax.ppermute(value, axis, pairs)  16.2 us
    all_to_all x1, blocking collectives, shards(): lax.all_to_all(jnp.broadcast_to((left_images - next_images)[None], (group...  11 us
    pallas_call x7, Pallas kernels, run(): pl.pallas_call(kernel, out_shape=outs, in_specs=[IN_VMEM] * len(operands)...  7.04 us
  transfers between devices with their start and end apart: 5, of which 3 were waited for; matrix products, arithmetic and copies ran while one was open for 0% of the time, Pallas kernels for 3%

profile of v2, /device:TPU:185, one launch (start us, length us, event | category | flops | bytes accessed | tf_op | source)
XLA Modules:
  0.0 51.2 jit_solution(9198709925629336743)
XLA Ops:
  0.6 2.7 %shard_map.41 = (bf16[3,8,1728]{2,1,0:T(8,128)(2,1)S(1)}, f32[24,224]{1,0:T(8,128)S(1)}, bf16[3,224,1728]{2,1,0:T(8,128)(2,1)S(1)}) custom-call(f32[3,8,1728]{2,1,0:T(8,128)} %bitcast.3, bf16[3,224,1728]{2,1,0:T(8,128)(2,1)} %bitcast.2), custom_call_target="tpu_custom_call" | custom-call | flops 18579456 | bytes 1048576 | tf_op jit(solution)/shard_map/pallas_call | solution.py:157
  3.3 6.8 %collective-permute-start.1 = (bf16[3,8,1728]{2,1,0:T(8,128)(2,1)S(1)}, bf16[3,8,1728]{2,1,0:T(8,128)(2,1)S(1)}, u32[]{:S(2)}, u32[]{:S(2)}) collective-permute-start(bf16[3,8,1728]{2,1,0:T(8,128)(2,1)S(1)} %get-tuple-element.13), channel_id=1, source_target_pairs={{0,8},{8,16},{16,24},{24,32},{32,40},{40,48},{48,56},{56,64},{64,7... | collective-permute-start | bytes 248840 | tf_op jit(solution)/shard_map/ppermute | solution.py:18
  10.1 1.9 %collective-permute-start = (f32[24,224]{1,0:T(8,128)S(1)}, f32[24,224]{1,0:T(8,128)S(1)}, u32[]{:S(2)}, u32[]{:S(2)}) collective-permute-start(f32[24,224]{1,0:T(8,128)S(1)} %get-tuple-element.12), channel_id=1, source_target_pairs={{0,8},{8,16},{16,24},{24,32},{32,40},{40,48},{48,56},{56,64},{64,7... | collective-permute-start | bytes 64520 | tf_op jit(solution)/shard_map/ppermute | solution.py:18
  12.0 0.0 collective-permute-done.1.vectors_ref
  12.1 0.7 %shard_map.42 = f32[24,224]{1,0:T(8,128)S(1)} custom-call(bf16[3,8,1728]{2,1,0:T(8,128)(2,1)S(1)} %collective-permute-done.1.vectors_ref, bf16[3,224,1728]{2,1,0:T(8,128)(2,1)S(1)} %get-tuple-element.14.window_ref), custom_call_target="tpu_custom_call" | custom-call | flops 18579456 | bytes 1048576 | tf_op jit(solution)/shard_map/pallas_call | solution.py:157
  12.8 0.4 collective-permute-done
  13.2 11.0 %all_to_all.5.parts_ref = f32[8,24,224]{2,1,0:T(8,128)S(1)} all-to-all(f32[8,24,224]{2,1,0:T(8,128)S(1)} %broadcast_in_dim.2), channel_id=1, replica_groups=mesh['replica'=64,'tensor'=8] {'tensor'}, dimensions={0} | all-to-all | bytes 344064 | tf_op jit(solution)/shard_map/all_to_all | solution.py:198
  24.2 0.8 %shard_map.43 = (f32[24,224]{1,0:T(8,128)S(1)}, bf16[24,480]{1,0:T(8,128)(2,1)S(1)}) custom-call(f32[8,24,224]{2,1,0:T(8,128)S(1)} %all_to_all.5.parts_ref), custom_call_target="tpu_custom_call" | custom-call | flops 4644864 | bytes 1048576 | tf_op jit(solution)/shard_map/pallas_call | solution.py:157
  25.0 3.2 %collective-permute-start.2 = (bf16[24,480]{1,0:T(8,128)(2,1)S(1)}, bf16[24,480]{1,0:T(8,128)(2,1)S(1)}, u32[]{:S(2)}, u32[]{:S(2)}) collective-permute-start(bf16[24,480]{1,0:T(8,128)(2,1)S(1)} %get-tuple-element.19.message_ref), channel_id=1, source_target_pairs={{0,504},{8,0},{16,8},{24,16},{32,24},{40,32},{48,40},{56,48},{64,5... | collective-permute-start | bytes 69128 | tf_op jit(solution)/shard_map/ppermute | solution.py:18
  28.3 7.9 %collective-permute-done.2.message_ref = bf16[24,480]{1,0:T(8,128)(2,1)S(1)} collective-permute-done((bf16[24,480]{1,0:T(8,128)(2,1)S(1)}, bf16[24,480]{1,0:T(8,128)(2,1)S(1)}, u32[]{:S(2)}, u32[]{:S(2)}) %collective-permute-start.2) | collective-permute-done | bytes 23072 | tf_op jit(solution)/shard_map/ppermute | solution.py:18
  36.1 0.4 shard_map.45
  36.6 1.9 %collective-permute-start.4 = (bf16[24,1728]{1,0:T(8,128)(2,1)S(1)}, bf16[24,1728]{1,0:T(8,128)(2,1)S(1)}, u32[]{:S(2)}, u32[]{:S(2)}) collective-permute-start(bf16[24,1728]{1,0:T(8,128)(2,1)S(1)} %get-tuple-element.18), channel_id=1, source_target_pairs={{0,8},{8,16},{16,24},{24,32},{32,40},{40,48},{48,56},{56,64},{64,7... | collective-permute-start | bytes 248840 | tf_op jit(solution)/shard_map/ppermute | solution.py:18
  38.5 0.4 shard_map.46
  38.9 2.4 %collective-permute-start.3 = (bf16[24,1728]{1,0:T(8,128)(2,1)S(1)}, bf16[24,1728]{1,0:T(8,128)(2,1)S(1)}, u32[]{:S(2)}, u32[]{:S(2)}) collective-permute-start(bf16[24,1728]{1,0:T(8,128)(2,1)S(1)} %get-tuple-element.20), channel_id=1, source_target_pairs={{0,504},{8,0},{16,8},{24,16},{32,24},{40,32},{48,40},{56,48},{64,5... | collective-permute-start | bytes 248840 | tf_op jit(solution)/shard_map/ppermute | solution.py:18
  41.3 0.1 shard_map.44.left_ref
  41.5 0.0 collective-permute-done.4.previous_ref
  41.5 7.9 %collective-permute-done.3.next_ref = bf16[24,1728]{1,0:T(8,128)(2,1)S(1)} collective-permute-done((bf16[24,1728]{1,0:T(8,128)(2,1)S(1)}, bf16[24,1728]{1,0:T(8,128)(2,1)S(1)}, u32[]{:S(2)}, u32[]{:S(2)}) %collective-permute-start.3) | collective-permute-done | bytes 82976 | tf_op jit(solution)/shard_map/ppermute | solution.py:18
  49.4 1.8 %shard_map.47 = (bf16[3,1,224,1728]{3,2,1,0:T(8,128)(2,1)}, f32[3,1,8,1728]{3,2,1,0:T(8,128)}) custom-call(bf16[3,224,48]{2,1,0:T(8,128)(2,1)S(1)} %shard_map.44.left_ref, f32[24,1728]{1,0:T(8,128)S(1)} %get-tuple-element.17.upper_ref, bf16[24,1728]{1,0:T(8,128)(2,1)S(1)} %collective-permute-done.3.next_ref, f32[24,1728]{1,0:T(8,128)S(1)} %get-tuple-element.21.lower_ref, ...), custom_call_target="tpu_custom_call" | custom-call | flops 74317824 | bytes 1048576 | tf_op jit(solution)/shard_map/pallas_call | solution.py:157
  (2 shorter events, 0.0 us)
Async XLA Ops:
  3.3 8.7 %collective-permute-start.1 = (bf16[3,8,1728]{2,1,0:T(8,128)(2,1)S(1)}, bf16[3,8,1728]{2,1,0:T(8,128)(2,1)S(1)}, u32[]{:S(2)}, u32[]{:S(2)}) collective-permute-start(bf16[3,8,1728]{2,1,0:T(8,128)(2,1)S(1)} %get-tuple-element.13), channel_id=1, source_target_pairs={{0,8},{8,16},{16,24},{24,32},{32,40},{40,48},{48,56},{56,64},{64,7... | collective-permute-start | bytes 248840 | tf_op jit(solution)/shard_map/ppermute | solution.py:18
  10.1 3.1 %collective-permute-start = (f32[24,224]{1,0:T(8,128)S(1)}, f32[24,224]{1,0:T(8,128)S(1)}, u32[]{:S(2)}, u32[]{:S(2)}) collective-permute-start(f32[24,224]{1,0:T(8,128)S(1)} %get-tuple-element.12), channel_id=1, source_target_pairs={{0,8},{8,16},{16,24},{24,32},{32,40},{40,48},{48,56},{56,64},{64,7... | collective-permute-start | bytes 64520 | tf_op jit(solution)/shard_map/ppermute | solution.py:18
  25.0 11.1 %collective-permute-start.2 = (bf16[24,480]{1,0:T(8,128)(2,1)S(1)}, bf16[24,480]{1,0:T(8,128)(2,1)S(1)}, u32[]{:S(2)}, u32[]{:S(2)}) collective-permute-start(bf16[24,480]{1,0:T(8,128)(2,1)S(1)} %get-tuple-element.19.message_ref), channel_id=1, source_target_pairs={{0,504},{8,0},{16,8},{24,16},{32,24},{40,32},{48,40},{56,48},{64,5... | collective-permute-start | bytes 69128 | tf_op jit(solution)/shard_map/ppermute | solution.py:18
  36.6 4.9 %collective-permute-start.4 = (bf16[24,1728]{1,0:T(8,128)(2,1)S(1)}, bf16[24,1728]{1,0:T(8,128)(2,1)S(1)}, u32[]{:S(2)}, u32[]{:S(2)}) collective-permute-start(bf16[24,1728]{1,0:T(8,128)(2,1)S(1)} %get-tuple-element.18), channel_id=1, source_target_pairs={{0,8},{8,16},{16,24},{24,32},{32,40},{40,48},{48,56},{56,64},{64,7... | collective-permute-start | bytes 248840 | tf_op jit(solution)/shard_map/ppermute | solution.py:18
  38.9 10.5 %collective-permute-start.3 = (bf16[24,1728]{1,0:T(8,128)(2,1)S(1)}, bf16[24,1728]{1,0:T(8,128)(2,1)S(1)}, u32[]{:S(2)}, u32[]{:S(2)}) collective-permute-start(bf16[24,1728]{1,0:T(8,128)(2,1)S(1)} %get-tuple-element.20), channel_id=1, source_target_pairs={{0,504},{8,0},{16,8},{24,16},{32,24},{40,32},{48,40},{56,48},{64,5... | collective-permute-start | bytes 248840 | tf_op jit(solution)/shard_map/ppermute | solution.py:18

commit v3 on v2

--- a/solution.py
+++ b/solution.py
@@ -18,6 +18,20 @@
     return lax.ppermute(value, axis, pairs)
 
 
+def parity_shifts(axis, steps):
+    count = lax.axis_size(axis)
+
+    def over(parity):
+        pairs = [
+            (source, (source + steps) % count)
+            for source in range(count)
+            if (source + min(steps, 0)) % 2 == parity
+        ]
+        return lambda value: lax.ppermute(value, axis, pairs)
+
+    return over(1), over(0)
+
+
 def padded(size):
     return -(-size // LANES) * LANES
 
@@ -28,20 +42,11 @@
     )
 
 
-def staging_kernel(vectors_hbm, window_hbm, vectors_ref, images_ref, window_ref, held_ref, sems):
-    mats, rank, _ = vectors_ref.shape
-    vectors_copy = pltpu.make_async_copy(vectors_hbm, held_ref, sems.at[mats])
-    vectors_copy.start()
-    copies = [
-        pltpu.make_async_copy(window_hbm.at[mat], window_ref.at[mat], sems.at[mat]) for mat in range(mats)
-    ]
-    for copy in copies:
-        copy.start()
-    vectors_copy.wait()
-    vectors_ref[...] = held_ref[...].astype(jnp.bfloat16)
-    for mat, copy in enumerate(copies):
-        copy.wait()
-        images_ref[mat * rank : (mat + 1) * rank] = images_of(vectors_ref, window_ref, mat)
+def round_kernel(vectors_hbm, rounded_ref, held_ref, sem):
+    copy = pltpu.make_async_copy(vectors_hbm, held_ref, sem)
+    copy.start()
+    copy.wait()
+    rounded_ref[...] = held_ref[...].astype(jnp.bfloat16)
 
 
 def images_kernel(vectors_ref, window_ref, images_ref):
@@ -88,10 +93,14 @@
     message_ref[:, start : start + row_count] = low.astype(jnp.bfloat16)
 
 
-def products_kernel(message_ref, window_ref, products_ref, rounded_ref):
+def odd_replica():
+    return lax.rem(lax.axis_index("replica"), 2) == 1
+
+
+def products_into(basis_ref, window_ref, products_ref, rounded_ref):
     mats, row_count, _ = window_ref.shape
-    rank = message_ref.shape[0] // mats
-    basis = message_ref[:, :row_count].astype(jnp.float32)
+    rank = products_ref.shape[0] // mats
+    basis = basis_ref[:, :row_count].astype(jnp.float32)
     for mat in range(mats):
         rows = slice(mat * rank, (mat + 1) * rank)
         products_ref[rows] = jnp.dot(
@@ -100,12 +109,25 @@
     rounded_ref[...] = products_ref[...].astype(jnp.bfloat16)
 
 
-def left_kernel(message_ref, basis_ref, left_ref):
+def lower_products_kernel(message_ref, window_ref, products_ref, rounded_ref):
+    products_into(message_ref, window_ref, products_ref, rounded_ref)
+
+
+def upper_products_kernel(odd, message_ref, window_ref, products_ref, rounded_ref):
+    @pl.when(odd_replica() == odd)
+    def _():
+        products_into(message_ref, window_ref, products_ref, rounded_ref)
+
+
+def left_kernel(odd_ref, even_ref, basis_ref, left_ref):
     mats, row_count, _ = left_ref.shape
     rank = basis_ref.shape[0] // mats
     start = padded(row_count)
-    upper_high = -0.5 * message_ref[:, :row_count].astype(jnp.float32)
-    upper_low = -0.5 * message_ref[:, start : start + row_count].astype(jnp.float32)
+    odd = odd_replica()
+    upper_high, upper_low = (
+        -0.5 * jnp.where(odd, odd_ref[:, own].astype(jnp.float32), even_ref[:, own].astype(jnp.float32))
+        for own in (slice(0, row_count), slice(start, start + row_count))
+    )
     lower_high, lower_low = split(0.5 * basis_ref[...])
     for mat in range(mats):
         rows = slice(mat * rank, (mat + 1) * rank)
@@ -114,23 +136,46 @@
 
 
 def update_kernel(
-    left_ref, upper_ref, next_ref, lower_ref, previous_ref, window_ref, updated_ref, factors_ref, held_ref, sums_ref, sems
+    left_ref,
+    odd_upper_ref,
+    even_upper_ref,
+    odd_next_ref,
+    even_next_ref,
+    lower_ref,
+    odd_previous_ref,
+    even_previous_ref,
+    window_ref,
+    updated_ref,
+    factors_ref,
+    held_ref,
+    sums_ref,
+    sems,
 ):
     mats, row_count, columns = window_ref.shape
-    rank = upper_ref.shape[0] // mats
+    rank = lower_ref.shape[0] // mats
     width = 2 * LANES
     pieces = sems.shape[1] - 1
     piece = row_count // pieces
+    odd = odd_replica()
+
+    def chosen(if_odd, if_even, start, stop):
+        picked = jnp.where(
+            odd, if_odd[:, start:stop].astype(jnp.float32), if_even[:, start:stop].astype(jnp.float32)
+        )
+        return picked[rows]
+
     copies = []
     for mat in range(mats):
         rows = slice(mat * rank, (mat + 1) * rank)
         rights = []
         for start in range(0, columns, width):
             stop = min(start + width, columns)
-            upper = upper_ref[rows, start:stop] - next_ref[:, start:stop].astype(jnp.float32)[rows]
+            upper = chosen(odd_upper_ref, even_upper_ref, start, stop) - chosen(
+                odd_next_ref, even_next_ref, start, stop
+            )
             sums_ref[mat, 0, :, start:stop] = upper
             upper_high, upper_low = split(upper)
-            lower = previous_ref[:, start:stop].astype(jnp.float32)[rows] - lower_ref[rows, start:stop]
+            lower = chosen(even_previous_ref, odd_previous_ref, start, stop) - lower_ref[rows, start:stop]
             lower_high, lower_low = split(lower)
             parts = [upper_high, upper_high, upper_low, lower_high, lower_high, lower_low]
             rights.append((start, stop, jnp.concatenate(parts, 0).astype(jnp.bfloat16)))
@@ -184,14 +229,15 @@
     products = whole(f32, stacked, columns)
     rounded_products = whole(bf16, stacked, columns)
 
-    vectors_b, own_images, window = call(
-        staging_kernel,
-        (whole(bf16, *own_vectors.shape), images, whole(bf16, *window.shape)),
-        flops,
-        in_specs=[pl.BlockSpec(memory_space=pltpu.HBM)] * 2,
-        scratch_shapes=[pltpu.VMEM(own_vectors.shape, f32), pltpu.SemaphoreType.DMA((mats + 1,))],
-    )(*(pltpu.with_memory_space_constraint(value, pltpu.HBM) for value in (own_vectors, window)))
+    vectors_b = call(
+        round_kernel,
+        whole(bf16, *own_vectors.shape),
+        100 * flops,
+        in_specs=[pl.BlockSpec(memory_space=pltpu.HBM)],
+        scratch_shapes=[pltpu.VMEM(own_vectors.shape, f32), pltpu.SemaphoreType.DMA],
+    )(pltpu.with_memory_space_constraint(own_vectors, pltpu.HBM))
     left_vectors = shifted(vectors_b, "replica", 1)
+    own_images = call(images_kernel, images, flops)(vectors_b, window)
     left_images = shifted(own_images, "replica", 1)
     next_images = call(images_kernel, images, flops)(left_vectors, window)
     group = lax.axis_size("tensor")
@@ -203,14 +249,26 @@
         (images, whole(bf16, stacked, padded(row_count) + row_count)),
         flops // 4,
     )(parts)
-    upper_message = shifted(message, "replica", -1)
-    column_products = call(products_kernel, (products, rounded_products), 400 * flops)
-    upper_products, rounded_upper = column_products(upper_message, window)
-    previous_products = shifted(rounded_upper, "replica", 1)
-    message, _ = lax.optimization_barrier((message, rounded_upper))
-    lower_products, rounded_lower = column_products(message, window)
-    next_products = shifted(rounded_lower, "replica", -1)
-    left = call(left_kernel, whole(bf16, mats, row_count, 6 * rank), flops // 4)(upper_message, lower_basis)
+    odd_down, even_down = parity_shifts("replica", -1)
+    odd_up, even_up = parity_shifts("replica", 1)
+    products_outs = (products, rounded_products)
+
+    odd_basis = odd_down(message)
+    lower_products, rounded = call(lower_products_kernel, products_outs, 400 * flops)(message, window)
+    odd_next = odd_down(rounded)
+    message, rounded = lax.optimization_barrier((message, rounded))
+    even_basis = even_down(message)
+    odd_upper, rounded_upper = call(functools.partial(upper_products_kernel, True), products_outs, 400 * flops)(
+        odd_basis, window
+    )
+    odd_previous = odd_up(rounded_upper)
+    even_upper, rounded_upper = call(functools.partial(upper_products_kernel, False), products_outs, 400 * flops)(
+        even_basis, window
+    )
+    even_previous = even_up(rounded_upper)
+    rounded, _ = lax.optimization_barrier((rounded, rounded_upper))
+    even_next = even_down(rounded)
+    left = call(left_kernel, whole(bf16, mats, row_count, 6 * rank), flops // 4)(odd_basis, even_basis, lower_basis)
     pieces = 2 if row_count % 32 == 0 else 1
     updated, factors = call(
         update_kernel,
@@ -222,7 +280,17 @@
             pltpu.VMEM((mats, 1, rank, columns), f32),
             pltpu.SemaphoreType.DMA((mats, pieces + 1)),
         ],
-    )(left, upper_products, next_products, lower_products, previous_products, window)
+    )(
+        left,
+        odd_upper,
+        even_upper,
+        odd_next,
+        even_next,
+        lower_products,
+        odd_previous,
+        even_previous,
+        window,
+    )
     return (updated, factors)
 
 

time: 51.5 us -> 48.1 us (0.934)
  the two profiles are of different devices: /device:TPU:185 before, /device:TPU:2 now
where the time goes in v3:
time: 48.1 us; the launch traced here: 47.8 us
  waiting for transfers between devices  15.1 us (31%)
  starting transfers between devices  15 us (31%)
  blocking collectives  10.7 us (22%)
  Pallas kernels  6.22 us (13%)
  between operations  0.76 us (2%)
    ppermute x2, waiting for transfers between devices, shifted(): return lax.ppermute(value, axis, pairs)  10.7 us
    all_to_all x1, blocking collectives, shards(): lax.all_to_all(jnp.broadcast_to((left_images - next_images)[None], (group...  10.7 us
    ppermute x6, starting transfers between devices, over(): return lambda value: lax.ppermute(value, axis, pairs)  9.5 us
    pallas_call x9, Pallas kernels, run(): pl.pallas_call(kernel, out_shape=outs, in_specs=[IN_VMEM] * len(operands)...  6.22 us
    ppermute x2, starting transfers between devices, shifted(): return lax.ppermute(value, axis, pairs)  5.53 us
    ppermute x6, waiting for transfers between devices, over(): return lambda value: lax.ppermute(value, axis, pairs)  4.34 us
  transfers between devices with their start and end apart: 8, of which 4 were waited for; matrix products, arithmetic and copies ran while one was open for 0% of the time, Pallas kernels for 5%

profile of v3, /device:TPU:2, one launch (start us, length us, event | category | flops | bytes accessed | tf_op | source)
XLA Modules:
  0.0 47.8 jit_solution(15508016425851454947)
XLA Ops:
  0.6 1.1 %shard_map.41.vectors_ref = bf16[3,8,1728]{2,1,0:T(8,128)(2,1)S(1)} custom-call(f32[3,8,1728]{2,1,0:T(8,128)} %bitcast.8), custom_call_target="tpu_custom_call" | custom-call | flops 1857945600 | bytes 1048576 | tf_op jit(solution)/shard_map/pallas_call | solution.py:202
  1.7 1.9 %collective-permute-start.1 = (bf16[3,8,1728]{2,1,0:T(8,128)(2,1)S(1)}, bf16[3,8,1728]{2,1,0:T(8,128)(2,1)S(1)}, u32[]{:S(2)}, u32[]{:S(2)}) collective-permute-start(bf16[3,8,1728]{2,1,0:T(8,128)(2,1)S(1)} %shard_map.41.vectors_ref), channel_id=1, source_target_pairs={{0,8},{8,16},{16,24},{24,32},{32,40},{40,48},{48,56},{56,64},{64,7... | collective-permute-start | bytes 248840 | tf_op jit(solution)/shard_map/ppermute | solution.py:18
  3.7 0.7 %shard_map.42 = f32[24,224]{1,0:T(8,128)S(1)} custom-call(bf16[3,8,1728]{2,1,0:T(8,128)(2,1)S(1)} %shard_map.41.vectors_ref, bf16[3,224,1728]{2,1,0:T(8,128)(2,1)S(1)} %bitcast.2), custom_call_target="tpu_custom_call" | custom-call | flops 18579456 | bytes 1048576 | tf_op jit(solution)/shard_map/pallas_call | solution.py:202
  4.4 3.6 %collective-permute-start = (f32[24,224]{1,0:T(8,128)S(1)}, f32[24,224]{1,0:T(8,128)S(1)}, u32[]{:S(2)}, u32[]{:S(2)}) collective-permute-start(f32[24,224]{1,0:T(8,128)S(1)} %shard_map.42), channel_id=1, source_target_pairs={{0,8},{8,16},{16,24},{24,32},{32,40},{40,48},{48,56},{56,64},{64,7... | collective-permute-start | bytes 64520 | tf_op jit(solution)/shard_map/ppermute | solution.py:18
  8.0 10.1 %collective-permute-done.1.vectors_ref = bf16[3,8,1728]{2,1,0:T(8,128)(2,1)S(1)} collective-permute-done((bf16[3,8,1728]{2,1,0:T(8,128)(2,1)S(1)}, bf16[3,8,1728]{2,1,0:T(8,128)(2,1)S(1)}, u32[]{:S(2)}, u32[]{:S(2)}) %collective-permute-start.1) | collective-permute-done | bytes 82976 | tf_op jit(solution)/shard_map/ppermute | solution.py:18
  18.1 0.7 %shard_map.43 = f32[24,224]{1,0:T(8,128)S(1)} custom-call(bf16[3,8,1728]{2,1,0:T(8,128)(2,1)S(1)} %collective-permute-done.1.vectors_ref, bf16[3,224,1728]{2,1,0:T(8,128)(2,1)S(1)} %bitcast.3), custom_call_target="tpu_custom_call" | custom-call | flops 18579456 | bytes 1048576 | tf_op jit(solution)/shard_map/pallas_call | solution.py:202
  18.8 0.7 %collective-permute-done = f32[24,224]{1,0:T(8,128)S(1)} collective-permute-done((f32[24,224]{1,0:T(8,128)S(1)}, f32[24,224]{1,0:T(8,128)S(1)}, u32[]{:S(2)}, u32[]{:S(2)}) %collective-permute-start) | collective-permute-done | bytes 21536 | tf_op jit(solution)/shard_map/ppermute | solution.py:18
  19.5 10.7 %all_to_all.5.parts_ref = f32[8,24,224]{2,1,0:T(8,128)S(1)} all-to-all(f32[8,24,224]{2,1,0:T(8,128)S(1)} %broadcast_in_dim.2), channel_id=1, replica_groups=mesh['replica'=64,'tensor'=8] {'tensor'}, dimensions={0} | all-to-all | bytes 344064 | tf_op jit(solution)/shard_map/all_to_all | solution.py:244
  30.2 0.8 %shard_map.44 = (f32[24,224]{1,0:T(8,128)S(1)}, bf16[24,480]{1,0:T(8,128)(2,1)S(1)}) custom-call(f32[8,24,224]{2,1,0:T(8,128)S(1)} %all_to_all.5.parts_ref), custom_call_target="tpu_custom_call" | custom-call | flops 4644864 | bytes 1048576 | tf_op jit(solution)/shard_map/pallas_call | solution.py:202
  31.0 1.3 %collective-permute-start.2 = (bf16[24,480]{1,0:T(8,128)(2,1)S(1)}, bf16[24,480]{1,0:T(8,128)(2,1)S(1)}, u32[]{:S(2)}, u32[]{:S(2)}) collective-permute-start(bf16[24,480]{1,0:T(8,128)(2,1)S(1)} %get-tuple-element.15.message_ref), channel_id=1, source_target_pairs={{0,504},{16,8},{32,24},{48,40},{64,56},{80,72},{96,88},{112,104},{... | collective-permute-start | bytes 69128 | tf_op jit(solution)/shard_map/ppermute | solution.py:30
  32.3 0.4 shard_map.45
  32.8 1.3 %collective-permute-start.4 = (bf16[24,1728]{1,0:T(8,128)(2,1)S(1)}, bf16[24,1728]{1,0:T(8,128)(2,1)S(1)}, u32[]{:S(2)}, u32[]{:S(2)}) collective-permute-start(bf16[24,1728]{1,0:T(8,128)(2,1)S(1)} %get-tuple-element.21), channel_id=1, source_target_pairs={{0,504},{16,8},{32,24},{48,40},{64,56},{80,72},{96,88},{112,104},{... | collective-permute-start | bytes 248840 | tf_op jit(solution)/shard_map/ppermute | solution.py:30
  34.1 1.3 %collective-permute-start.3 = (bf16[24,480]{1,0:T(8,128)(2,1)S(1)}, bf16[24,480]{1,0:T(8,128)(2,1)S(1)}, u32[]{:S(2)}, u32[]{:S(2)}) collective-permute-start(bf16[24,480]{1,0:T(8,128)(2,1)S(1)} %get-tuple-element.15.message_ref), channel_id=1, source_target_pairs={{8,0},{24,16},{40,32},{56,48},{72,64},{88,80},{104,96},{120,112},{... | collective-permute-start | bytes 69128 | tf_op jit(solution)/shard_map/ppermute | solution.py:30
  35.4 0.0 collective-permute-done.2.odd_ref.message_ref
  35.4 1.3 %collective-permute-start.6 = (bf16[24,1728]{1,0:T(8,128)(2,1)S(1)}, bf16[24,1728]{1,0:T(8,128)(2,1)S(1)}, u32[]{:S(2)}, u32[]{:S(2)}) collective-permute-start(bf16[24,1728]{1,0:T(8,128)(2,1)S(1)} %get-tuple-element.23), channel_id=1, source_target_pairs={{8,16},{24,32},{40,48},{56,64},{72,80},{88,96},{104,112},{120,128}... | collective-permute-start | bytes 248840 | tf_op jit(solution)/shard_map/ppermute | solution.py:30
  36.7 0.5 collective-permute-done.3.even_ref.message_ref
  37.2 0.4 shard_map.48
  37.6 1.3 %collective-permute-start.5 = (bf16[24,1728]{1,0:T(8,128)(2,1)S(1)}, bf16[24,1728]{1,0:T(8,128)(2,1)S(1)}, u32[]{:S(2)}, u32[]{:S(2)}) collective-permute-start(bf16[24,1728]{1,0:T(8,128)(2,1)S(1)} %get-tuple-element.21), channel_id=1, source_target_pairs={{8,0},{24,16},{40,32},{56,48},{72,64},{88,80},{104,96},{120,112},{... | collective-permute-start | bytes 248840 | tf_op jit(solution)/shard_map/ppermute | solution.py:30
  38.9 3.0 %collective-permute-start.7 = (bf16[24,1728]{1,0:T(8,128)(2,1)S(1)}, bf16[24,1728]{1,0:T(8,128)(2,1)S(1)}, u32[]{:S(2)}, u32[]{:S(2)}) collective-permute-start(bf16[24,1728]{1,0:T(8,128)(2,1)S(1)} %get-tuple-element.20), channel_id=1, source_target_pairs={{0,8},{16,24},{32,40},{48,56},{64,72},{80,88},{96,104},{112,120},{... | collective-permute-start | bytes 248840 | tf_op jit(solution)/shard_map/ppermute | solution.py:30
  41.9 0.1 shard_map.46.left_ref
  42.1 0.0 collective-permute-done.4.odd_next_ref
  42.1 3.9 %collective-permute-done.6.odd_previous_ref = bf16[24,1728]{1,0:T(8,128)(2,1)S(1)} collective-permute-done((bf16[24,1728]{1,0:T(8,128)(2,1)S(1)}, bf16[24,1728]{1,0:T(8,128)(2,1)S(1)}, u32[]{:S(2)}, u32[]{:S(2)}) %collective-permute-start.6) | collective-permute-done | bytes 82976 | tf_op jit(solution)/shard_map/ppermute | solution.py:30
  46.0 0.0 collective-permute-done.7.even_previous_ref
  46.0 1.8 %shard_map.49 = (bf16[3,1,224,1728]{3,2,1,0:T(8,128)(2,1)}, f32[3,1,8,1728]{3,2,1,0:T(8,128)}) custom-call(bf16[3,224,48]{2,1,0:T(8,128)(2,1)S(1)} %shard_map.46.left_ref, f32[24,1728]{1,0:T(8,128)S(1)} %get-tuple-element.17.odd_upper_ref, f32[24,1728]{1,0:T(8,128)S(1)} %get-tuple-element.18.even_upper_ref, ...), custom_call_target="tpu_custom_call" | custom-call | flops 74317824 | bytes 1048576 | tf_op jit(solution)/shard_map/pallas_call | solution.py:202
  (6 shorter events, 0.0 us)
Async XLA Ops:
  0.6 3.0 %copy-start = (bf16[3,1,224,1728]{3,2,1,0:T(8,128)(2,1)S(1)}, bf16[3,1,224,1728]{3,2,1,0:T(8,128)(2,1)}, u32[]{:S(2)}) copy-start(bf16[3,1,224,1728]{3,2,1,0:T(8,128)(2,1)} %param.2) | copy-start | bytes 6967300
  1.7 16.4 %collective-permute-start.1 = (bf16[3,8,1728]{2,1,0:T(8,128)(2,1)S(1)}, bf16[3,8,1728]{2,1,0:T(8,128)(2,1)S(1)}, u32[]{:S(2)}, u32[]{:S(2)}) collective-permute-start(bf16[3,8,1728]{2,1,0:T(8,128)(2,1)S(1)} %shard_map.41.vectors_ref), channel_id=1, source_target_pairs={{0,8},{8,16},{16,24},{24,32},{32,40},{40,48},{48,56},{56,64},{64,7... | collective-permute-start | bytes 248840 | tf_op jit(solution)/shard_map/ppermute | solution.py:18
  4.4 15.1 %collective-permute-start = (f32[24,224]{1,0:T(8,128)S(1)}, f32[24,224]{1,0:T(8,128)S(1)}, u32[]{:S(2)}, u32[]{:S(2)}) collective-permute-start(f32[24,224]{1,0:T(8,128)S(1)} %shard_map.42), channel_id=1, source_target_pairs={{0,8},{8,16},{16,24},{24,32},{32,40},{40,48},{48,56},{56,64},{64,7... | collective-permute-start | bytes 64520 | tf_op jit(solution)/shard_map/ppermute | solution.py:18
  31.0 4.3 %collective-permute-start.2 = (bf16[24,480]{1,0:T(8,128)(2,1)S(1)}, bf16[24,480]{1,0:T(8,128)(2,1)S(1)}, u32[]{:S(2)}, u32[]{:S(2)}) collective-permute-start(bf16[24,480]{1,0:T(8,128)(2,1)S(1)} %get-tuple-element.15.message_ref), channel_id=1, source_target_pairs={{0,504},{16,8},{32,24},{48,40},{64,56},{80,72},{96,88},{112,104},{... | collective-permute-start | bytes 69128 | tf_op jit(solution)/shard_map/ppermute | solution.py:30
  32.8 9.3 %collective-permute-start.4 = (bf16[24,1728]{1,0:T(8,128)(2,1)S(1)}, bf16[24,1728]{1,0:T(8,128)(2,1)S(1)}, u32[]{:S(2)}, u32[]{:S(2)}) collective-permute-start(bf16[24,1728]{1,0:T(8,128)(2,1)S(1)} %get-tuple-element.21), channel_id=1, source_target_pairs={{0,504},{16,8},{32,24},{48,40},{64,56},{80,72},{96,88},{112,104},{... | collective-permute-start | bytes 248840 | tf_op jit(solution)/shard_map/ppermute | solution.py:30
  34.1 3.1 %collective-permute-start.3 = (bf16[24,480]{1,0:T(8,128)(2,1)S(1)}, bf16[24,480]{1,0:T(8,128)(2,1)S(1)}, u32[]{:S(2)}, u32[]{:S(2)}) collective-permute-start(bf16[24,480]{1,0:T(8,128)(2,1)S(1)} %get-tuple-element.15.message_ref), channel_id=1, source_target_pairs={{8,0},{24,16},{40,32},{56,48},{72,64},{88,80},{104,96},{120,112},{... | collective-permute-start | bytes 69128 | tf_op jit(solution)/shard_map/ppermute | solution.py:30
  35.4 10.6 %collective-permute-start.6 = (bf16[24,1728]{1,0:T(8,128)(2,1)S(1)}, bf16[24,1728]{1,0:T(8,128)(2,1)S(1)}, u32[]{:S(2)}, u32[]{:S(2)}) collective-permute-start(bf16[24,1728]{1,0:T(8,128)(2,1)S(1)} %get-tuple-element.23), channel_id=1, source_target_pairs={{8,16},{24,32},{40,48},{56,64},{72,80},{88,96},{104,112},{120,128}... | collective-permute-start | bytes 248840 | tf_op jit(solution)/shard_map/ppermute | solution.py:30
  37.6 8.4 %collective-permute-start.5 = (bf16[24,1728]{1,0:T(8,128)(2,1)S(1)}, bf16[24,1728]{1,0:T(8,128)(2,1)S(1)}, u32[]{:S(2)}, u32[]{:S(2)}) collective-permute-start(bf16[24,1728]{1,0:T(8,128)(2,1)S(1)} %get-tuple-element.21), channel_id=1, source_target_pairs={{8,0},{24,16},{40,32},{56,48},{72,64},{88,80},{104,96},{120,112},{... | collective-permute-start | bytes 248840 | tf_op jit(solution)/shard_map/ppermute | solution.py:30
  38.9 7.1 %collective-permute-start.7 = (bf16[24,1728]{1,0:T(8,128)(2,1)S(1)}, bf16[24,1728]{1,0:T(8,128)(2,1)S(1)}, u32[]{:S(2)}, u32[]{:S(2)}) collective-permute-start(bf16[24,1728]{1,0:T(8,128)(2,1)S(1)} %get-tuple-element.20), channel_id=1, source_target_pairs={{0,8},{16,24},{32,40},{48,56},{64,72},{80,88},{96,104},{112,120},{... | collective-permute-start | bytes 248840 | tf_op jit(solution)/shard_map/ppermute | solution.py:30

commit v4 on v3

v4 whole, which is shorter than its diff:
```python
import functools

import jax
import jax.numpy as jnp
from jax import lax
from jax.experimental import pallas as pl
from jax.experimental.pallas import tpu as pltpu
from jax.sharding import PartitionSpec as P

LANES = 128
ROWS_BY_ROWS = (((1,), (1,)), ((), ()))
IN_VMEM = pl.BlockSpec(memory_space=pltpu.VMEM)


def shifted(value, axis, steps):
    count = lax.axis_size(axis)
    return lax.ppermute(value, axis, [(source, (source + steps) % count) for source in range(count)])


def parity_shifts(axis, steps):
    count = lax.axis_size(axis)

    def over(parity):
        pairs = [
            (source, (source + steps) % count)
            for source in range(count)
            if (source + min(steps, 0)) % 2 == parity
        ]
        return lambda value: lax.ppermute(value, axis, pairs)

    return over(1), over(0)


def padded(size):
    return -(-size // LANES) * LANES


def odd_replica():
    return lax.rem(lax.axis_index("replica"), 2) == 1


def images_kernel(vectors_ref, window_ref, images_ref):
    mats, rank, _ = vectors_ref.shape
    for mat in range(mats):
        images_ref[mat * rank : (mat + 1) * rank] = lax.dot_general(
            vectors_ref[mat], window_ref[mat], ROWS_BY_ROWS, preferred_element_type=jnp.float32
        )


def round_kernel(vectors_hbm, rounded_ref, held_ref, sem):
    copy = pltpu.make_async_copy(vectors_hbm, held_ref, sem)
    copy.start()
    copy.wait()
    rounded_ref[...] = held_ref[...].astype(jnp.bfloat16)


def own_images_kernel(vectors_ref, window_ref, images_ref, vectors_out_ref):
    mats, rank, _ = vectors_ref.shape
    vectors_out_ref[...] = vectors_ref[...]
    for mat in range(mats):
        images_ref[mat * rank : (mat + 1) * rank] = images_of(vectors_ref[mat], window_ref[mat])


def differences_kernel(
    even_images_ref, even_vectors_ref, odd_images_ref, odd_vectors_ref, window_ref, differences_ref
):
    mats, rank, _ = odd_vectors_ref.shape
    odd = odd_replica()

    def chosen(if_odd, if_even):
        return jnp.where(odd, if_odd.astype(jnp.float32), if_even.astype(jnp.float32))

    for mat in range(mats):
        rows = slice(mat * rank, (mat + 1) * rank)
        vectors = chosen(even_vectors_ref[mat], odd_vectors_ref[mat]).astype(jnp.bfloat16)
        images = chosen(even_images_ref[rows], odd_images_ref[rows])
        differences_ref[rows] = images - images_of(vectors, window_ref[mat])


def round_kernel(vectors_hbm, rounded_ref, held_ref, sem):
    copy = pltpu.make_async_copy(vectors_hbm, held_ref, sem)
    copy.start()
    copy.wait()
    rounded_ref[...] = held_ref[...].astype(jnp.bfloat16)


def own_images_kernel(vectors_ref, window_ref, images_ref, vectors_out_ref):
    mats, rank, _ = vectors_ref.shape
    vectors_out_ref[...] = vectors_ref[...]
    for mat in range(mats):
        images_ref[mat * rank : (mat + 1) * rank] = images_of(vectors_ref[mat], window_ref[mat])


def next_images_kernel(even_ref, odd_ref, window_ref, images_ref):
    mats, rank, _ = odd_ref.shape
    odd = odd_replica()
    for mat in range(mats):
        vectors = jnp.where(odd, even_ref[mat].astype(jnp.float32), odd_ref[mat].astype(jnp.float32))
        images_ref[mat * rank : (mat + 1) * rank] = images_of(vectors.astype(jnp.bfloat16), window_ref[mat])


def orthonormal_rows(gram, images, rank):
    mats = gram.shape[0] // rank
    grams = [gram[mat * rank : (mat + 1) * rank] for mat in range(mats)]
    rows = [images[mat * rank : (mat + 1) * rank] for mat in range(mats)]
    place = lax.broadcasted_iota(jnp.int32, (rank, 1), 0)
    pivots = [jnp.ones((rank, 1), jnp.float32) for _ in range(mats)]
    for step in range(rank):
        for mat in range(mats):
            column = grams[mat][:, mat * rank + step : mat * rank + step + 1]
            pivot = column[step : step + 1]
            pivots[mat] = jnp.where(place == step, pivot, pivots[mat])
            if step < rank - 1:
                factor = jnp.where(place > step, column / pivot, 0.0)
                rows[mat] = rows[mat] - factor * rows[mat][step : step + 1]
                grams[mat] = grams[mat] - factor * grams[mat][step : step + 1]
    return jnp.concatenate([row / jnp.sqrt(pivot) for row, pivot in zip(rows, pivots)], 0)


def split(value):
    high = value.astype(jnp.bfloat16).astype(jnp.float32)
    return high, value - high


def basis_kernel(mats, parts_ref, basis_ref, message_ref):
    rank = parts_ref.shape[1] // mats
    row_count = parts_ref.shape[2]
    images = jnp.sum(parts_ref[...], 0)
    gram = lax.dot_general(
        images, images, ROWS_BY_ROWS, precision=lax.Precision.HIGHEST, preferred_element_type=jnp.float32
    )
    basis = orthonormal_rows(gram, images, rank)
    basis_ref[...] = basis
    high, low = split(basis)
    message_ref[:, :row_count] = high.astype(jnp.bfloat16)
    start = padded(row_count)
    message_ref[:, start : start + row_count] = low.astype(jnp.bfloat16)


def products_into(basis_ref, window_ref, products_ref, rounded_ref):
    mats, row_count, _ = window_ref.shape
    rank = products_ref.shape[0] // mats
    basis = basis_ref[:, :row_count].astype(jnp.float32)
    for mat in range(mats):
        rows = slice(mat * rank, (mat + 1) * rank)
        products_ref[rows] = jnp.dot(
            basis[rows].astype(jnp.bfloat16), window_ref[mat], preferred_element_type=jnp.float32
        )
    rounded_ref[...] = products_ref[...].astype(jnp.bfloat16)


def lower_products_kernel(basis_ref, window_ref, products_ref, message_ref):
    columns = products_ref.shape[1]
    products_into(basis_ref, window_ref, products_ref, message_ref.at[:, :columns])
    message_ref[:, padded(columns) :] = basis_ref[...]


def upper_products_kernel(odd, start, message_ref, window_ref, products_ref, rounded_ref):
    @pl.when(odd_replica() == odd)
    def _():
        products_into(message_ref.at[:, start:], window_ref, products_ref, rounded_ref)


def factors_kernel(
    message_ref,
    odd_products_ref,
    even_products_ref,
    lower_basis_ref,
    lower_products_ref,
    left_ref,
    right_ref,
    factors_hbm,
    factors_ref,
    sem,
):
    mats, row_count, _ = left_ref.shape
    stacked, columns = lower_products_ref.shape
    rank = stacked // mats
    upper = jnp.where(odd_replica(), odd_products_ref[...], even_products_ref[...]) - message_ref[
        :, :columns
    ].astype(jnp.float32)
    for mat in range(mats):
        factors_ref[mat, 0] = upper[mat * rank : (mat + 1) * rank]
    copy = pltpu.make_async_copy(factors_ref, factors_hbm, sem)
    copy.start()
    high, low = padded(columns), padded(columns) + padded(row_count)
    upper_high = -0.5 * message_ref[:, high : high + row_count].astype(jnp.float32)
    upper_low = -0.5 * message_ref[:, low : low + row_count].astype(jnp.float32)
    lower_high, lower_low = split(0.5 * lower_basis_ref[...])
    factor_high, factor_low = split(upper)
    products_high, products_low = split(-lower_products_ref[...])
    for mat in range(mats):
        rows = slice(mat * rank, (mat + 1) * rank)
        lefts = [upper_high, upper_low, upper_high, lower_high, lower_low, lower_high, lower_high, lower_low]
        left_ref[mat] = jnp.concatenate([part[rows] for part in lefts], 0).T.astype(jnp.bfloat16)
        rights = [factor_high, factor_high, factor_low, products_high, products_high, products_low]
        right_ref[mat] = jnp.concatenate([part[rows] for part in rights], 0).astype(jnp.bfloat16)
    copy.wait()


def update_kernel(left_ref, right_ref, odd_ref, even_ref, window_ref, updated_ref, held_ref, sems):
    mats, _, columns = window_ref.shape
    rank = odd_ref.shape[0] // mats
    width = 2 * LANES
    odd = odd_replica()
    copies = []
    for mat in range(mats):
        rows = slice(mat * rank, (mat + 1) * rank)
        for start in range(0, columns, width):
            stop = min(start + width, columns)
            lower = jnp.where(
                odd, even_ref[:, start:stop].astype(jnp.float32), odd_ref[:, start:stop].astype(jnp.float32)
            )[rows]
            last = jnp.concatenate([lower, lower], 0).astype(jnp.bfloat16)
            right = jnp.concatenate([right_ref[mat, :, start:stop], last], 0)
            change = jnp.dot(left_ref[mat], right, preferred_element_type=jnp.float32)
            held_ref[mat, :, start:stop] = (window_ref[mat, :, start:stop].astype(jnp.float32) + change).astype(
                jnp.bfloat16
            )
        copies.append(pltpu.make_async_copy(held_ref.at[mat], updated_ref.at[mat, 0], sems.at[mat]))
        copies[-1].start()
    for copy in copies:
        copy.wait()


def call(kernel, outs, flops, in_specs=None, out_specs=None, **more):
    def run(*operands):
        return pl.pallas_call(
            kernel,
            out_shape=outs,
            in_specs=[IN_VMEM] * len(operands) if in_specs is None else in_specs,
            out_specs=jax.tree.map(lambda _: IN_VMEM, outs) if out_specs is None else out_specs,
            cost_estimate=pl.CostEstimate(flops=flops, bytes_accessed=1 << 20, transcendentals=0),
            compiler_params=pltpu.CompilerParams(vmem_limit_bytes=24 << 20),
            **more,
        )(*operands)

    return run


def shards(weights, vectors):
    window = weights[:, 0]
    own_vectors = vectors[:, 0]
    mats, rank, columns = own_vectors.shape
    row_count = window.shape[1]
    stacked = mats * rank
    flops = 2 * stacked * row_count * columns

    def whole(dtype, *dims):
        return jax.ShapeDtypeStruct(dims, dtype)

    f32, bf16 = jnp.float32, jnp.bfloat16
    images = whole(f32, stacked, row_count)
    rounded_images = whole(bf16, stacked, row_count)
    products = whole(f32, stacked, columns)
    rounded_products = whole(bf16, stacked, columns)

    vectors_b = call(
        round_kernel,
        whole(bf16, *own_vectors.shape),
        100 * flops,
        in_specs=[pl.BlockSpec(memory_space=pltpu.HBM)],
        scratch_shapes=[pltpu.VMEM(own_vectors.shape, f32), pltpu.SemaphoreType.DMA],
    )(pltpu.with_memory_space_constraint(own_vectors, pltpu.HBM))
    left_vectors = shifted(vectors_b, "replica", 1)
    own_images = call(images_kernel, images, flops)(vectors_b, window)
    left_images = shifted(own_images, "replica", 1)
    next_images = call(images_kernel, images, flops)(left_vectors, window)
    group = lax.axis_size("tensor")
    parts = lax.all_to_all(
        jnp.broadcast_to((left_images - next_images)[None], (group, stacked, row_count)), "tensor", 0, 0
    )
    lower_basis, basis = call(
        functools.partial(basis_kernel, mats),
        (images, whole(bf16, stacked, padded(row_count) + row_count)),
        flops // 4,
    )(parts)
    products_outs = (products, rounded_products)
    base = padded(columns)
    odd_up, even_up = parity_shifts("replica", 1)
    odd_down, _ = parity_shifts("replica", -1)

    odd_basis = odd_down(basis)
    lower_products, message = call(
        lower_products_kernel, (products, whole(bf16, stacked, base + basis.shape[1])), 400 * flops
    )(basis, window)
    message = shifted(message, "replica", -1)
    odd_upper, rounded_upper = call(functools.partial(upper_products_kernel, True, 0), products_outs, 400 * flops)(
        odd_basis, window
    )
    odd_previous = odd_up(rounded_upper)
    even_upper, rounded_upper = call(functools.partial(upper_products_kernel, False, base), products_outs, 0)(
        message, window
    )
    even_previous = even_up(rounded_upper)
    left, right, factors = call(
        factors_kernel,
        (
            whole(bf16, mats, row_count, 8 * rank),
            whole(bf16, mats, 6 * rank, columns),
            whole(f32, mats, 1, rank, columns),
        ),
        flops // 4,
        out_specs=(IN_VMEM, IN_VMEM, pl.BlockSpec(memory_space=pl.ANY)),
        scratch_shapes=[pltpu.VMEM((mats, 1, rank, columns), f32), pltpu.SemaphoreType.DMA],
    )(message, odd_upper, even_upper, lower_basis, lower_products)
    updated = call(
        update_kernel,
        whole(bf16, mats, 1, row_count, columns),
        4 * flops,
        out_specs=pl.BlockSpec(memory_space=pl.ANY),
        scratch_shapes=[pltpu.VMEM((mats, row_count, columns), bf16), pltpu.SemaphoreType.DMA((mats,))],
    )(left, right, odd_previous, even_previous, window)
    return (updated, factors)


def solution(mesh):
    placed = (P(None, "replica", None, "tensor"), P(None, "replica", None, "tensor"))
    return jax.shard_map(
        shards,
        mesh=mesh,
        in_specs=placed,
        out_specs=(P(None, "replica", None, "tensor"), P(None, "replica", None, "tensor")),
        check_vma=False,
    )
```

time: 48.1 us -> 47.4 us (0.985)
  starting transfers between devices: 15 us -> 11.5 us
  waiting for transfers between devices: 15.1 us -> 17.3 us
  Pallas kernels: 6.22 us -> 6.85 us
    ppermute x6 -> x3, starting transfers between devices: 9.5 us -> 4.05 us  [over(): return lambda value: lax.ppermute(value, axis, pairs)]
    ppermute x2 -> x3, starting transfers between devices: 5.53 us -> 7.46 us  [shifted(): lax.ppermute(value, axis, [(source, (source + steps) % count) for source...]
    ppermute x6 -> x3, waiting for transfers between devices: 4.34 us -> 5.6 us  [over(): return lambda value: lax.ppermute(value, axis, pairs)]
    ppermute x2 -> x3, waiting for transfers between devices: 10.7 us -> 11.7 us  [shifted(): lax.ppermute(value, axis, [(source, (source + steps) % count) for source...]
    pallas_call x9, Pallas kernels: 6.22 us -> 6.85 us  [run(): pl.pallas_call(kernel, out_shape=outs, in_specs=[IN_VMEM] * len(operands)...]
  transfers between devices with their start and end apart: 8 -> 6, of which waited for: 4 -> 4; matrix products, arithmetic and copies ran while one was open for 0% -> 0% of each run, Pallas kernels for 5% -> 7%
where the time goes in v4:
time: 47.4 us; the launch traced here: 47.1 us
  waiting for transfers between devices  17.3 us (36%)
  starting transfers between devices  11.5 us (24%)
  blocking collectives  10.7 us (23%)
  Pallas kernels  6.85 us (14%)
  between operations  0.74 us (2%)
    ppermute x3, waiting for transfers between devices, shifted(): lax.ppermute(value, axis, [(source, (source + steps) % count) for source...  11.7 us
    all_to_all x1, blocking collectives, shards(): lax.all_to_all(jnp.broadcast_to((left_images - next_images)[None], (group...  10.7 us
    ppermute x3, starting transfers between devices, shifted(): lax.ppermute(value, axis, [(source, (source + steps) % count) for source...  7.46 us
    pallas_call x9, Pallas kernels, run(): pl.pallas_call(kernel, out_shape=outs, in_specs=[IN_VMEM] * len(operands)...  6.85 us
    ppermute x3, waiting for transfers between devices, over(): return lambda value: lax.ppermute(value, axis, pairs)  5.6 us
    ppermute x3, starting transfers between devices, over(): return lambda value: lax.ppermute(value, axis, pairs)  4.05 us
  transfers between devices with their start and end apart: 6, of which 4 were waited for; matrix products, arithmetic and copies ran while one was open for 0% of the time, Pallas kernels for 7%

profile of v4, /device:TPU:2, one launch (start us, length us, event | category | flops | bytes accessed | tf_op | source)
XLA Modules:
  0.0 47.1 jit_solution(15701937680573039589)
XLA Ops:
  0.6 0.0 copy-start
  0.6 1.1 %shard_map.41.vectors_ref = bf16[3,8,1728]{2,1,0:T(8,128)(2,1)S(1)} custom-call(f32[3,8,1728]{2,1,0:T(8,128)} %bitcast.8), custom_call_target="tpu_custom_call" | custom-call | flops 1857945600 | bytes 1048576 | tf_op jit(solution)/shard_map/pallas_call | solution.py:228
  1.7 1.9 %collective-permute-start.1 = (bf16[3,8,1728]{2,1,0:T(8,128)(2,1)S(1)}, bf16[3,8,1728]{2,1,0:T(8,128)(2,1)S(1)}, u32[]{:S(2)}, u32[]{:S(2)}) collective-permute-start(bf16[3,8,1728]{2,1,0:T(8,128)(2,1)S(1)} %shard_map.41.vectors_ref), channel_id=1, source_target_pairs={{0,8},{8,16},{16,24},{24,32},{32,40},{40,48},{48,56},{56,64},{64,7... | collective-permute-start | bytes 248840 | tf_op jit(solution)/shard_map/ppermute | solution.py:17
  3.7 0.0 copy-done
  3.7 0.7 %shard_map.42 = f32[24,224]{1,0:T(8,128)S(1)} custom-call(bf16[3,8,1728]{2,1,0:T(8,128)(2,1)S(1)} %shard_map.41.vectors_ref, bf16[3,224,1728]{2,1,0:T(8,128)(2,1)S(1)} %bitcast.2), custom_call_target="tpu_custom_call" | custom-call | flops 18579456 | bytes 1048576 | tf_op jit(solution)/shard_map/pallas_call | solution.py:228
  4.4 3.6 %collective-permute-start = (f32[24,224]{1,0:T(8,128)S(1)}, f32[24,224]{1,0:T(8,128)S(1)}, u32[]{:S(2)}, u32[]{:S(2)}) collective-permute-start(f32[24,224]{1,0:T(8,128)S(1)} %shard_map.42), channel_id=1, source_target_pairs={{0,8},{8,16},{16,24},{24,32},{32,40},{40,48},{48,56},{56,64},{64,7... | collective-permute-start | bytes 64520 | tf_op jit(solution)/shard_map/ppermute | solution.py:17
  8.0 10.1 %collective-permute-done.1.vectors_ref = bf16[3,8,1728]{2,1,0:T(8,128)(2,1)S(1)} collective-permute-done((bf16[3,8,1728]{2,1,0:T(8,128)(2,1)S(1)}, bf16[3,8,1728]{2,1,0:T(8,128)(2,1)S(1)}, u32[]{:S(2)}, u32[]{:S(2)}) %collective-permute-start.1) | collective-permute-done | bytes 82976 | tf_op jit(solution)/shard_map/ppermute | solution.py:17
  18.1 0.7 %shard_map.43 = f32[24,224]{1,0:T(8,128)S(1)} custom-call(bf16[3,8,1728]{2,1,0:T(8,128)(2,1)S(1)} %collective-permute-done.1.vectors_ref, bf16[3,224,1728]{2,1,0:T(8,128)(2,1)S(1)} %bitcast.3), custom_call_target="tpu_custom_call" | custom-call | flops 18579456 | bytes 1048576 | tf_op jit(solution)/shard_map/pallas_call | solution.py:228
  18.8 0.7 %collective-permute-done = f32[24,224]{1,0:T(8,128)S(1)} collective-permute-done((f32[24,224]{1,0:T(8,128)S(1)}, f32[24,224]{1,0:T(8,128)S(1)}, u32[]{:S(2)}, u32[]{:S(2)}) %collective-permute-start) | collective-permute-done | bytes 21536 | tf_op jit(solution)/shard_map/ppermute | solution.py:17
  19.5 10.7 %all_to_all.5.parts_ref = f32[8,24,224]{2,1,0:T(8,128)S(1)} all-to-all(f32[8,24,224]{2,1,0:T(8,128)S(1)} %broadcast_in_dim.2), channel_id=1, replica_groups=mesh['replica'=64,'tensor'=8] {'tensor'}, dimensions={0} | all-to-all | bytes 344064 | tf_op jit(solution)/shard_map/all_to_all | solution.py:270
  30.2 0.8 %shard_map.44 = (f32[24,224]{1,0:T(8,128)S(1)}, bf16[24,480]{1,0:T(8,128)(2,1)S(1)}) custom-call(f32[8,24,224]{2,1,0:T(8,128)S(1)} %all_to_all.5.parts_ref), custom_call_target="tpu_custom_call" | custom-call | flops 4644864 | bytes 1048576 | tf_op jit(solution)/shard_map/pallas_call | solution.py:228
  31.0 1.3 %collective-permute-start.3 = (bf16[24,480]{1,0:T(8,128)(2,1)S(1)}, bf16[24,480]{1,0:T(8,128)(2,1)S(1)}, u32[]{:S(2)}, u32[]{:S(2)}) collective-permute-start(bf16[24,480]{1,0:T(8,128)(2,1)S(1)} %get-tuple-element.13.basis_ref), channel_id=1, source_target_pairs={{0,504},{16,8},{32,24},{48,40},{64,56},{80,72},{96,88},{112,104},{... | collective-permute-start | bytes 69128 | tf_op jit(solution)/shard_map/ppermute | solution.py:29
  32.3 0.4 shard_map.45
  32.8 1.9 %collective-permute-start.2 = (bf16[24,2272]{1,0:T(8,128)(2,1)S(1)}, bf16[24,2272]{1,0:T(8,128)(2,1)S(1)}, u32[]{:S(2)}, u32[]{:S(2)}) collective-permute-start(bf16[24,2272]{1,0:T(8,128)(2,1)S(1)} %get-tuple-element.14), channel_id=1, source_target_pairs={{0,504},{8,0},{16,8},{24,16},{32,24},{40,32},{48,40},{56,48},{64,5... | collective-permute-start | bytes 327176 | tf_op jit(solution)/shard_map/ppermute | solution.py:17
  34.7 0.0 collective-permute-done.3.message_ref
  34.7 1.3 %collective-permute-start.4 = (bf16[24,1728]{1,0:T(8,128)(2,1)S(1)}, bf16[24,1728]{1,0:T(8,128)(2,1)S(1)}, u32[]{:S(2)}, u32[]{:S(2)}) collective-permute-start(bf16[24,1728]{1,0:T(8,128)(2,1)S(1)} %get-tuple-element.21), channel_id=1, source_target_pairs={{8,16},{24,32},{40,48},{56,64},{72,80},{88,96},{104,112},{120,128}... | collective-permute-start | bytes 248840 | tf_op jit(solution)/shard_map/ppermute | solution.py:29
  36.0 1.0 %collective-permute-done.2.message_ref = bf16[24,2272]{1,0:T(8,128)(2,1)S(1)} collective-permute-done((bf16[24,2272]{1,0:T(8,128)(2,1)S(1)}, bf16[24,2272]{1,0:T(8,128)(2,1)S(1)}, u32[]{:S(2)}, u32[]{:S(2)}) %collective-permute-start.2) | collective-permute-done | bytes 109088 | tf_op jit(solution)/shard_map/ppermute | solution.py:17
  37.0 0.4 shard_map.47
  37.4 1.5 %collective-permute-start.5 = (bf16[24,1728]{1,0:T(8,128)(2,1)S(1)}, bf16[24,1728]{1,0:T(8,128)(2,1)S(1)}, u32[]{:S(2)}, u32[]{:S(2)}) collective-permute-start(bf16[24,1728]{1,0:T(8,128)(2,1)S(1)} %get-tuple-element.22), channel_id=1, source_target_pairs={{0,8},{16,24},{32,40},{48,56},{64,72},{80,88},{96,104},{112,120},{... | collective-permute-start | bytes 248840 | tf_op jit(solution)/shard_map/ppermute | solution.py:29
  38.9 0.8 %shard_map.48 = (bf16[3,224,64]{2,1,0:T(8,128)(2,1)S(1)}, bf16[3,48,1728]{2,1,0:T(8,128)(2,1)S(1)}, f32[3,1,8,1728]{3,2,1,0:T(8,128)}) custom-call(bf16[24,2272]{1,0:T(8,128)(2,1)S(1)} %collective-permute-done.2.message_ref, f32[24,1728]{1,0:T(8,128)S(1)} %get-tuple-element.15.odd_products_ref, f32[24,1728]{1,0:T(8,128)S(1)} %get-tuple-element.16.even_products_ref, ...), custom_call_target="tpu_custom_call" | custom-call | flops 4644864 | bytes 1048576 | tf_op jit(solution)/shard_map/pallas_call | solution.py:228
  39.7 5.6 %collective-permute-done.4.odd_ref = bf16[24,1728]{1,0:T(8,128)(2,1)S(1)} collective-permute-done((bf16[24,1728]{1,0:T(8,128)(2,1)S(1)}, bf16[24,1728]{1,0:T(8,128)(2,1)S(1)}, u32[]{:S(2)}, u32[]{:S(2)}) %collective-permute-start.4) | collective-permute-done | bytes 82976 | tf_op jit(solution)/shard_map/ppermute | solution.py:29
  45.3 0.0 collective-permute-done.5.even_ref
  45.3 1.8 %shard_map.49 = bf16[3,1,224,1728]{3,2,1,0:T(8,128)(2,1)} custom-call(bf16[3,224,64]{2,1,0:T(8,128)(2,1)S(1)} %get-tuple-element.19.left_ref, bf16[3,48,1728]{2,1,0:T(8,128)(2,1)S(1)} %get-tuple-element.20.right_ref, bf16[24,1728]{1,0:T(8,128)(2,1)S(1)} %collective-permute-done.4.odd_ref, bf16[24,1728]{1,0:T(8,128)(2,1)S(1)} %collective-permute-done.5.even_ref, ...), custom_call_target="tpu_custom_call" | custom-call | flops 74317824 | bytes 1048576 | tf_op jit(solution)/shard_map/pallas_call | solution.py:228
  (3 shorter events, 0.0 us)
Async XLA Ops:
  0.6 3.0 %copy-start = (bf16[3,1,224,1728]{3,2,1,0:T(8,128)(2,1)S(1)}, bf16[3,1,224,1728]{3,2,1,0:T(8,128)(2,1)}, u32[]{:S(2)}) copy-start(bf16[3,1,224,1728]{3,2,1,0:T(8,128)(2,1)} %param.2) | copy-start | bytes 6967300
  1.7 16.4 %collective-permute-start.1 = (bf16[3,8,1728]{2,1,0:T(8,128)(2,1)S(1)}, bf16[3,8,1728]{2,1,0:T(8,128)(2,1)S(1)}, u32[]{:S(2)}, u32[]{:S(2)}) collective-permute-start(bf16[3,8,1728]{2,1,0:T(8,128)(2,1)S(1)} %shard_map.41.vectors_ref), channel_id=1, source_target_pairs={{0,8},{8,16},{16,24},{24,32},{32,40},{40,48},{48,56},{56,64},{64,7... | collective-permute-start | bytes 248840 | tf_op jit(solution)/shard_map/ppermute | solution.py:17
  4.4 15.1 %collective-permute-start = (f32[24,224]{1,0:T(8,128)S(1)}, f32[24,224]{1,0:T(8,128)S(1)}, u32[]{:S(2)}, u32[]{:S(2)}) collective-permute-start(f32[24,224]{1,0:T(8,128)S(1)} %shard_map.42), channel_id=1, source_target_pairs={{0,8},{8,16},{16,24},{24,32},{32,40},{40,48},{48,56},{56,64},{64,7... | collective-permute-start | bytes 64520 | tf_op jit(solution)/shard_map/ppermute | solution.py:17
  31.0 3.7 %collective-permute-start.3 = (bf16[24,480]{1,0:T(8,128)(2,1)S(1)}, bf16[24,480]{1,0:T(8,128)(2,1)S(1)}, u32[]{:S(2)}, u32[]{:S(2)}) collective-permute-start(bf16[24,480]{1,0:T(8,128)(2,1)S(1)} %get-tuple-element.13.basis_ref), channel_id=1, source_target_pairs={{0,504},{16,8},{32,24},{48,40},{64,56},{80,72},{96,88},{112,104},{... | collective-permute-start | bytes 69128 | tf_op jit(solution)/shard_map/ppermute | solution.py:29
  32.8 4.2 %collective-permute-start.2 = (bf16[24,2272]{1,0:T(8,128)(2,1)S(1)}, bf16[24,2272]{1,0:T(8,128)(2,1)S(1)}, u32[]{:S(2)}, u32[]{:S(2)}) collective-permute-start(bf16[24,2272]{1,0:T(8,128)(2,1)S(1)} %get-tuple-element.14), channel_id=1, source_target_pairs={{0,504},{8,0},{16,8},{24,16},{32,24},{40,32},{48,40},{56,48},{64,5... | collective-permute-start | bytes 327176 | tf_op jit(solution)/shard_map/ppermute | solution.py:17
  34.7 10.6 %collective-permute-start.4 = (bf16[24,1728]{1,0:T(8,128)(2,1)S(1)}, bf16[24,1728]{1,0:T(8,128)(2,1)S(1)}, u32[]{:S(2)}, u32[]{:S(2)}) collective-permute-start(bf16[24,1728]{1,0:T(8,128)(2,1)S(1)} %get-tuple-element.21), channel_id=1, source_target_pairs={{8,16},{24,32},{40,48},{56,64},{72,80},{88,96},{104,112},{120,128}... | collective-permute-start | bytes 248840 | tf_op jit(solution)/shard_map/ppermute | solution.py:29
  37.4 7.9 %collective-permute-start.5 = (bf16[24,1728]{1,0:T(8,128)(2,1)S(1)}, bf16[24,1728]{1,0:T(8,128)(2,1)S(1)}, u32[]{:S(2)}, u32[]{:S(2)}) collective-permute-start(bf16[24,1728]{1,0:T(8,128)(2,1)S(1)} %get-tuple-element.22), channel_id=1, source_target_pairs={{0,8},{16,24},{32,40},{48,56},{64,72},{80,88},{96,104},{112,120},{... | collective-permute-start | bytes 248840 | tf_op jit(solution)/shard_map/ppermute | solution.py:29

commit v5 on v4

--- a/solution.py
+++ b/solution.py
@@ -39,12 +39,53 @@
     return lax.rem(lax.axis_index("replica"), 2) == 1
 
 
-def images_kernel(vectors_ref, window_ref, images_ref):
+def images_of(vectors, window_ref, mat):
+    return lax.dot_general(
+        vectors.astype(jnp.bfloat16), window_ref[mat], ROWS_BY_ROWS, preferred_element_type=jnp.float32
+    )
+
+
+def own_images_kernel(vectors_ref, window_ref, images_ref, message_ref):
+    mats, _, columns = vectors_ref.shape
+    row_count = window_ref.shape[1]
+    images = jnp.concatenate([images_of(vectors_ref[mat], window_ref, mat) for mat in range(mats)], 0)
+    images_ref[...] = images
+    vectors = jnp.concatenate([vectors_ref[mat].astype(jnp.float32) for mat in range(mats)], 0)
+    message_ref[:, :columns] = vectors.astype(jnp.bfloat16)
+    for part in range(3):
+        start = padded(columns) + part * padded(row_count)
+        high, images = split(images)
+        message_ref[:, start : start + row_count] = high.astype(jnp.bfloat16)
+
+
+def odd_images_kernel(vectors_ref, window_ref, images_ref):
     mats, rank, _ = vectors_ref.shape
-    for mat in range(mats):
-        images_ref[mat * rank : (mat + 1) * rank] = lax.dot_general(
-            vectors_ref[mat], window_ref[mat], ROWS_BY_ROWS, preferred_element_type=jnp.float32
+
+    @pl.when(jnp.logical_not(odd_replica()))
+    def _():
+        for mat in range(mats):
+            images_ref[mat * rank : (mat + 1) * rank] = images_of(vectors_ref[mat], window_ref, mat)
+
+
+def differences_kernel(even_message_ref, odd_left_ref, odd_images_ref, window_ref, differences_ref):
+    mats, row_count, columns = window_ref.shape
+    rank = odd_images_ref.shape[0] // mats
+
+    @pl.when(odd_replica())
+    def _():
+        starts = [padded(columns) + part * padded(row_count) for part in range(3)]
+        high, middle, low = (
+            even_message_ref[:, start : start + row_count].astype(jnp.float32) for start in starts
         )
+        left_images = high + (middle + low)
+        vectors = even_message_ref[:, :columns].astype(jnp.float32)
+        for mat in range(mats):
+            rows = slice(mat * rank, (mat + 1) * rank)
+            differences_ref[rows] = left_images[rows] - images_of(vectors[rows], window_ref, mat)
+
+    @pl.when(jnp.logical_not(odd_replica()))
+    def _():
+        differences_ref[...] = odd_left_ref[...] - odd_images_ref[...]
 
 
 def round_kernel(vectors_hbm, rounded_ref, held_ref, sem):
@@ -54,87 +95,36 @@
     rounded_ref[...] = held_ref[...].astype(jnp.bfloat16)
 
 
-def own_images_kernel(vectors_ref, window_ref, images_ref, vectors_out_ref):
-    mats, rank, _ = vectors_ref.shape
-    vectors_out_ref[...] = vectors_ref[...]
-    for mat in range(mats):
-        images_ref[mat * rank : (mat + 1) * rank] = images_of(vectors_ref[mat], window_ref[mat])
-
-
-def differences_kernel(
-    even_images_ref, even_vectors_ref, odd_images_ref, odd_vectors_ref, window_ref, differences_ref
-):
-    mats, rank, _ = odd_vectors_ref.shape
-    odd = odd_replica()
-
-    def chosen(if_odd, if_even):
-        return jnp.where(odd, if_odd.astype(jnp.float32), if_even.astype(jnp.float32))
-
-    for mat in range(mats):
-        rows = slice(mat * rank, (mat + 1) * rank)
-        vectors = chosen(even_vectors_ref[mat], odd_vectors_ref[mat]).astype(jnp.bfloat16)
-        images = chosen(even_images_ref[rows], odd_images_ref[rows])
-        differences_ref[rows] = images - images_of(vectors, window_ref[mat])
-
-
-def round_kernel(vectors_hbm, rounded_ref, held_ref, sem):
-    copy = pltpu.make_async_copy(vectors_hbm, held_ref, sem)
-    copy.start()
-    copy.wait()
-    rounded_ref[...] = held_ref[...].astype(jnp.bfloat16)
-
-
-def own_images_kernel(vectors_ref, window_ref, images_ref, vectors_out_ref):
-    mats, rank, _ = vectors_ref.shape
-    vectors_out_ref[...] = vectors_ref[...]
-    for mat in range(mats):
-        images_ref[mat * rank : (mat + 1) * rank] = images_of(vectors_ref[mat], window_ref[mat])
-
-
-def next_images_kernel(even_ref, odd_ref, window_ref, images_ref):
-    mats, rank, _ = odd_ref.shape
-    odd = odd_replica()
-    for mat in range(mats):
-        vectors = jnp.where(odd, even_ref[mat].astype(jnp.float32), odd_ref[mat].astype(jnp.float32))
-        images_ref[mat * rank : (mat + 1) * rank] = images_of(vectors.astype(jnp.bfloat16), window_ref[mat])
-
-
 def orthonormal_rows(gram, images, rank):
     mats = gram.shape[0] // rank
-    grams = [gram[mat * rank : (mat + 1) * rank] for mat in range(mats)]
+    count = images.shape[1]
+
+    def column(mat, step):
+        at = mat * rank + step
+        return jnp.broadcast_to(gram[mat * rank : (mat + 1) * rank, at : at + 1], (rank, LANES))
+
+    def widened(value):
+        return jnp.concatenate([value] * (padded(count) // LANES), 1)[:, :count]
+
+    place = lax.broadcasted_iota(jnp.int32, (rank, LANES), 0)
+    columns = [[column(mat, step) for step in range(rank)] for mat in range(mats)]
     rows = [images[mat * rank : (mat + 1) * rank] for mat in range(mats)]
-    place = lax.broadcasted_iota(jnp.int32, (rank, 1), 0)
-    pivots = [jnp.ones((rank, 1), jnp.float32) for _ in range(mats)]
+    pivots = [jnp.ones((rank, LANES), jnp.float32) for _ in range(mats)]
     for step in range(rank):
         for mat in range(mats):
-            column = grams[mat][:, mat * rank + step : mat * rank + step + 1]
-            pivot = column[step : step + 1]
+            pivot = columns[mat][step][step : step + 1]
             pivots[mat] = jnp.where(place == step, pivot, pivots[mat])
+            factor = jnp.where(place > step, columns[mat][step] / pivot, 0.0)
+            for later in range(step + 1, rank):
+                columns[mat][later] = columns[mat][later] - factor * columns[mat][later][step : step + 1]
             if step < rank - 1:
-                factor = jnp.where(place > step, column / pivot, 0.0)
-                rows[mat] = rows[mat] - factor * rows[mat][step : step + 1]
-                grams[mat] = grams[mat] - factor * grams[mat][step : step + 1]
-    return jnp.concatenate([row / jnp.sqrt(pivot) for row, pivot in zip(rows, pivots)], 0)
+                rows[mat] = rows[mat] - widened(factor) * rows[mat][step : step + 1]
+    return jnp.concatenate([row / widened(jnp.sqrt(pivot)) for row, pivot in zip(rows, pivots)], 0)
 
 
 def split(value):
     high = value.astype(jnp.bfloat16).astype(jnp.float32)
     return high, value - high
-
-
-def basis_kernel(mats, parts_ref, basis_ref, message_ref):
-    rank = parts_ref.shape[1] // mats
-    row_count = parts_ref.shape[2]
-    images = jnp.sum(parts_ref[...], 0)
-    gram = lax.dot_general(
-        images, images, ROWS_BY_ROWS, precision=lax.Precision.HIGHEST, preferred_element_type=jnp.float32
-    )
-    basis = orthonormal_rows(gram, images, rank)
-    basis_ref[...] = basis
-    high, low = split(basis)
-    message_ref[:, :row_count] = high.astype(jnp.bfloat16)
-    start = padded(row_count)
-    message_ref[:, start : start + row_count] = low.astype(jnp.bfloat16)
 
 
 def products_into(basis_ref, window_ref, products_ref, rounded_ref):
@@ -149,10 +139,35 @@
     rounded_ref[...] = products_ref[...].astype(jnp.bfloat16)
 
 
-def lower_products_kernel(basis_ref, window_ref, products_ref, message_ref):
+def lower_products(basis_ref, window_ref, products_ref, message_ref):
     columns = products_ref.shape[1]
     products_into(basis_ref, window_ref, products_ref, message_ref.at[:, :columns])
     message_ref[:, padded(columns) :] = basis_ref[...]
+
+
+def basis_kernel(parts_ref, window_ref, basis_ref, parts_out_ref, products_ref, message_ref):
+    rank = parts_ref.shape[1] // window_ref.shape[0]
+    row_count = parts_ref.shape[2]
+    images = jnp.sum(parts_ref[...], 0)
+    gram = lax.dot_general(
+        images, images, ROWS_BY_ROWS, precision=lax.Precision.HIGHEST, preferred_element_type=jnp.float32
+    )
+    basis = orthonormal_rows(gram, images, rank)
+    basis_ref[...] = basis
+    high, low = split(basis)
+    parts_out_ref[:, :row_count] = high.astype(jnp.bfloat16)
+    start = padded(row_count)
+    parts_out_ref[:, start : start + row_count] = low.astype(jnp.bfloat16)
+
+    @pl.when(jnp.logical_not(odd_replica()))
+    def _():
+        lower_products(parts_out_ref, window_ref, products_ref, message_ref)
+
+
+def odd_products_kernel(basis_ref, window_ref, _, __, products_ref, message_ref):
+    @pl.when(odd_replica())
+    def _():
+        lower_products(basis_ref, window_ref, products_ref, message_ref)
 
 
 def upper_products_kernel(odd, start, message_ref, window_ref, products_ref, rounded_ref):
@@ -262,28 +277,33 @@
         in_specs=[pl.BlockSpec(memory_space=pltpu.HBM)],
         scratch_shapes=[pltpu.VMEM(own_vectors.shape, f32), pltpu.SemaphoreType.DMA],
     )(pltpu.with_memory_space_constraint(own_vectors, pltpu.HBM))
-    left_vectors = shifted(vectors_b, "replica", 1)
-    own_images = call(images_kernel, images, flops)(vectors_b, window)
-    left_images = shifted(own_images, "replica", 1)
-    next_images = call(images_kernel, images, flops)(left_vectors, window)
+    odd_up, even_up = parity_shifts("replica", 1)
+    odd_down, _ = parity_shifts("replica", -1)
+    base = padded(columns)
+    odd_vectors = odd_up(vectors_b)
+    own_images, message = call(
+        own_images_kernel, (images, whole(bf16, stacked, base + 2 * padded(row_count) + row_count)), 400 * flops
+    )(vectors_b, window)
+    odd_left = odd_up(own_images)
+    even_message = even_up(message)
+    odd_images = call(odd_images_kernel, images, 400 * flops)(odd_vectors, window)
+    differences = call(differences_kernel, images, flops)(even_message, odd_left, odd_images, window)
     group = lax.axis_size("tensor")
     parts = lax.all_to_all(
-        jnp.broadcast_to((left_images - next_images)[None], (group, stacked, row_count)), "tensor", 0, 0
-    )
-    lower_basis, basis = call(
-        functools.partial(basis_kernel, mats),
-        (images, whole(bf16, stacked, padded(row_count) + row_count)),
-        flops // 4,
-    )(parts)
+        jnp.broadcast_to(differences[None], (group, stacked, row_count)), "tensor", 0, 0
+    )
+    message_out = whole(bf16, stacked, base + padded(row_count) + row_count)
+    lower_basis, basis, lower_products, message = call(
+        basis_kernel,
+        (images, whole(bf16, stacked, padded(row_count) + row_count), products, message_out),
+        flops,
+    )(parts, window)
     products_outs = (products, rounded_products)
-    base = padded(columns)
-    odd_up, even_up = parity_shifts("replica", 1)
-    odd_down, _ = parity_shifts("replica", -1)
 
     odd_basis = odd_down(basis)
     lower_products, message = call(
-        lower_products_kernel, (products, whole(bf16, stacked, base + basis.shape[1])), 400 * flops
-    )(basis, window)
+        odd_products_kernel, (products, message_out), 400 * flops, input_output_aliases={2: 0, 3: 1}
+    )(basis, window, lower_products, message)
     message = shifted(message, "replica", -1)
     odd_upper, rounded_upper = call(functools.partial(upper_products_kernel, True, 0), products_outs, 400 * flops)(
         odd_basis, window

time: 47.4 us -> 47.1 us (level)
  starting transfers between devices: 11.5 us -> 13.8 us
  waiting for transfers between devices: 17.3 us -> 15 us
    ppermute x3 -> x1, waiting for transfers between devices: 11.7 us -> 0.97 us  [shifted(): lax.ppermute(value, axis, [(source, (source + steps) % count) for source...]
    ppermute x3 -> x6, waiting for transfers between devices: 5.6 us -> 14 us  [over(): return lambda value: lax.ppermute(value, axis, pairs)]
    ppermute x3 -> x6, starting transfers between devices: 4.05 us -> 11.9 us  [over(): return lambda value: lax.ppermute(value, axis, pairs)]
    ppermute x3 -> x1, starting transfers between devices: 7.46 us -> 1.92 us  [shifted(): lax.ppermute(value, axis, [(source, (source + steps) % count) for source...]
    pallas_call x9 -> x10, Pallas kernels: 6.85 us -> 6.46 us  [run(): pl.pallas_call(kernel, out_shape=outs, in_specs=[IN_VMEM] * len(operands)...]
  transfers between devices with their start and end apart: 6 -> 7, of which waited for: 4 -> 3; matrix products, arithmetic and copies ran while one was open for 0% -> 0% of each run, Pallas kernels for 7% -> 6%
where the time goes in v5:
time: 47.1 us; the launch traced here: 46.9 us
  waiting for transfers between devices  15 us (32%)
  starting transfers between devices  13.8 us (29%)
  blocking collectives  10.8 us (23%)
  Pallas kernels  6.46 us (14%)
  between operations  0.76 us (2%)
    ppermute x6, waiting for transfers between devices, over(): return lambda value: lax.ppermute(value, axis, pairs)  14 us
    ppermute x6, starting transfers between devices, over(): return lambda value: lax.ppermute(value, axis, pairs)  11.9 us
    all_to_all x1, blocking collectives, shards(): lax.all_to_all(jnp.broadcast_to(differences[None], (group, stacked, row_c...  10.8 us
    pallas_call x10, Pallas kernels, run(): pl.pallas_call(kernel, out_shape=outs, in_specs=[IN_VMEM] * len(operands)...  6.46 us
    ppermute x1, starting transfers between devices, shifted(): lax.ppermute(value, axis, [(source, (source + steps) % count) for source...  1.92 us
    ppermute x1, waiting for transfers between devices, shifted(): lax.ppermute(value, axis, [(source, (source + steps) % count) for source...  0.97 us
  transfers between devices with their start and end apart: 7, of which 3 were waited for; matrix products, arithmetic and copies ran while one was open for 0% of the time, Pallas kernels for 6%

profile of v5, /device:TPU:2, one launch (start us, length us, event | category | flops | bytes accessed | tf_op | source)
XLA Modules:
  0.0 46.9 jit_solution(17110347786308225532)
XLA Ops:
  0.6 0.0 copy-start
  0.6 1.1 %shard_map.41.vectors_ref = bf16[3,8,1728]{2,1,0:T(8,128)(2,1)S(1)} custom-call(f32[3,8,1728]{2,1,0:T(8,128)} %bitcast.10), custom_call_target="tpu_custom_call" | custom-call | flops 1857945600 | bytes 1048576 | tf_op jit(solution)/shard_map/pallas_call | solution.py:243
  1.7 1.3 %collective-permute-start.2 = (bf16[3,8,1728]{2,1,0:T(8,128)(2,1)S(1)}, bf16[3,8,1728]{2,1,0:T(8,128)(2,1)S(1)}, u32[]{:S(2)}, u32[]{:S(2)}) collective-permute-start(bf16[3,8,1728]{2,1,0:T(8,128)(2,1)S(1)} %shard_map.41.vectors_ref), channel_id=1, source_target_pairs={{8,16},{24,32},{40,48},{56,64},{72,80},{88,96},{104,112},{120,128}... | collective-permute-start | bytes 248840 | tf_op jit(solution)/shard_map/ppermute | solution.py:29
  3.0 0.0 copy-done
  3.0 0.7 %shard_map.42 = (f32[24,224]{1,0:T(8,128)S(1)}, bf16[24,2528]{1,0:T(8,128)(2,1)S(1)}) custom-call(bf16[3,8,1728]{2,1,0:T(8,128)(2,1)S(1)} %shard_map.41.vectors_ref, bf16[3,224,1728]{2,1,0:T(8,128)(2,1)S(1)} %bitcast.2), custom_call_target="tpu_custom_call" | custom-call | flops 7431782400 | bytes 1048576 | tf_op jit(solution)/shard_map/pallas_call | solution.py:243
  3.8 1.3 %collective-permute-start.1 = (f32[24,224]{1,0:T(8,128)S(1)}, f32[24,224]{1,0:T(8,128)S(1)}, u32[]{:S(2)}, u32[]{:S(2)}) collective-permute-start(f32[24,224]{1,0:T(8,128)S(1)} %get-tuple-element.18), channel_id=1, source_target_pairs={{8,16},{24,32},{40,48},{56,64},{72,80},{88,96},{104,112},{120,128}... | collective-permute-start | bytes 64520 | tf_op jit(solution)/shard_map/ppermute | solution.py:29
  5.1 4.2 %collective-permute-start = (bf16[24,2528]{1,0:T(8,128)(2,1)S(1)}, bf16[24,2528]{1,0:T(8,128)(2,1)S(1)}, u32[]{:S(2)}, u32[]{:S(2)}) collective-permute-start(bf16[24,2528]{1,0:T(8,128)(2,1)S(1)} %get-tuple-element.17), channel_id=1, source_target_pairs={{0,8},{16,24},{32,40},{48,56},{64,72},{80,88},{96,104},{112,120},{... | collective-permute-start | bytes 364040 | tf_op jit(solution)/shard_map/ppermute | solution.py:29
  9.3 8.1 %collective-permute-done.2.vectors_ref = bf16[3,8,1728]{2,1,0:T(8,128)(2,1)S(1)} collective-permute-done((bf16[3,8,1728]{2,1,0:T(8,128)(2,1)S(1)}, bf16[3,8,1728]{2,1,0:T(8,128)(2,1)S(1)}, u32[]{:S(2)}, u32[]{:S(2)}) %collective-permute-start.2) | collective-permute-done | bytes 82976 | tf_op jit(solution)/shard_map/ppermute | solution.py:29
  17.5 0.7 %shard_map.43.odd_images_ref = f32[24,224]{1,0:T(8,128)S(1)} custom-call(bf16[3,8,1728]{2,1,0:T(8,128)(2,1)S(1)} %collective-permute-done.2.vectors_ref, bf16[3,224,1728]{2,1,0:T(8,128)(2,1)S(1)} %bitcast.3), custom_call_target="tpu_custom_call" | custom-call | flops 7431782400 | bytes 1048576 | tf_op jit(solution)/shard_map/pallas_call | solution.py:243
  18.2 0.0 collective-permute-done.1.odd_left_ref
  18.2 0.0 collective-permute-done.even_message_ref
  18.3 10.8 %all_to_all.5.parts_ref = f32[8,24,224]{2,1,0:T(8,128)S(1)} all-to-all(f32[8,24,224]{2,1,0:T(8,128)S(1)} %broadcast_in_dim.2), channel_id=1, replica_groups=mesh['replica'=64,'tensor'=8] {'tensor'}, dimensions={0} | all-to-all | bytes 344064 | tf_op jit(solution)/shard_map/all_to_all | solution.py:292
  29.1 0.8 %shard_map.45 = (f32[24,224]{1,0:T(8,128)S(1)}, bf16[24,480]{1,0:T(8,128)(2,1)S(1)}, f32[24,1728]{1,0:T(8,128)S(1)}, bf16[24,2272]{1,0:T(8,128)(2,1)S(1)}) custom-call(f32[8,24,224]{2,1,0:T(8,128)S(1)} %all_to_all.5.parts_ref, bf16[3,224,1728]{2,1,0:T(8,128)(2,1)S(1)} %bitcast.5), custom_call_target="tpu_custom_call" | custom-call | flops 18579456 | bytes 1048576 | tf_op jit(solution)/shard_map/pallas_call | solution.py:243
  29.8 2.3 %collective-permute-start.4 = (bf16[24,480]{1,0:T(8,128)(2,1)S(1)}, bf16[24,480]{1,0:T(8,128)(2,1)S(1)}, u32[]{:S(2)}, u32[]{:S(2)}) collective-permute-start(bf16[24,480]{1,0:T(8,128)(2,1)S(1)} %get-tuple-element.19.basis_ref), channel_id=1, source_target_pairs={{0,504},{16,8},{32,24},{48,40},{64,56},{80,72},{96,88},{112,104},{... | collective-permute-start | bytes 69128 | tf_op jit(solution)/shard_map/ppermute | solution.py:29
  32.2 1.9 %collective-permute-start.3 = (bf16[24,2272]{1,0:T(8,128)(2,1)S(1)}, bf16[24,2272]{1,0:T(8,128)(2,1)S(1)}, u32[]{:S(2)}, u32[]{:S(2)}) collective-permute-start(bf16[24,2272]{1,0:T(8,128)(2,1)S(1)} %get-tuple-element.22), channel_id=1, source_target_pairs={{0,504},{8,0},{16,8},{24,16},{32,24},{40,32},{48,40},{56,48},{64,5... | collective-permute-start | bytes 327176 | tf_op jit(solution)/shard_map/ppermute | solution.py:17
  34.1 0.0 collective-permute-done.4.message_ref
  34.2 1.3 %collective-permute-start.5 = (bf16[24,1728]{1,0:T(8,128)(2,1)S(1)}, bf16[24,1728]{1,0:T(8,128)(2,1)S(1)}, u32[]{:S(2)}, u32[]{:S(2)}) collective-permute-start(bf16[24,1728]{1,0:T(8,128)(2,1)S(1)} %get-tuple-element.29), channel_id=1, source_target_pairs={{8,16},{24,32},{40,48},{56,64},{72,80},{88,96},{104,112},{120,128}... | collective-permute-start | bytes 248840 | tf_op jit(solution)/shard_map/ppermute | solution.py:29
  35.5 1.0 %collective-permute-done.3.message_ref = bf16[24,2272]{1,0:T(8,128)(2,1)S(1)} collective-permute-done((bf16[24,2272]{1,0:T(8,128)(2,1)S(1)}, bf16[24,2272]{1,0:T(8,128)(2,1)S(1)}, u32[]{:S(2)}, u32[]{:S(2)}) %collective-permute-start.3) | collective-permute-done | bytes 109088 | tf_op jit(solution)/shard_map/ppermute | solution.py:17
  36.5 0.4 shard_map.48
  36.9 1.5 %collective-permute-start.6 = (bf16[24,1728]{1,0:T(8,128)(2,1)S(1)}, bf16[24,1728]{1,0:T(8,128)(2,1)S(1)}, u32[]{:S(2)}, u32[]{:S(2)}) collective-permute-start(bf16[24,1728]{1,0:T(8,128)(2,1)S(1)} %get-tuple-element.30), channel_id=1, source_target_pairs={{0,8},{16,24},{32,40},{48,56},{64,72},{80,88},{96,104},{112,120},{... | collective-permute-start | bytes 248840 | tf_op jit(solution)/shard_map/ppermute | solution.py:29
  38.4 0.8 %shard_map.49 = (bf16[3,224,64]{2,1,0:T(8,128)(2,1)S(1)}, bf16[3,48,1728]{2,1,0:T(8,128)(2,1)S(1)}, f32[3,1,8,1728]{3,2,1,0:T(8,128)}) custom-call(bf16[24,2272]{1,0:T(8,128)(2,1)S(1)} %collective-permute-done.3.message_ref, f32[24,1728]{1,0:T(8,128)S(1)} %get-tuple-element.23.odd_products_ref, f32[24,1728]{1,0:T(8,128)S(1)} %get-tuple-element.24.even_products_ref, ...), custom_call_target="tpu_custom_call" | custom-call | flops 4644864 | bytes 1048576 | tf_op jit(solution)/shard_map/pallas_call | solution.py:243
  39.2 5.9 %collective-permute-done.5.odd_ref = bf16[24,1728]{1,0:T(8,128)(2,1)S(1)} collective-permute-done((bf16[24,1728]{1,0:T(8,128)(2,1)S(1)}, bf16[24,1728]{1,0:T(8,128)(2,1)S(1)}, u32[]{:S(2)}, u32[]{:S(2)}) %collective-permute-start.5) | collective-permute-done | bytes 82976 | tf_op jit(solution)/shard_map/ppermute | solution.py:29
  45.0 0.0 collective-permute-done.6.even_ref
  45.1 1.8 %shard_map.50 = bf16[3,1,224,1728]{3,2,1,0:T(8,128)(2,1)} custom-call(bf16[3,224,64]{2,1,0:T(8,128)(2,1)S(1)} %get-tuple-element.27.left_ref, bf16[3,48,1728]{2,1,0:T(8,128)(2,1)S(1)} %get-tuple-element.28.right_ref, bf16[24,1728]{1,0:T(8,128)(2,1)S(1)} %collective-permute-done.5.odd_ref, bf16[24,1728]{1,0:T(8,128)(2,1)S(1)} %collective-permute-done.6.even_ref, ...), custom_call_target="tpu_custom_call" | custom-call | flops 74317824 | bytes 1048576 | tf_op jit(solution)/shard_map/pallas_call | solution.py:243
  (4 shorter events, 0.1 us)
Async XLA Ops:
  0.6 2.4 %copy-start = (bf16[3,1,224,1728]{3,2,1,0:T(8,128)(2,1)S(1)}, bf16[3,1,224,1728]{3,2,1,0:T(8,128)(2,1)}, u32[]{:S(2)}) copy-start(bf16[3,1,224,1728]{3,2,1,0:T(8,128)(2,1)} %param.2) | copy-start | bytes 6967300
  1.7 15.7 %collective-permute-start.2 = (bf16[3,8,1728]{2,1,0:T(8,128)(2,1)S(1)}, bf16[3,8,1728]{2,1,0:T(8,128)(2,1)S(1)}, u32[]{:S(2)}, u32[]{:S(2)}) collective-permute-start(bf16[3,8,1728]{2,1,0:T(8,128)(2,1)S(1)} %shard_map.41.vectors_ref), channel_id=1, source_target_pairs={{8,16},{24,32},{40,48},{56,64},{72,80},{88,96},{104,112},{120,128}... | collective-permute-start | bytes 248840 | tf_op jit(solution)/shard_map/ppermute | solution.py:29
  3.8 14.4 %collective-permute-start.1 = (f32[24,224]{1,0:T(8,128)S(1)}, f32[24,224]{1,0:T(8,128)S(1)}, u32[]{:S(2)}, u32[]{:S(2)}) collective-permute-start(f32[24,224]{1,0:T(8,128)S(1)} %get-tuple-element.18), channel_id=1, source_target_pairs={{8,16},{24,32},{40,48},{56,64},{72,80},{88,96},{104,112},{120,128}... | collective-permute-start | bytes 64520 | tf_op jit(solution)/shard_map/ppermute | solution.py:29
  5.1 13.1 %collective-permute-start = (bf16[24,2528]{1,0:T(8,128)(2,1)S(1)}, bf16[24,2528]{1,0:T(8,128)(2,1)S(1)}, u32[]{:S(2)}, u32[]{:S(2)}) collective-permute-start(bf16[24,2528]{1,0:T(8,128)(2,1)S(1)} %get-tuple-element.17), channel_id=1, source_target_pairs={{0,8},{16,24},{32,40},{48,56},{64,72},{80,88},{96,104},{112,120},{... | collective-permute-start | bytes 364040 | tf_op jit(solution)/shard_map/ppermute | solution.py:29
  29.8 4.3 %collective-permute-start.4 = (bf16[24,480]{1,0:T(8,128)(2,1)S(1)}, bf16[24,480]{1,0:T(8,128)(2,1)S(1)}, u32[]{:S(2)}, u32[]{:S(2)}) collective-permute-start(bf16[24,480]{1,0:T(8,128)(2,1)S(1)} %get-tuple-element.19.basis_ref), channel_id=1, source_target_pairs={{0,504},{16,8},{32,24},{48,40},{64,56},{80,72},{96,88},{112,104},{... | collective-permute-start | bytes 69128 | tf_op jit(solution)/shard_map/ppermute | solution.py:29
  32.2 4.2 %collective-permute-start.3 = (bf16[24,2272]{1,0:T(8,128)(2,1)S(1)}, bf16[24,2272]{1,0:T(8,128)(2,1)S(1)}, u32[]{:S(2)}, u32[]{:S(2)}) collective-permute-start(bf16[24,2272]{1,0:T(8,128)(2,1)S(1)} %get-tuple-element.22), channel_id=1, source_target_pairs={{0,504},{8,0},{16,8},{24,16},{32,24},{40,32},{48,40},{56,48},{64,5... | collective-permute-start | bytes 327176 | tf_op jit(solution)/shard_map/ppermute | solution.py:17
  34.2 10.9 %collective-permute-start.5 = (bf16[24,1728]{1,0:T(8,128)(2,1)S(1)}, bf16[24,1728]{1,0:T(8,128)(2,1)S(1)}, u32[]{:S(2)}, u32[]{:S(2)}) collective-permute-start(bf16[24,1728]{1,0:T(8,128)(2,1)S(1)} %get-tuple-element.29), channel_id=1, source_target_pairs={{8,16},{24,32},{40,48},{56,64},{72,80},{88,96},{104,112},{120,128}... | collective-permute-start | bytes 248840 | tf_op jit(solution)/shard_map/ppermute | solution.py:29
  36.9 8.2 %collective-permute-start.6 = (bf16[24,1728]{1,0:T(8,128)(2,1)S(1)}, bf16[24,1728]{1,0:T(8,128)(2,1)S(1)}, u32[]{:S(2)}, u32[]{:S(2)}) collective-permute-start(bf16[24,1728]{1,0:T(8,128)(2,1)S(1)} %get-tuple-element.30), channel_id=1, source_target_pairs={{0,8},{16,24},{32,40},{48,56},{64,72},{80,88},{96,104},{112,120},{... | collective-permute-start | bytes 248840 | tf_op jit(solution)/shard_map/ppermute | solution.py:29

commit v6 on v5

--- a/solution.py
+++ b/solution.py
@@ -46,25 +46,34 @@
 
 
 def own_images_kernel(vectors_ref, window_ref, images_ref, message_ref):
-    mats, _, columns = vectors_ref.shape
-    row_count = window_ref.shape[1]
-    images = jnp.concatenate([images_of(vectors_ref[mat], window_ref, mat) for mat in range(mats)], 0)
+    mats, row_count, columns = window_ref.shape
+    rank = images_ref.shape[0] // mats
+    vectors = vectors_ref[...].astype(jnp.float32)
+    images = jnp.concatenate(
+        [images_of(vectors[mat * rank : (mat + 1) * rank], window_ref, mat) for mat in range(mats)], 0
+    )
     images_ref[...] = images
-    vectors = jnp.concatenate([vectors_ref[mat].astype(jnp.float32) for mat in range(mats)], 0)
-    message_ref[:, :columns] = vectors.astype(jnp.bfloat16)
-    for part in range(3):
-        start = padded(columns) + part * padded(row_count)
-        high, images = split(images)
-        message_ref[:, start : start + row_count] = high.astype(jnp.bfloat16)
+
+    @pl.when(jnp.logical_not(odd_replica()))
+    def _():
+        message_ref[:, :columns] = vectors_ref[...]
+        rest = images
+        for part in range(3):
+            start = padded(columns) + part * padded(row_count)
+            high, rest = split(rest)
+            message_ref[:, start : start + row_count] = high.astype(jnp.bfloat16)
 
 
 def odd_images_kernel(vectors_ref, window_ref, images_ref):
-    mats, rank, _ = vectors_ref.shape
+    mats = window_ref.shape[0]
+    rank = images_ref.shape[0] // mats
 
     @pl.when(jnp.logical_not(odd_replica()))
     def _():
+        vectors = vectors_ref[...].astype(jnp.float32)
         for mat in range(mats):
-            images_ref[mat * rank : (mat + 1) * rank] = images_of(vectors_ref[mat], window_ref, mat)
+            rows = slice(mat * rank, (mat + 1) * rank)
+            images_ref[rows] = images_of(vectors[rows], window_ref, mat)
 
 
 def differences_kernel(even_message_ref, odd_left_ref, odd_images_ref, window_ref, differences_ref):
@@ -92,7 +101,8 @@
     copy = pltpu.make_async_copy(vectors_hbm, held_ref, sem)
     copy.start()
     copy.wait()
-    rounded_ref[...] = held_ref[...].astype(jnp.bfloat16)
+    mats = held_ref.shape[0]
+    rounded_ref[...] = jnp.concatenate([held_ref[mat] for mat in range(mats)], 0).astype(jnp.bfloat16)
 
 
 def orthonormal_rows(gram, images, rank):
@@ -272,7 +282,7 @@
 
     vectors_b = call(
         round_kernel,
-        whole(bf16, *own_vectors.shape),
+        rounded_products,
         100 * flops,
         in_specs=[pl.BlockSpec(memory_space=pltpu.HBM)],
         scratch_shapes=[pltpu.VMEM(own_vectors.shape, f32), pltpu.SemaphoreType.DMA],

time: 47.1 us -> 47.1 us (level)
  no operation moved by 1% of the time
where the time goes in v6:
time: 47.1 us; the launch traced here: 46.8 us
  waiting for transfers between devices  15 us (32%)
  starting transfers between devices  13.8 us (29%)
  blocking collectives  10.8 us (23%)
  Pallas kernels  6.46 us (14%)
  between operations  0.76 us (2%)
    ppermute x6, waiting for transfers between devices, over(): return lambda value: lax.ppermute(value, axis, pairs)  14 us
    ppermute x6, starting transfers between devices, over(): return lambda value: lax.ppermute(value, axis, pairs)  11.9 us
    all_to_all x1, blocking collectives, shards(): lax.all_to_all(jnp.broadcast_to(differences[None], (group, stacked, row_c...  10.8 us
    pallas_call x10, Pallas kernels, run(): pl.pallas_call(kernel, out_shape=outs, in_specs=[IN_VMEM] * len(operands)...  6.46 us
    ppermute x1, starting transfers between devices, shifted(): lax.ppermute(value, axis, [(source, (source + steps) % count) for source...  1.92 us
    ppermute x1, waiting for transfers between devices, shifted(): lax.ppermute(value, axis, [(source, (source + steps) % count) for source...  0.97 us
  transfers between devices with their start and end apart: 7, of which 3 were waited for; matrix products, arithmetic and copies ran while one was open for 0% of the time, Pallas kernels for 6%

profile of v6, /device:TPU:2, one launch (start us, length us, event | category | flops | bytes accessed | tf_op | source)
XLA Modules:
  0.0 46.8 jit_solution(5345010057126908528)
XLA Ops:
  0.6 0.0 copy-start
  0.6 1.1 %shard_map.41.vectors_ref = bf16[24,1728]{1,0:T(8,128)(2,1)S(1)} custom-call(f32[3,8,1728]{2,1,0:T(8,128)} %bitcast.10), custom_call_target="tpu_custom_call" | custom-call | flops 1857945600 | bytes 1048576 | tf_op jit(solution)/shard_map/pallas_call | solution.py:253
  1.7 1.3 %collective-permute-start.2 = (bf16[24,1728]{1,0:T(8,128)(2,1)S(1)}, bf16[24,1728]{1,0:T(8,128)(2,1)S(1)}, u32[]{:S(2)}, u32[]{:S(2)}) collective-permute-start(bf16[24,1728]{1,0:T(8,128)(2,1)S(1)} %shard_map.41.vectors_ref), channel_id=1, source_target_pairs={{8,16},{24,32},{40,48},{56,64},{72,80},{88,96},{104,112},{120,128}... | collective-permute-start | bytes 248840 | tf_op jit(solution)/shard_map/ppermute | solution.py:29
  3.0 0.0 copy-done
  3.0 0.7 %shard_map.42 = (f32[24,224]{1,0:T(8,128)S(1)}, bf16[24,2528]{1,0:T(8,128)(2,1)S(1)}) custom-call(bf16[24,1728]{1,0:T(8,128)(2,1)S(1)} %shard_map.41.vectors_ref, bf16[3,224,1728]{2,1,0:T(8,128)(2,1)S(1)} %bitcast.2), custom_call_target="tpu_custom_call" | custom-call | flops 7431782400 | bytes 1048576 | tf_op jit(solution)/shard_map/pallas_call | solution.py:253
  3.8 1.3 %collective-permute-start.1 = (f32[24,224]{1,0:T(8,128)S(1)}, f32[24,224]{1,0:T(8,128)S(1)}, u32[]{:S(2)}, u32[]{:S(2)}) collective-permute-start(f32[24,224]{1,0:T(8,128)S(1)} %get-tuple-element.18), channel_id=1, source_target_pairs={{8,16},{24,32},{40,48},{56,64},{72,80},{88,96},{104,112},{120,128}... | collective-permute-start | bytes 64520 | tf_op jit(solution)/shard_map/ppermute | solution.py:29
  5.1 4.2 %collective-permute-start = (bf16[24,2528]{1,0:T(8,128)(2,1)S(1)}, bf16[24,2528]{1,0:T(8,128)(2,1)S(1)}, u32[]{:S(2)}, u32[]{:S(2)}) collective-permute-start(bf16[24,2528]{1,0:T(8,128)(2,1)S(1)} %get-tuple-element.17), channel_id=1, source_target_pairs={{0,8},{16,24},{32,40},{48,56},{64,72},{80,88},{96,104},{112,120},{... | collective-permute-start | bytes 364040 | tf_op jit(solution)/shard_map/ppermute | solution.py:29
  9.3 8.1 %collective-permute-done.2.vectors_ref = bf16[24,1728]{1,0:T(8,128)(2,1)S(1)} collective-permute-done((bf16[24,1728]{1,0:T(8,128)(2,1)S(1)}, bf16[24,1728]{1,0:T(8,128)(2,1)S(1)}, u32[]{:S(2)}, u32[]{:S(2)}) %collective-permute-start.2) | collective-permute-done | bytes 82976 | tf_op jit(solution)/shard_map/ppermute | solution.py:29
  17.5 0.7 %shard_map.43.odd_images_ref = f32[24,224]{1,0:T(8,128)S(1)} custom-call(bf16[24,1728]{1,0:T(8,128)(2,1)S(1)} %collective-permute-done.2.vectors_ref, bf16[3,224,1728]{2,1,0:T(8,128)(2,1)S(1)} %bitcast.3), custom_call_target="tpu_custom_call" | custom-call | flops 7431782400 | bytes 1048576 | tf_op jit(solution)/shard_map/pallas_call | solution.py:253
  18.2 0.0 collective-permute-done.1.odd_left_ref
  18.2 0.0 collective-permute-done.even_message_ref
  18.3 10.8 %all_to_all.5.parts_ref = f32[8,24,224]{2,1,0:T(8,128)S(1)} all-to-all(f32[8,24,224]{2,1,0:T(8,128)S(1)} %broadcast_in_dim.2), channel_id=1, replica_groups=mesh['replica'=64,'tensor'=8] {'tensor'}, dimensions={0} | all-to-all | bytes 344064 | tf_op jit(solution)/shard_map/all_to_all | solution.py:302
  29.1 0.8 %shard_map.45 = (f32[24,224]{1,0:T(8,128)S(1)}, bf16[24,480]{1,0:T(8,128)(2,1)S(1)}, f32[24,1728]{1,0:T(8,128)S(1)}, bf16[24,2272]{1,0:T(8,128)(2,1)S(1)}) custom-call(f32[8,24,224]{2,1,0:T(8,128)S(1)} %all_to_all.5.parts_ref, bf16[3,224,1728]{2,1,0:T(8,128)(2,1)S(1)} %bitcast.5), custom_call_target="tpu_custom_call" | custom-call | flops 18579456 | bytes 1048576 | tf_op jit(solution)/shard_map/pallas_call | solution.py:253
  29.8 2.3 %collective-permute-start.4 = (bf16[24,480]{1,0:T(8,128)(2,1)S(1)}, bf16[24,480]{1,0:T(8,128)(2,1)S(1)}, u32[]{:S(2)}, u32[]{:S(2)}) collective-permute-start(bf16[24,480]{1,0:T(8,128)(2,1)S(1)} %get-tuple-element.19.basis_ref), channel_id=1, source_target_pairs={{0,504},{16,8},{32,24},{48,40},{64,56},{80,72},{96,88},{112,104},{... | collective-permute-start | bytes 69128 | tf_op jit(solution)/shard_map/ppermute | solution.py:29
  32.2 1.9 %collective-permute-start.3 = (bf16[24,2272]{1,0:T(8,128)(2,1)S(1)}, bf16[24,2272]{1,0:T(8,128)(2,1)S(1)}, u32[]{:S(2)}, u32[]{:S(2)}) collective-permute-start(bf16[24,2272]{1,0:T(8,128)(2,1)S(1)} %get-tuple-element.22), channel_id=1, source_target_pairs={{0,504},{8,0},{16,8},{24,16},{32,24},{40,32},{48,40},{56,48},{64,5... | collective-permute-start | bytes 327176 | tf_op jit(solution)/shard_map/ppermute | solution.py:17
  34.1 0.0 collective-permute-done.4.message_ref
  34.2 1.3 %collective-permute-start.5 = (bf16[24,1728]{1,0:T(8,128)(2,1)S(1)}, bf16[24,1728]{1,0:T(8,128)(2,1)S(1)}, u32[]{:S(2)}, u32[]{:S(2)}) collective-permute-start(bf16[24,1728]{1,0:T(8,128)(2,1)S(1)} %get-tuple-element.29), channel_id=1, source_target_pairs={{8,16},{24,32},{40,48},{56,64},{72,80},{88,96},{104,112},{120,128}... | collective-permute-start | bytes 248840 | tf_op jit(solution)/shard_map/ppermute | solution.py:29
  35.5 1.0 %collective-permute-done.3.message_ref = bf16[24,2272]{1,0:T(8,128)(2,1)S(1)} collective-permute-done((bf16[24,2272]{1,0:T(8,128)(2,1)S(1)}, bf16[24,2272]{1,0:T(8,128)(2,1)S(1)}, u32[]{:S(2)}, u32[]{:S(2)}) %collective-permute-start.3) | collective-permute-done | bytes 109088 | tf_op jit(solution)/shard_map/ppermute | solution.py:17
  36.5 0.4 shard_map.48
  36.9 1.5 %collective-permute-start.6 = (bf16[24,1728]{1,0:T(8,128)(2,1)S(1)}, bf16[24,1728]{1,0:T(8,128)(2,1)S(1)}, u32[]{:S(2)}, u32[]{:S(2)}) collective-permute-start(bf16[24,1728]{1,0:T(8,128)(2,1)S(1)} %get-tuple-element.30), channel_id=1, source_target_pairs={{0,8},{16,24},{32,40},{48,56},{64,72},{80,88},{96,104},{112,120},{... | collective-permute-start | bytes 248840 | tf_op jit(solution)/shard_map/ppermute | solution.py:29
  38.4 0.8 %shard_map.49 = (bf16[3,224,64]{2,1,0:T(8,128)(2,1)S(1)}, bf16[3,48,1728]{2,1,0:T(8,128)(2,1)S(1)}, f32[3,1,8,1728]{3,2,1,0:T(8,128)}) custom-call(bf16[24,2272]{1,0:T(8,128)(2,1)S(1)} %collective-permute-done.3.message_ref, f32[24,1728]{1,0:T(8,128)S(1)} %get-tuple-element.23.odd_products_ref, f32[24,1728]{1,0:T(8,128)S(1)} %get-tuple-element.24.even_products_ref, ...), custom_call_target="tpu_custom_call" | custom-call | flops 4644864 | bytes 1048576 | tf_op jit(solution)/shard_map/pallas_call | solution.py:253
  39.2 5.9 %collective-permute-done.5.odd_ref = bf16[24,1728]{1,0:T(8,128)(2,1)S(1)} collective-permute-done((bf16[24,1728]{1,0:T(8,128)(2,1)S(1)}, bf16[24,1728]{1,0:T(8,128)(2,1)S(1)}, u32[]{:S(2)}, u32[]{:S(2)}) %collective-permute-start.5) | collective-permute-done | bytes 82976 | tf_op jit(solution)/shard_map/ppermute | solution.py:29
  45.0 0.0 collective-permute-done.6.even_ref
  45.0 1.8 %shard_map.50 = bf16[3,1,224,1728]{3,2,1,0:T(8,128)(2,1)} custom-call(bf16[3,224,64]{2,1,0:T(8,128)(2,1)S(1)} %get-tuple-element.27.left_ref, bf16[3,48,1728]{2,1,0:T(8,128)(2,1)S(1)} %get-tuple-element.28.right_ref, bf16[24,1728]{1,0:T(8,128)(2,1)S(1)} %collective-permute-done.5.odd_ref, bf16[24,1728]{1,0:T(8,128)(2,1)S(1)} %collective-permute-done.6.even_ref, ...), custom_call_target="tpu_custom_call" | custom-call | flops 74317824 | bytes 1048576 | tf_op jit(solution)/shard_map/pallas_call | solution.py:253
  (4 shorter events, 0.1 us)
Async XLA Ops:
  0.6 2.4 %copy-start = (bf16[3,1,224,1728]{3,2,1,0:T(8,128)(2,1)S(1)}, bf16[3,1,224,1728]{3,2,1,0:T(8,128)(2,1)}, u32[]{:S(2)}) copy-start(bf16[3,1,224,1728]{3,2,1,0:T(8,128)(2,1)} %param.2) | copy-start | bytes 6967300
  1.7 15.7 %collective-permute-start.2 = (bf16[24,1728]{1,0:T(8,128)(2,1)S(1)}, bf16[24,1728]{1,0:T(8,128)(2,1)S(1)}, u32[]{:S(2)}, u32[]{:S(2)}) collective-permute-start(bf16[24,1728]{1,0:T(8,128)(2,1)S(1)} %shard_map.41.vectors_ref), channel_id=1, source_target_pairs={{8,16},{24,32},{40,48},{56,64},{72,80},{88,96},{104,112},{120,128}... | collective-permute-start | bytes 248840 | tf_op jit(solution)/shard_map/ppermute | solution.py:29
  3.8 14.4 %collective-permute-start.1 = (f32[24,224]{1,0:T(8,128)S(1)}, f32[24,224]{1,0:T(8,128)S(1)}, u32[]{:S(2)}, u32[]{:S(2)}) collective-permute-start(f32[24,224]{1,0:T(8,128)S(1)} %get-tuple-element.18), channel_id=1, source_target_pairs={{8,16},{24,32},{40,48},{56,64},{72,80},{88,96},{104,112},{120,128}... | collective-permute-start | bytes 64520 | tf_op jit(solution)/shard_map/ppermute | solution.py:29
  5.1 13.1 %collective-permute-start = (bf16[24,2528]{1,0:T(8,128)(2,1)S(1)}, bf16[24,2528]{1,0:T(8,128)(2,1)S(1)}, u32[]{:S(2)}, u32[]{:S(2)}) collective-permute-start(bf16[24,2528]{1,0:T(8,128)(2,1)S(1)} %get-tuple-element.17), channel_id=1, source_target_pairs={{0,8},{16,24},{32,40},{48,56},{64,72},{80,88},{96,104},{112,120},{... | collective-permute-start | bytes 364040 | tf_op jit(solution)/shard_map/ppermute | solution.py:29
  29.8 4.3 %collective-permute-start.4 = (bf16[24,480]{1,0:T(8,128)(2,1)S(1)}, bf16[24,480]{1,0:T(8,128)(2,1)S(1)}, u32[]{:S(2)}, u32[]{:S(2)}) collective-permute-start(bf16[24,480]{1,0:T(8,128)(2,1)S(1)} %get-tuple-element.19.basis_ref), channel_id=1, source_target_pairs={{0,504},{16,8},{32,24},{48,40},{64,56},{80,72},{96,88},{112,104},{... | collective-permute-start | bytes 69128 | tf_op jit(solution)/shard_map/ppermute | solution.py:29
  32.2 4.2 %collective-permute-start.3 = (bf16[24,2272]{1,0:T(8,128)(2,1)S(1)}, bf16[24,2272]{1,0:T(8,128)(2,1)S(1)}, u32[]{:S(2)}, u32[]{:S(2)}) collective-permute-start(bf16[24,2272]{1,0:T(8,128)(2,1)S(1)} %get-tuple-element.22), channel_id=1, source_target_pairs={{0,504},{8,0},{16,8},{24,16},{32,24},{40,32},{48,40},{56,48},{64,5... | collective-permute-start | bytes 327176 | tf_op jit(solution)/shard_map/ppermute | solution.py:17
  34.2 10.9 %collective-permute-start.5 = (bf16[24,1728]{1,0:T(8,128)(2,1)S(1)}, bf16[24,1728]{1,0:T(8,128)(2,1)S(1)}, u32[]{:S(2)}, u32[]{:S(2)}) collective-permute-start(bf16[24,1728]{1,0:T(8,128)(2,1)S(1)} %get-tuple-element.29), channel_id=1, source_target_pairs={{8,16},{24,32},{40,48},{56,64},{72,80},{88,96},{104,112},{120,128}... | collective-permute-start | bytes 248840 | tf_op jit(solution)/shard_map/ppermute | solution.py:29
  36.9 8.2 %collective-permute-start.6 = (bf16[24,1728]{1,0:T(8,128)(2,1)S(1)}, bf16[24,1728]{1,0:T(8,128)(2,1)S(1)}, u32[]{:S(2)}, u32[]{:S(2)}) collective-permute-start(bf16[24,1728]{1,0:T(8,128)(2,1)S(1)} %get-tuple-element.30), channel_id=1, source_target_pairs={{0,8},{16,24},{32,40},{48,56},{64,72},{80,88},{96,104},{112,120},{... | collective-permute-start | bytes 248840 | tf_op jit(solution)/shard_map/ppermute | solution.py:29

commit v7 on v6

--- a/solution.py
+++ b/solution.py
@@ -155,7 +155,7 @@
     message_ref[:, padded(columns) :] = basis_ref[...]
 
 
-def basis_kernel(parts_ref, window_ref, basis_ref, parts_out_ref, products_ref, message_ref):
+def basis_and_products(parts_ref, window_ref, basis_ref, split_ref, products_ref, message_ref):
     rank = parts_ref.shape[1] // window_ref.shape[0]
     row_count = parts_ref.shape[2]
     images = jnp.sum(parts_ref[...], 0)
@@ -165,19 +165,22 @@
     basis = orthonormal_rows(gram, images, rank)
     basis_ref[...] = basis
     high, low = split(basis)
-    parts_out_ref[:, :row_count] = high.astype(jnp.bfloat16)
+    split_ref[:, :row_count] = high.astype(jnp.bfloat16)
     start = padded(row_count)
-    parts_out_ref[:, start : start + row_count] = low.astype(jnp.bfloat16)
-
+    split_ref[:, start : start + row_count] = low.astype(jnp.bfloat16)
+    lower_products(split_ref, window_ref, products_ref, message_ref)
+
+
+def even_basis_kernel(parts_ref, window_ref, basis_ref, split_ref, products_ref, message_ref):
     @pl.when(jnp.logical_not(odd_replica()))
     def _():
-        lower_products(parts_out_ref, window_ref, products_ref, message_ref)
-
-
-def odd_products_kernel(basis_ref, window_ref, _, __, products_ref, message_ref):
+        basis_and_products(parts_ref, window_ref, basis_ref, split_ref, products_ref, message_ref)
+
+
+def odd_basis_kernel(parts_ref, window_ref, _, __, ___, basis_ref, products_ref, message_ref, split_ref):
     @pl.when(odd_replica())
     def _():
-        lower_products(basis_ref, window_ref, products_ref, message_ref)
+        basis_and_products(parts_ref, window_ref, basis_ref, split_ref, products_ref, message_ref)
 
 
 def upper_products_kernel(odd, start, message_ref, window_ref, products_ref, rounded_ref):
@@ -303,17 +306,20 @@
         jnp.broadcast_to(differences[None], (group, stacked, row_count)), "tensor", 0, 0
     )
     message_out = whole(bf16, stacked, base + padded(row_count) + row_count)
+    split_basis = whole(bf16, stacked, padded(row_count) + row_count)
     lower_basis, basis, lower_products, message = call(
-        basis_kernel,
-        (images, whole(bf16, stacked, padded(row_count) + row_count), products, message_out),
-        flops,
+        even_basis_kernel, (images, split_basis, products, message_out), flops
     )(parts, window)
     products_outs = (products, rounded_products)
 
     odd_basis = odd_down(basis)
-    lower_products, message = call(
-        odd_products_kernel, (products, message_out), 400 * flops, input_output_aliases={2: 0, 3: 1}
-    )(basis, window, lower_products, message)
+    lower_basis, lower_products, message = call(
+        odd_basis_kernel,
+        (images, products, message_out),
+        400 * flops,
+        input_output_aliases={2: 0, 3: 1, 4: 2},
+        scratch_shapes=[pltpu.VMEM(split_basis.shape, bf16)],
+    )(parts, window, lower_basis, lower_products, message)
     message = shifted(message, "replica", -1)
     odd_upper, rounded_upper = call(functools.partial(upper_products_kernel, True, 0), products_outs, 400 * flops)(
         odd_basis, window

time: 47.1 us -> 46.9 us (level)
    ppermute x6, starting transfers between devices: 11.9 us -> 11.4 us  [over(): return lambda value: lax.ppermute(value, axis, pairs)]
where the time goes in v7:
time: 46.9 us; the launch traced here: 46.6 us
  waiting for transfers between devices  15.1 us (32%)
  starting transfers between devices  13.4 us (29%)
  blocking collectives  10.8 us (23%)
  Pallas kernels  6.45 us (14%)
  between operations  0.76 us (2%)
    ppermute x6, waiting for transfers between devices, over(): return lambda value: lax.ppermute(value, axis, pairs)  14.2 us
    ppermute x6, starting transfers between devices, over(): return lambda value: lax.ppermute(value, axis, pairs)  11.4 us
    all_to_all x1, blocking collectives, shards(): lax.all_to_all(jnp.broadcast_to(differences[None], (group, stacked, row_c...  10.8 us
    pallas_call x10, Pallas kernels, run(): pl.pallas_call(kernel, out_shape=outs, in_specs=[IN_VMEM] * len(operands)...  6.45 us
    ppermute x1, starting transfers between devices, shifted(): lax.ppermute(value, axis, [(source, (source + steps) % count) for source...  2.07 us
    ppermute x1, waiting for transfers between devices, shifted(): lax.ppermute(value, axis, [(source, (source + steps) % count) for source...  0.97 us
  transfers between devices with their start and end apart: 7, of which 3 were waited for; matrix products, arithmetic and copies ran while one was open for 0% of the time, Pallas kernels for 6%

profile of v7, /device:TPU:2, one launch (start us, length us, event | category | flops | bytes accessed | tf_op | source)
XLA Modules:
  0.0 46.6 jit_solution(4182852138814590611)
XLA Ops:
  0.6 0.0 copy-start
  0.6 1.1 %shard_map.41.vectors_ref = bf16[24,1728]{1,0:T(8,128)(2,1)S(1)} custom-call(f32[3,8,1728]{2,1,0:T(8,128)} %bitcast.10), custom_call_target="tpu_custom_call" | custom-call | flops 1857945600 | bytes 1048576 | tf_op jit(solution)/shard_map/pallas_call | solution.py:256
  1.7 1.3 %collective-permute-start.2 = (bf16[24,1728]{1,0:T(8,128)(2,1)S(1)}, bf16[24,1728]{1,0:T(8,128)(2,1)S(1)}, u32[]{:S(2)}, u32[]{:S(2)}) collective-permute-start(bf16[24,1728]{1,0:T(8,128)(2,1)S(1)} %shard_map.41.vectors_ref), channel_id=1, source_target_pairs={{8,16},{24,32},{40,48},{56,64},{72,80},{88,96},{104,112},{120,128}... | collective-permute-start | bytes 248840 | tf_op jit(solution)/shard_map/ppermute | solution.py:29
  3.0 0.0 copy-done
  3.0 0.7 %shard_map.42 = (f32[24,224]{1,0:T(8,128)S(1)}, bf16[24,2528]{1,0:T(8,128)(2,1)S(1)}) custom-call(bf16[24,1728]{1,0:T(8,128)(2,1)S(1)} %shard_map.41.vectors_ref, bf16[3,224,1728]{2,1,0:T(8,128)(2,1)S(1)} %bitcast.2), custom_call_target="tpu_custom_call" | custom-call | flops 7431782400 | bytes 1048576 | tf_op jit(solution)/shard_map/pallas_call | solution.py:256
  3.8 1.3 %collective-permute-start.1 = (f32[24,224]{1,0:T(8,128)S(1)}, f32[24,224]{1,0:T(8,128)S(1)}, u32[]{:S(2)}, u32[]{:S(2)}) collective-permute-start(f32[24,224]{1,0:T(8,128)S(1)} %get-tuple-element.19), channel_id=1, source_target_pairs={{8,16},{24,32},{40,48},{56,64},{72,80},{88,96},{104,112},{120,128}... | collective-permute-start | bytes 64520 | tf_op jit(solution)/shard_map/ppermute | solution.py:29
  5.1 4.2 %collective-permute-start = (bf16[24,2528]{1,0:T(8,128)(2,1)S(1)}, bf16[24,2528]{1,0:T(8,128)(2,1)S(1)}, u32[]{:S(2)}, u32[]{:S(2)}) collective-permute-start(bf16[24,2528]{1,0:T(8,128)(2,1)S(1)} %get-tuple-element.18), channel_id=1, source_target_pairs={{0,8},{16,24},{32,40},{48,56},{64,72},{80,88},{96,104},{112,120},{... | collective-permute-start | bytes 364040 | tf_op jit(solution)/shard_map/ppermute | solution.py:29
  9.3 8.1 %collective-permute-done.2.vectors_ref = bf16[24,1728]{1,0:T(8,128)(2,1)S(1)} collective-permute-done((bf16[24,1728]{1,0:T(8,128)(2,1)S(1)}, bf16[24,1728]{1,0:T(8,128)(2,1)S(1)}, u32[]{:S(2)}, u32[]{:S(2)}) %collective-permute-start.2) | collective-permute-done | bytes 82976 | tf_op jit(solution)/shard_map/ppermute | solution.py:29
  17.5 0.7 %shard_map.43.odd_images_ref = f32[24,224]{1,0:T(8,128)S(1)} custom-call(bf16[24,1728]{1,0:T(8,128)(2,1)S(1)} %collective-permute-done.2.vectors_ref, bf16[3,224,1728]{2,1,0:T(8,128)(2,1)S(1)} %bitcast.3), custom_call_target="tpu_custom_call" | custom-call | flops 7431782400 | bytes 1048576 | tf_op jit(solution)/shard_map/pallas_call | solution.py:256
  18.2 0.0 collective-permute-done.1.odd_left_ref
  18.2 0.0 collective-permute-done.even_message_ref
  18.3 10.8 %all_to_all.5.parts_ref = f32[8,24,224]{2,1,0:T(8,128)S(1)} all-to-all(f32[8,24,224]{2,1,0:T(8,128)S(1)} %broadcast_in_dim.2), channel_id=1, replica_groups=mesh['replica'=64,'tensor'=8] {'tensor'}, dimensions={0} | all-to-all | bytes 344064 | tf_op jit(solution)/shard_map/all_to_all | solution.py:305
  29.1 0.8 %shard_map.45 = (f32[24,224]{1,0:T(8,128)S(1)}, bf16[24,480]{1,0:T(8,128)(2,1)S(1)}, f32[24,1728]{1,0:T(8,128)S(1)}, bf16[24,2272]{1,0:T(8,128)(2,1)S(1)}) custom-call(f32[8,24,224]{2,1,0:T(8,128)S(1)} %all_to_all.5.parts_ref, bf16[3,224,1728]{2,1,0:T(8,128)(2,1)S(1)} %bitcast.5), custom_call_target="tpu_custom_call" | custom-call | flops 18579456 | bytes 1048576 | tf_op jit(solution)/shard_map/pallas_call | solution.py:256
  29.8 1.9 %collective-permute-start.4 = (bf16[24,480]{1,0:T(8,128)(2,1)S(1)}, bf16[24,480]{1,0:T(8,128)(2,1)S(1)}, u32[]{:S(2)}, u32[]{:S(2)}) collective-permute-start(bf16[24,480]{1,0:T(8,128)(2,1)S(1)} %get-tuple-element.24), channel_id=1, source_target_pairs={{0,504},{16,8},{32,24},{48,40},{64,56},{80,72},{96,88},{112,104},{... | collective-permute-start | bytes 69128 | tf_op jit(solution)/shard_map/ppermute | solution.py:29
  31.8 2.1 %collective-permute-start.3 = (bf16[24,2272]{1,0:T(8,128)(2,1)S(1)}, bf16[24,2272]{1,0:T(8,128)(2,1)S(1)}, u32[]{:S(2)}, u32[]{:S(2)}) collective-permute-start(bf16[24,2272]{1,0:T(8,128)(2,1)S(1)} %get-tuple-element.23), channel_id=1, source_target_pairs={{0,504},{8,0},{16,8},{24,16},{32,24},{40,32},{48,40},{56,48},{64,5... | collective-permute-start | bytes 327176 | tf_op jit(solution)/shard_map/ppermute | solution.py:17
  33.9 0.0 collective-permute-done.4.message_ref
  33.9 1.3 %collective-permute-start.5 = (bf16[24,1728]{1,0:T(8,128)(2,1)S(1)}, bf16[24,1728]{1,0:T(8,128)(2,1)S(1)}, u32[]{:S(2)}, u32[]{:S(2)}) collective-permute-start(bf16[24,1728]{1,0:T(8,128)(2,1)S(1)} %get-tuple-element.31), channel_id=1, source_target_pairs={{8,16},{24,32},{40,48},{56,64},{72,80},{88,96},{104,112},{120,128}... | collective-permute-start | bytes 248840 | tf_op jit(solution)/shard_map/ppermute | solution.py:29
  35.2 1.0 %collective-permute-done.3.message_ref = bf16[24,2272]{1,0:T(8,128)(2,1)S(1)} collective-permute-done((bf16[24,2272]{1,0:T(8,128)(2,1)S(1)}, bf16[24,2272]{1,0:T(8,128)(2,1)S(1)}, u32[]{:S(2)}, u32[]{:S(2)}) %collective-permute-start.3) | collective-permute-done | bytes 109088 | tf_op jit(solution)/shard_map/ppermute | solution.py:17
  36.2 0.4 shard_map.48
  36.6 1.3 %collective-permute-start.6 = (bf16[24,1728]{1,0:T(8,128)(2,1)S(1)}, bf16[24,1728]{1,0:T(8,128)(2,1)S(1)}, u32[]{:S(2)}, u32[]{:S(2)}) collective-permute-start(bf16[24,1728]{1,0:T(8,128)(2,1)S(1)} %get-tuple-element.32), channel_id=1, source_target_pairs={{0,8},{16,24},{32,40},{48,56},{64,72},{80,88},{96,104},{112,120},{... | collective-permute-start | bytes 248840 | tf_op jit(solution)/shard_map/ppermute | solution.py:29
  38.0 0.8 %shard_map.49 = (bf16[3,224,64]{2,1,0:T(8,128)(2,1)S(1)}, bf16[3,48,1728]{2,1,0:T(8,128)(2,1)S(1)}, f32[3,1,8,1728]{3,2,1,0:T(8,128)}) custom-call(bf16[24,2272]{1,0:T(8,128)(2,1)S(1)} %collective-permute-done.3.message_ref, f32[24,1728]{1,0:T(8,128)S(1)} %get-tuple-element.25.odd_products_ref, f32[24,1728]{1,0:T(8,128)S(1)} %get-tuple-element.26.even_products_ref, ...), custom_call_target="tpu_custom_call" | custom-call | flops 4644864 | bytes 1048576 | tf_op jit(solution)/shard_map/pallas_call | solution.py:256
  38.8 6.0 %collective-permute-done.5.odd_ref = bf16[24,1728]{1,0:T(8,128)(2,1)S(1)} collective-permute-done((bf16[24,1728]{1,0:T(8,128)(2,1)S(1)}, bf16[24,1728]{1,0:T(8,128)(2,1)S(1)}, u32[]{:S(2)}, u32[]{:S(2)}) %collective-permute-start.5) | collective-permute-done | bytes 82976 | tf_op jit(solution)/shard_map/ppermute | solution.py:29
  44.8 0.0 collective-permute-done.6.even_ref
  44.8 1.8 %shard_map.50 = bf16[3,1,224,1728]{3,2,1,0:T(8,128)(2,1)} custom-call(bf16[3,224,64]{2,1,0:T(8,128)(2,1)S(1)} %get-tuple-element.29.left_ref, bf16[3,48,1728]{2,1,0:T(8,128)(2,1)S(1)} %get-tuple-element.30.right_ref, bf16[24,1728]{1,0:T(8,128)(2,1)S(1)} %collective-permute-done.5.odd_ref, bf16[24,1728]{1,0:T(8,128)(2,1)S(1)} %collective-permute-done.6.even_ref, ...), custom_call_target="tpu_custom_call" | custom-call | flops 74317824 | bytes 1048576 | tf_op jit(solution)/shard_map/pallas_call | solution.py:256
  (4 shorter events, 0.1 us)
Async XLA Ops:
  0.6 2.4 %copy-start = (bf16[3,1,224,1728]{3,2,1,0:T(8,128)(2,1)S(1)}, bf16[3,1,224,1728]{3,2,1,0:T(8,128)(2,1)}, u32[]{:S(2)}) copy-start(bf16[3,1,224,1728]{3,2,1,0:T(8,128)(2,1)} %param.2) | copy-start | bytes 6967300
  1.7 15.7 %collective-permute-start.2 = (bf16[24,1728]{1,0:T(8,128)(2,1)S(1)}, bf16[24,1728]{1,0:T(8,128)(2,1)S(1)}, u32[]{:S(2)}, u32[]{:S(2)}) collective-permute-start(bf16[24,1728]{1,0:T(8,128)(2,1)S(1)} %shard_map.41.vectors_ref), channel_id=1, source_target_pairs={{8,16},{24,32},{40,48},{56,64},{72,80},{88,96},{104,112},{120,128}... | collective-permute-start | bytes 248840 | tf_op jit(solution)/shard_map/ppermute | solution.py:29
  3.8 14.4 %collective-permute-start.1 = (f32[24,224]{1,0:T(8,128)S(1)}, f32[24,224]{1,0:T(8,128)S(1)}, u32[]{:S(2)}, u32[]{:S(2)}) collective-permute-start(f32[24,224]{1,0:T(8,128)S(1)} %get-tuple-element.19), channel_id=1, source_target_pairs={{8,16},{24,32},{40,48},{56,64},{72,80},{88,96},{104,112},{120,128}... | collective-permute-start | bytes 64520 | tf_op jit(solution)/shard_map/ppermute | solution.py:29
  5.1 13.1 %collective-permute-start = (bf16[24,2528]{1,0:T(8,128)(2,1)S(1)}, bf16[24,2528]{1,0:T(8,128)(2,1)S(1)}, u32[]{:S(2)}, u32[]{:S(2)}) collective-permute-start(bf16[24,2528]{1,0:T(8,128)(2,1)S(1)} %get-tuple-element.18), channel_id=1, source_target_pairs={{0,8},{16,24},{32,40},{48,56},{64,72},{80,88},{96,104},{112,120},{... | collective-permute-start | bytes 364040 | tf_op jit(solution)/shard_map/ppermute | solution.py:29
  29.8 4.1 %collective-permute-start.4 = (bf16[24,480]{1,0:T(8,128)(2,1)S(1)}, bf16[24,480]{1,0:T(8,128)(2,1)S(1)}, u32[]{:S(2)}, u32[]{:S(2)}) collective-permute-start(bf16[24,480]{1,0:T(8,128)(2,1)S(1)} %get-tuple-element.24), channel_id=1, source_target_pairs={{0,504},{16,8},{32,24},{48,40},{64,56},{80,72},{96,88},{112,104},{... | collective-permute-start | bytes 69128 | tf_op jit(solution)/shard_map/ppermute | solution.py:29
  31.8 4.4 %collective-permute-start.3 = (bf16[24,2272]{1,0:T(8,128)(2,1)S(1)}, bf16[24,2272]{1,0:T(8,128)(2,1)S(1)}, u32[]{:S(2)}, u32[]{:S(2)}) collective-permute-start(bf16[24,2272]{1,0:T(8,128)(2,1)S(1)} %get-tuple-element.23), channel_id=1, source_target_pairs={{0,504},{8,0},{16,8},{24,16},{32,24},{40,32},{48,40},{56,48},{64,5... | collective-permute-start | bytes 327176 | tf_op jit(solution)/shard_map/ppermute | solution.py:17
  33.9 10.9 %collective-permute-start.5 = (bf16[24,1728]{1,0:T(8,128)(2,1)S(1)}, bf16[24,1728]{1,0:T(8,128)(2,1)S(1)}, u32[]{:S(2)}, u32[]{:S(2)}) collective-permute-start(bf16[24,1728]{1,0:T(8,128)(2,1)S(1)} %get-tuple-element.31), channel_id=1, source_target_pairs={{8,16},{24,32},{40,48},{56,64},{72,80},{88,96},{104,112},{120,128}... | collective-permute-start | bytes 248840 | tf_op jit(solution)/shard_map/ppermute | solution.py:29
  36.6 8.2 %collective-permute-start.6 = (bf16[24,1728]{1,0:T(8,128)(2,1)S(1)}, bf16[24,1728]{1,0:T(8,128)(2,1)S(1)}, u32[]{:S(2)}, u32[]{:S(2)}) collective-permute-start(bf16[24,1728]{1,0:T(8,128)(2,1)S(1)} %get-tuple-element.32), channel_id=1, source_target_pairs={{0,8},{16,24},{32,40},{48,56},{64,72},{80,88},{96,104},{112,120},{... | collective-permute-start | bytes 248840 | tf_op jit(solution)/shard_map/ppermute | solution.py:29

commit v8 on v7

--- a/solution.py
+++ b/solution.py
@@ -245,8 +245,14 @@
             held_ref[mat, :, start:stop] = (window_ref[mat, :, start:stop].astype(jnp.float32) + change).astype(
                 jnp.bfloat16
             )
-        copies.append(pltpu.make_async_copy(held_ref.at[mat], updated_ref.at[mat, 0], sems.at[mat]))
-        copies[-1].start()
+            if stop % (2 * width) == 0 or stop == columns:
+                piece = slice(start // (2 * width) * (2 * width), stop)
+                copies.append(
+                    pltpu.make_async_copy(
+                        held_ref.at[mat, :, piece], updated_ref.at[mat, 0, :, piece], sems.at[len(copies)]
+                    )
+                )
+                copies[-1].start()
     for copy in copies:
         copy.wait()
 
@@ -345,7 +351,7 @@
         whole(bf16, mats, 1, row_count, columns),
         4 * flops,
         out_specs=pl.BlockSpec(memory_space=pl.ANY),
-        scratch_shapes=[pltpu.VMEM((mats, row_count, columns), bf16), pltpu.SemaphoreType.DMA((mats,))],
+        scratch_shapes=[pltpu.VMEM((mats, row_count, columns), bf16), pltpu.SemaphoreType.DMA((mats * (-(-columns // (4 * LANES))),))],
     )(left, right, odd_previous, even_previous, window)
     return (updated, factors)
 

time: 46.9 us -> 46.8 us (level)
  no operation moved by 1% of the time
where the time goes in v8:
time: 46.8 us; the launch traced here: 46.5 us
  waiting for transfers between devices  15.1 us (32%)
  starting transfers between devices  13.4 us (29%)
  blocking collectives  10.8 us (23%)
  Pallas kernels  6.39 us (14%)
  between operations  0.76 us (2%)
    ppermute x6, waiting for transfers between devices, over(): return lambda value: lax.ppermute(value, axis, pairs)  14.2 us
    ppermute x6, starting transfers between devices, over(): return lambda value: lax.ppermute(value, axis, pairs)  11.4 us
    all_to_all x1, blocking collectives, shards(): lax.all_to_all(jnp.broadcast_to(differences[None], (group, stacked, row_c...  10.8 us
    pallas_call x10, Pallas kernels, run(): pl.pallas_call(kernel, out_shape=outs, in_specs=[IN_VMEM] * len(operands)...  6.39 us
    ppermute x1, starting transfers between devices, shifted(): lax.ppermute(value, axis, [(source, (source + steps) % count) for source...  2.07 us
    ppermute x1, waiting for transfers between devices, shifted(): lax.ppermute(value, axis, [(source, (source + steps) % count) for source...  0.97 us
  transfers between devices with their start and end apart: 7, of which 3 were waited for; matrix products, arithmetic and copies ran while one was open for 0% of the time, Pallas kernels for 6%

profile of v8, /device:TPU:2, one launch (start us, length us, event | category | flops | bytes accessed | tf_op | source)
XLA Modules:
  0.0 46.5 jit_solution(16766998141801554010)
XLA Ops:
  0.6 0.0 copy-start
  0.6 1.1 %shard_map.41.vectors_ref = bf16[24,1728]{1,0:T(8,128)(2,1)S(1)} custom-call(f32[3,8,1728]{2,1,0:T(8,128)} %bitcast.10), custom_call_target="tpu_custom_call" | custom-call | flops 1857945600 | bytes 1048576 | tf_op jit(solution)/shard_map/pallas_call | solution.py:262
  1.7 1.3 %collective-permute-start.2 = (bf16[24,1728]{1,0:T(8,128)(2,1)S(1)}, bf16[24,1728]{1,0:T(8,128)(2,1)S(1)}, u32[]{:S(2)}, u32[]{:S(2)}) collective-permute-start(bf16[24,1728]{1,0:T(8,128)(2,1)S(1)} %shard_map.41.vectors_ref), channel_id=1, source_target_pairs={{8,16},{24,32},{40,48},{56,64},{72,80},{88,96},{104,112},{120,128}... | collective-permute-start | bytes 248840 | tf_op jit(solution)/shard_map/ppermute | solution.py:29
  3.0 0.0 copy-done
  3.0 0.7 %shard_map.42 = (f32[24,224]{1,0:T(8,128)S(1)}, bf16[24,2528]{1,0:T(8,128)(2,1)S(1)}) custom-call(bf16[24,1728]{1,0:T(8,128)(2,1)S(1)} %shard_map.41.vectors_ref, bf16[3,224,1728]{2,1,0:T(8,128)(2,1)S(1)} %bitcast.2), custom_call_target="tpu_custom_call" | custom-call | flops 7431782400 | bytes 1048576 | tf_op jit(solution)/shard_map/pallas_call | solution.py:262
  3.8 1.3 %collective-permute-start.1 = (f32[24,224]{1,0:T(8,128)S(1)}, f32[24,224]{1,0:T(8,128)S(1)}, u32[]{:S(2)}, u32[]{:S(2)}) collective-permute-start(f32[24,224]{1,0:T(8,128)S(1)} %get-tuple-element.19), channel_id=1, source_target_pairs={{8,16},{24,32},{40,48},{56,64},{72,80},{88,96},{104,112},{120,128}... | collective-permute-start | bytes 64520 | tf_op jit(solution)/shard_map/ppermute | solution.py:29
  5.1 4.2 %collective-permute-start = (bf16[24,2528]{1,0:T(8,128)(2,1)S(1)}, bf16[24,2528]{1,0:T(8,128)(2,1)S(1)}, u32[]{:S(2)}, u32[]{:S(2)}) collective-permute-start(bf16[24,2528]{1,0:T(8,128)(2,1)S(1)} %get-tuple-element.18), channel_id=1, source_target_pairs={{0,8},{16,24},{32,40},{48,56},{64,72},{80,88},{96,104},{112,120},{... | collective-permute-start | bytes 364040 | tf_op jit(solution)/shard_map/ppermute | solution.py:29
  9.3 8.1 %collective-permute-done.2.vectors_ref = bf16[24,1728]{1,0:T(8,128)(2,1)S(1)} collective-permute-done((bf16[24,1728]{1,0:T(8,128)(2,1)S(1)}, bf16[24,1728]{1,0:T(8,128)(2,1)S(1)}, u32[]{:S(2)}, u32[]{:S(2)}) %collective-permute-start.2) | collective-permute-done | bytes 82976 | tf_op jit(solution)/shard_map/ppermute | solution.py:29
  17.5 0.7 %shard_map.43.odd_images_ref = f32[24,224]{1,0:T(8,128)S(1)} custom-call(bf16[24,1728]{1,0:T(8,128)(2,1)S(1)} %collective-permute-done.2.vectors_ref, bf16[3,224,1728]{2,1,0:T(8,128)(2,1)S(1)} %bitcast.3), custom_call_target="tpu_custom_call" | custom-call | flops 7431782400 | bytes 1048576 | tf_op jit(solution)/shard_map/pallas_call | solution.py:262
  18.2 0.0 collective-permute-done.1.odd_left_ref
  18.2 0.0 collective-permute-done.even_message_ref
  18.3 10.8 %all_to_all.5.parts_ref = f32[8,24,224]{2,1,0:T(8,128)S(1)} all-to-all(f32[8,24,224]{2,1,0:T(8,128)S(1)} %broadcast_in_dim.2), channel_id=1, replica_groups=mesh['replica'=64,'tensor'=8] {'tensor'}, dimensions={0} | all-to-all | bytes 344064 | tf_op jit(solution)/shard_map/all_to_all | solution.py:311
  29.1 0.8 %shard_map.45 = (f32[24,224]{1,0:T(8,128)S(1)}, bf16[24,480]{1,0:T(8,128)(2,1)S(1)}, f32[24,1728]{1,0:T(8,128)S(1)}, bf16[24,2272]{1,0:T(8,128)(2,1)S(1)}) custom-call(f32[8,24,224]{2,1,0:T(8,128)S(1)} %all_to_all.5.parts_ref, bf16[3,224,1728]{2,1,0:T(8,128)(2,1)S(1)} %bitcast.5), custom_call_target="tpu_custom_call" | custom-call | flops 18579456 | bytes 1048576 | tf_op jit(solution)/shard_map/pallas_call | solution.py:262
  29.8 1.9 %collective-permute-start.4 = (bf16[24,480]{1,0:T(8,128)(2,1)S(1)}, bf16[24,480]{1,0:T(8,128)(2,1)S(1)}, u32[]{:S(2)}, u32[]{:S(2)}) collective-permute-start(bf16[24,480]{1,0:T(8,128)(2,1)S(1)} %get-tuple-element.24), channel_id=1, source_target_pairs={{0,504},{16,8},{32,24},{48,40},{64,56},{80,72},{96,88},{112,104},{... | collective-permute-start | bytes 69128 | tf_op jit(solution)/shard_map/ppermute | solution.py:29
  31.8 2.1 %collective-permute-start.3 = (bf16[24,2272]{1,0:T(8,128)(2,1)S(1)}, bf16[24,2272]{1,0:T(8,128)(2,1)S(1)}, u32[]{:S(2)}, u32[]{:S(2)}) collective-permute-start(bf16[24,2272]{1,0:T(8,128)(2,1)S(1)} %get-tuple-element.23), channel_id=1, source_target_pairs={{0,504},{8,0},{16,8},{24,16},{32,24},{40,32},{48,40},{56,48},{64,5... | collective-permute-start | bytes 327176 | tf_op jit(solution)/shard_map/ppermute | solution.py:17
  33.9 0.0 collective-permute-done.4.message_ref
  33.9 1.3 %collective-permute-start.5 = (bf16[24,1728]{1,0:T(8,128)(2,1)S(1)}, bf16[24,1728]{1,0:T(8,128)(2,1)S(1)}, u32[]{:S(2)}, u32[]{:S(2)}) collective-permute-start(bf16[24,1728]{1,0:T(8,128)(2,1)S(1)} %get-tuple-element.31), channel_id=1, source_target_pairs={{8,16},{24,32},{40,48},{56,64},{72,80},{88,96},{104,112},{120,128}... | collective-permute-start | bytes 248840 | tf_op jit(solution)/shard_map/ppermute | solution.py:29
  35.2 1.0 %collective-permute-done.3.message_ref = bf16[24,2272]{1,0:T(8,128)(2,1)S(1)} collective-permute-done((bf16[24,2272]{1,0:T(8,128)(2,1)S(1)}, bf16[24,2272]{1,0:T(8,128)(2,1)S(1)}, u32[]{:S(2)}, u32[]{:S(2)}) %collective-permute-start.3) | collective-permute-done | bytes 109088 | tf_op jit(solution)/shard_map/ppermute | solution.py:17
  36.2 0.4 shard_map.48
  36.6 1.3 %collective-permute-start.6 = (bf16[24,1728]{1,0:T(8,128)(2,1)S(1)}, bf16[24,1728]{1,0:T(8,128)(2,1)S(1)}, u32[]{:S(2)}, u32[]{:S(2)}) collective-permute-start(bf16[24,1728]{1,0:T(8,128)(2,1)S(1)} %get-tuple-element.32), channel_id=1, source_target_pairs={{0,8},{16,24},{32,40},{48,56},{64,72},{80,88},{96,104},{112,120},{... | collective-permute-start | bytes 248840 | tf_op jit(solution)/shard_map/ppermute | solution.py:29
  38.0 0.8 %shard_map.49 = (bf16[3,224,64]{2,1,0:T(8,128)(2,1)S(1)}, bf16[3,48,1728]{2,1,0:T(8,128)(2,1)S(1)}, f32[3,1,8,1728]{3,2,1,0:T(8,128)}) custom-call(bf16[24,2272]{1,0:T(8,128)(2,1)S(1)} %collective-permute-done.3.message_ref, f32[24,1728]{1,0:T(8,128)S(1)} %get-tuple-element.25.odd_products_ref, f32[24,1728]{1,0:T(8,128)S(1)} %get-tuple-element.26.even_products_ref, ...), custom_call_target="tpu_custom_call" | custom-call | flops 4644864 | bytes 1048576 | tf_op jit(solution)/shard_map/pallas_call | solution.py:262
  38.8 6.0 %collective-permute-done.5.odd_ref = bf16[24,1728]{1,0:T(8,128)(2,1)S(1)} collective-permute-done((bf16[24,1728]{1,0:T(8,128)(2,1)S(1)}, bf16[24,1728]{1,0:T(8,128)(2,1)S(1)}, u32[]{:S(2)}, u32[]{:S(2)}) %collective-permute-start.5) | collective-permute-done | bytes 82976 | tf_op jit(solution)/shard_map/ppermute | solution.py:29
  44.8 0.0 collective-permute-done.6.even_ref
  44.8 1.7 %shard_map.50 = bf16[3,1,224,1728]{3,2,1,0:T(8,128)(2,1)} custom-call(bf16[3,224,64]{2,1,0:T(8,128)(2,1)S(1)} %get-tuple-element.29.left_ref, bf16[3,48,1728]{2,1,0:T(8,128)(2,1)S(1)} %get-tuple-element.30.right_ref, bf16[24,1728]{1,0:T(8,128)(2,1)S(1)} %collective-permute-done.5.odd_ref, bf16[24,1728]{1,0:T(8,128)(2,1)S(1)} %collective-permute-done.6.even_ref, ...), custom_call_target="tpu_custom_call" | custom-call | flops 74317824 | bytes 1048576 | tf_op jit(solution)/shard_map/pallas_call | solution.py:262
  (4 shorter events, 0.1 us)
Async XLA Ops:
  0.6 2.4 %copy-start = (bf16[3,1,224,1728]{3,2,1,0:T(8,128)(2,1)S(1)}, bf16[3,1,224,1728]{3,2,1,0:T(8,128)(2,1)}, u32[]{:S(2)}) copy-start(bf16[3,1,224,1728]{3,2,1,0:T(8,128)(2,1)} %param.2) | copy-start | bytes 6967300
  1.7 15.7 %collective-permute-start.2 = (bf16[24,1728]{1,0:T(8,128)(2,1)S(1)}, bf16[24,1728]{1,0:T(8,128)(2,1)S(1)}, u32[]{:S(2)}, u32[]{:S(2)}) collective-permute-start(bf16[24,1728]{1,0:T(8,128)(2,1)S(1)} %shard_map.41.vectors_ref), channel_id=1, source_target_pairs={{8,16},{24,32},{40,48},{56,64},{72,80},{88,96},{104,112},{120,128}... | collective-permute-start | bytes 248840 | tf_op jit(solution)/shard_map/ppermute | solution.py:29
  3.8 14.4 %collective-permute-start.1 = (f32[24,224]{1,0:T(8,128)S(1)}, f32[24,224]{1,0:T(8,128)S(1)}, u32[]{:S(2)}, u32[]{:S(2)}) collective-permute-start(f32[24,224]{1,0:T(8,128)S(1)} %get-tuple-element.19), channel_id=1, source_target_pairs={{8,16},{24,32},{40,48},{56,64},{72,80},{88,96},{104,112},{120,128}... | collective-permute-start | bytes 64520 | tf_op jit(solution)/shard_map/ppermute | solution.py:29
  5.1 13.1 %collective-permute-start = (bf16[24,2528]{1,0:T(8,128)(2,1)S(1)}, bf16[24,2528]{1,0:T(8,128)(2,1)S(1)}, u32[]{:S(2)}, u32[]{:S(2)}) collective-permute-start(bf16[24,2528]{1,0:T(8,128)(2,1)S(1)} %get-tuple-element.18), channel_id=1, source_target_pairs={{0,8},{16,24},{32,40},{48,56},{64,72},{80,88},{96,104},{112,120},{... | collective-permute-start | bytes 364040 | tf_op jit(solution)/shard_map/ppermute | solution.py:29
  29.8 4.1 %collective-permute-start.4 = (bf16[24,480]{1,0:T(8,128)(2,1)S(1)}, bf16[24,480]{1,0:T(8,128)(2,1)S(1)}, u32[]{:S(2)}, u32[]{:S(2)}) collective-permute-start(bf16[24,480]{1,0:T(8,128)(2,1)S(1)} %get-tuple-element.24), channel_id=1, source_target_pairs={{0,504},{16,8},{32,24},{48,40},{64,56},{80,72},{96,88},{112,104},{... | collective-permute-start | bytes 69128 | tf_op jit(solution)/shard_map/ppermute | solution.py:29
  31.8 4.4 %collective-permute-start.3 = (bf16[24,2272]{1,0:T(8,128)(2,1)S(1)}, bf16[24,2272]{1,0:T(8,128)(2,1)S(1)}, u32[]{:S(2)}, u32[]{:S(2)}) collective-permute-start(bf16[24,2272]{1,0:T(8,128)(2,1)S(1)} %get-tuple-element.23), channel_id=1, source_target_pairs={{0,504},{8,0},{16,8},{24,16},{32,24},{40,32},{48,40},{56,48},{64,5... | collective-permute-start | bytes 327176 | tf_op jit(solution)/shard_map/ppermute | solution.py:17
  33.9 10.9 %collective-permute-start.5 = (bf16[24,1728]{1,0:T(8,128)(2,1)S(1)}, bf16[24,1728]{1,0:T(8,128)(2,1)S(1)}, u32[]{:S(2)}, u32[]{:S(2)}) collective-permute-start(bf16[24,1728]{1,0:T(8,128)(2,1)S(1)} %get-tuple-element.31), channel_id=1, source_target_pairs={{8,16},{24,32},{40,48},{56,64},{72,80},{88,96},{104,112},{120,128}... | collective-permute-start | bytes 248840 | tf_op jit(solution)/shard_map/ppermute | solution.py:29
  36.6 8.2 %collective-permute-start.6 = (bf16[24,1728]{1,0:T(8,128)(2,1)S(1)}, bf16[24,1728]{1,0:T(8,128)(2,1)S(1)}, u32[]{:S(2)}, u32[]{:S(2)}) collective-permute-start(bf16[24,1728]{1,0:T(8,128)(2,1)S(1)} %get-tuple-element.32), channel_id=1, source_target_pairs={{0,8},{16,24},{32,40},{48,56},{64,72},{80,88},{96,104},{112,120},{... | collective-permute-start | bytes 248840 | tf_op jit(solution)/shard_map/ppermute | solution.py:29

commit v9 on v8

--- a/solution.py
+++ b/solution.py
@@ -245,8 +245,8 @@
             held_ref[mat, :, start:stop] = (window_ref[mat, :, start:stop].astype(jnp.float32) + change).astype(
                 jnp.bfloat16
             )
-            if stop % (2 * width) == 0 or stop == columns:
-                piece = slice(start // (2 * width) * (2 * width), stop)
+            if stop % width == 0 or stop == columns:
+                piece = slice(start, stop)
                 copies.append(
                     pltpu.make_async_copy(
                         held_ref.at[mat, :, piece], updated_ref.at[mat, 0, :, piece], sems.at[len(copies)]
@@ -351,7 +351,7 @@
         whole(bf16, mats, 1, row_count, columns),
         4 * flops,
         out_specs=pl.BlockSpec(memory_space=pl.ANY),
-        scratch_shapes=[pltpu.VMEM((mats, row_count, columns), bf16), pltpu.SemaphoreType.DMA((mats * (-(-columns // (4 * LANES))),))],
+        scratch_shapes=[pltpu.VMEM((mats, row_count, columns), bf16), pltpu.SemaphoreType.DMA((mats * (-(-columns // (2 * LANES))),))],
     )(left, right, odd_previous, even_previous, window)
     return (updated, factors)
 

time: 46.8 us -> 46.9 us (level)
  no operation moved by 1% of the time
where the time goes in v9:
time: 46.9 us; the launch traced here: 46.6 us
  waiting for transfers between devices  15.1 us (32%)
  starting transfers between devices  13.4 us (29%)
  blocking collectives  10.8 us (23%)
  Pallas kernels  6.43 us (14%)
  between operations  0.76 us (2%)
    ppermute x6, waiting for transfers between devices, over(): return lambda value: lax.ppermute(value, axis, pairs)  14.2 us
    ppermute x6, starting transfers between devices, over(): return lambda value: lax.ppermute(value, axis, pairs)  11.4 us
    all_to_all x1, blocking collectives, shards(): lax.all_to_all(jnp.broadcast_to(differences[None], (group, stacked, row_c...  10.8 us
    pallas_call x10, Pallas kernels, run(): pl.pallas_call(kernel, out_shape=outs, in_specs=[IN_VMEM] * len(operands)...  6.43 us
    ppermute x1, starting transfers between devices, shifted(): lax.ppermute(value, axis, [(source, (source + steps) % count) for source...  2.07 us
    ppermute x1, waiting for transfers between devices, shifted(): lax.ppermute(value, axis, [(source, (source + steps) % count) for source...  0.97 us
  transfers between devices with their start and end apart: 7, of which 3 were waited for; matrix products, arithmetic and copies ran while one was open for 0% of the time, Pallas kernels for 6%

profile of v9, /device:TPU:2, one launch (start us, length us, event | category | flops | bytes accessed | tf_op | source)
XLA Modules:
  0.0 46.6 jit_solution(11860438570023642552)
XLA Ops:
  0.6 0.0 copy-start
  0.6 1.1 %shard_map.41.vectors_ref = bf16[24,1728]{1,0:T(8,128)(2,1)S(1)} custom-call(f32[3,8,1728]{2,1,0:T(8,128)} %bitcast.10), custom_call_target="tpu_custom_call" | custom-call | flops 1857945600 | bytes 1048576 | tf_op jit(solution)/shard_map/pallas_call | solution.py:262
  1.7 1.3 %collective-permute-start.2 = (bf16[24,1728]{1,0:T(8,128)(2,1)S(1)}, bf16[24,1728]{1,0:T(8,128)(2,1)S(1)}, u32[]{:S(2)}, u32[]{:S(2)}) collective-permute-start(bf16[24,1728]{1,0:T(8,128)(2,1)S(1)} %shard_map.41.vectors_ref), channel_id=1, source_target_pairs={{8,16},{24,32},{40,48},{56,64},{72,80},{88,96},{104,112},{120,128}... | collective-permute-start | bytes 248840 | tf_op jit(solution)/shard_map/ppermute | solution.py:29
  3.0 0.0 copy-done
  3.0 0.7 %shard_map.42 = (f32[24,224]{1,0:T(8,128)S(1)}, bf16[24,2528]{1,0:T(8,128)(2,1)S(1)}) custom-call(bf16[24,1728]{1,0:T(8,128)(2,1)S(1)} %shard_map.41.vectors_ref, bf16[3,224,1728]{2,1,0:T(8,128)(2,1)S(1)} %bitcast.2), custom_call_target="tpu_custom_call" | custom-call | flops 7431782400 | bytes 1048576 | tf_op jit(solution)/shard_map/pallas_call | solution.py:262
  3.8 1.3 %collective-permute-start.1 = (f32[24,224]{1,0:T(8,128)S(1)}, f32[24,224]{1,0:T(8,128)S(1)}, u32[]{:S(2)}, u32[]{:S(2)}) collective-permute-start(f32[24,224]{1,0:T(8,128)S(1)} %get-tuple-element.19), channel_id=1, source_target_pairs={{8,16},{24,32},{40,48},{56,64},{72,80},{88,96},{104,112},{120,128}... | collective-permute-start | bytes 64520 | tf_op jit(solution)/shard_map/ppermute | solution.py:29
  5.1 4.2 %collective-permute-start = (bf16[24,2528]{1,0:T(8,128)(2,1)S(1)}, bf16[24,2528]{1,0:T(8,128)(2,1)S(1)}, u32[]{:S(2)}, u32[]{:S(2)}) collective-permute-start(bf16[24,2528]{1,0:T(8,128)(2,1)S(1)} %get-tuple-element.18), channel_id=1, source_target_pairs={{0,8},{16,24},{32,40},{48,56},{64,72},{80,88},{96,104},{112,120},{... | collective-permute-start | bytes 364040 | tf_op jit(solution)/shard_map/ppermute | solution.py:29
  9.3 8.1 %collective-permute-done.2.vectors_ref = bf16[24,1728]{1,0:T(8,128)(2,1)S(1)} collective-permute-done((bf16[24,1728]{1,0:T(8,128)(2,1)S(1)}, bf16[24,1728]{1,0:T(8,128)(2,1)S(1)}, u32[]{:S(2)}, u32[]{:S(2)}) %collective-permute-start.2) | collective-permute-done | bytes 82976 | tf_op jit(solution)/shard_map/ppermute | solution.py:29
  17.5 0.7 %shard_map.43.odd_images_ref = f32[24,224]{1,0:T(8,128)S(1)} custom-call(bf16[24,1728]{1,0:T(8,128)(2,1)S(1)} %collective-permute-done.2.vectors_ref, bf16[3,224,1728]{2,1,0:T(8,128)(2,1)S(1)} %bitcast.3), custom_call_target="tpu_custom_call" | custom-call | flops 7431782400 | bytes 1048576 | tf_op jit(solution)/shard_map/pallas_call | solution.py:262
  18.2 0.0 collective-permute-done.1.odd_left_ref
  18.2 0.0 collective-permute-done.even_message_ref
  18.3 10.8 %all_to_all.5.parts_ref = f32[8,24,224]{2,1,0:T(8,128)S(1)} all-to-all(f32[8,24,224]{2,1,0:T(8,128)S(1)} %broadcast_in_dim.2), channel_id=1, replica_groups=mesh['replica'=64,'tensor'=8] {'tensor'}, dimensions={0} | all-to-all | bytes 344064 | tf_op jit(solution)/shard_map/all_to_all | solution.py:311
  29.1 0.8 %shard_map.45 = (f32[24,224]{1,0:T(8,128)S(1)}, bf16[24,480]{1,0:T(8,128)(2,1)S(1)}, f32[24,1728]{1,0:T(8,128)S(1)}, bf16[24,2272]{1,0:T(8,128)(2,1)S(1)}) custom-call(f32[8,24,224]{2,1,0:T(8,128)S(1)} %all_to_all.5.parts_ref, bf16[3,224,1728]{2,1,0:T(8,128)(2,1)S(1)} %bitcast.5), custom_call_target="tpu_custom_call" | custom-call | flops 18579456 | bytes 1048576 | tf_op jit(solution)/shard_map/pallas_call | solution.py:262
  29.8 1.9 %collective-permute-start.4 = (bf16[24,480]{1,0:T(8,128)(2,1)S(1)}, bf16[24,480]{1,0:T(8,128)(2,1)S(1)}, u32[]{:S(2)}, u32[]{:S(2)}) collective-permute-start(bf16[24,480]{1,0:T(8,128)(2,1)S(1)} %get-tuple-element.24), channel_id=1, source_target_pairs={{0,504},{16,8},{32,24},{48,40},{64,56},{80,72},{96,88},{112,104},{... | collective-permute-start | bytes 69128 | tf_op jit(solution)/shard_map/ppermute | solution.py:29
  31.8 2.1 %collective-permute-start.3 = (bf16[24,2272]{1,0:T(8,128)(2,1)S(1)}, bf16[24,2272]{1,0:T(8,128)(2,1)S(1)}, u32[]{:S(2)}, u32[]{:S(2)}) collective-permute-start(bf16[24,2272]{1,0:T(8,128)(2,1)S(1)} %get-tuple-element.23), channel_id=1, source_target_pairs={{0,504},{8,0},{16,8},{24,16},{32,24},{40,32},{48,40},{56,48},{64,5... | collective-permute-start | bytes 327176 | tf_op jit(solution)/shard_map/ppermute | solution.py:17
  33.9 0.0 collective-permute-done.4.message_ref
  33.9 1.3 %collective-permute-start.5 = (bf16[24,1728]{1,0:T(8,128)(2,1)S(1)}, bf16[24,1728]{1,0:T(8,128)(2,1)S(1)}, u32[]{:S(2)}, u32[]{:S(2)}) collective-permute-start(bf16[24,1728]{1,0:T(8,128)(2,1)S(1)} %get-tuple-element.31), channel_id=1, source_target_pairs={{8,16},{24,32},{40,48},{56,64},{72,80},{88,96},{104,112},{120,128}... | collective-permute-start | bytes 248840 | tf_op jit(solution)/shard_map/ppermute | solution.py:29
  35.2 1.0 %collective-permute-done.3.message_ref = bf16[24,2272]{1,0:T(8,128)(2,1)S(1)} collective-permute-done((bf16[24,2272]{1,0:T(8,128)(2,1)S(1)}, bf16[24,2272]{1,0:T(8,128)(2,1)S(1)}, u32[]{:S(2)}, u32[]{:S(2)}) %collective-permute-start.3) | collective-permute-done | bytes 109088 | tf_op jit(solution)/shard_map/ppermute | solution.py:17
  36.2 0.4 shard_map.48
  36.6 1.3 %collective-permute-start.6 = (bf16[24,1728]{1,0:T(8,128)(2,1)S(1)}, bf16[24,1728]{1,0:T(8,128)(2,1)S(1)}, u32[]{:S(2)}, u32[]{:S(2)}) collective-permute-start(bf16[24,1728]{1,0:T(8,128)(2,1)S(1)} %get-tuple-element.32), channel_id=1, source_target_pairs={{0,8},{16,24},{32,40},{48,56},{64,72},{80,88},{96,104},{112,120},{... | collective-permute-start | bytes 248840 | tf_op jit(solution)/shard_map/ppermute | solution.py:29
  38.0 0.8 %shard_map.49 = (bf16[3,224,64]{2,1,0:T(8,128)(2,1)S(1)}, bf16[3,48,1728]{2,1,0:T(8,128)(2,1)S(1)}, f32[3,1,8,1728]{3,2,1,0:T(8,128)}) custom-call(bf16[24,2272]{1,0:T(8,128)(2,1)S(1)} %collective-permute-done.3.message_ref, f32[24,1728]{1,0:T(8,128)S(1)} %get-tuple-element.25.odd_products_ref, f32[24,1728]{1,0:T(8,128)S(1)} %get-tuple-element.26.even_products_ref, ...), custom_call_target="tpu_custom_call" | custom-call | flops 4644864 | bytes 1048576 | tf_op jit(solution)/shard_map/pallas_call | solution.py:262
  38.8 6.0 %collective-permute-done.5.odd_ref = bf16[24,1728]{1,0:T(8,128)(2,1)S(1)} collective-permute-done((bf16[24,1728]{1,0:T(8,128)(2,1)S(1)}, bf16[24,1728]{1,0:T(8,128)(2,1)S(1)}, u32[]{:S(2)}, u32[]{:S(2)}) %collective-permute-start.5) | collective-permute-done | bytes 82976 | tf_op jit(solution)/shard_map/ppermute | solution.py:29
  44.8 0.0 collective-permute-done.6.even_ref
  44.8 1.8 %shard_map.50 = bf16[3,1,224,1728]{3,2,1,0:T(8,128)(2,1)} custom-call(bf16[3,224,64]{2,1,0:T(8,128)(2,1)S(1)} %get-tuple-element.29.left_ref, bf16[3,48,1728]{2,1,0:T(8,128)(2,1)S(1)} %get-tuple-element.30.right_ref, bf16[24,1728]{1,0:T(8,128)(2,1)S(1)} %collective-permute-done.5.odd_ref, bf16[24,1728]{1,0:T(8,128)(2,1)S(1)} %collective-permute-done.6.even_ref, ...), custom_call_target="tpu_custom_call" | custom-call | flops 74317824 | bytes 1048576 | tf_op jit(solution)/shard_map/pallas_call | solution.py:262
  (4 shorter events, 0.1 us)
Async XLA Ops:
  0.6 2.4 %copy-start = (bf16[3,1,224,1728]{3,2,1,0:T(8,128)(2,1)S(1)}, bf16[3,1,224,1728]{3,2,1,0:T(8,128)(2,1)}, u32[]{:S(2)}) copy-start(bf16[3,1,224,1728]{3,2,1,0:T(8,128)(2,1)} %param.2) | copy-start | bytes 6967300
  1.7 15.7 %collective-permute-start.2 = (bf16[24,1728]{1,0:T(8,128)(2,1)S(1)}, bf16[24,1728]{1,0:T(8,128)(2,1)S(1)}, u32[]{:S(2)}, u32[]{:S(2)}) collective-permute-start(bf16[24,1728]{1,0:T(8,128)(2,1)S(1)} %shard_map.41.vectors_ref), channel_id=1, source_target_pairs={{8,16},{24,32},{40,48},{56,64},{72,80},{88,96},{104,112},{120,128}... | collective-permute-start | bytes 248840 | tf_op jit(solution)/shard_map/ppermute | solution.py:29
  3.8 14.4 %collective-permute-start.1 = (f32[24,224]{1,0:T(8,128)S(1)}, f32[24,224]{1,0:T(8,128)S(1)}, u32[]{:S(2)}, u32[]{:S(2)}) collective-permute-start(f32[24,224]{1,0:T(8,128)S(1)} %get-tuple-element.19), channel_id=1, source_target_pairs={{8,16},{24,32},{40,48},{56,64},{72,80},{88,96},{104,112},{120,128}... | collective-permute-start | bytes 64520 | tf_op jit(solution)/shard_map/ppermute | solution.py:29
  5.1 13.1 %collective-permute-start = (bf16[24,2528]{1,0:T(8,128)(2,1)S(1)}, bf16[24,2528]{1,0:T(8,128)(2,1)S(1)}, u32[]{:S(2)}, u32[]{:S(2)}) collective-permute-start(bf16[24,2528]{1,0:T(8,128)(2,1)S(1)} %get-tuple-element.18), channel_id=1, source_target_pairs={{0,8},{16,24},{32,40},{48,56},{64,72},{80,88},{96,104},{112,120},{... | collective-permute-start | bytes 364040 | tf_op jit(solution)/shard_map/ppermute | solution.py:29
  29.8 4.1 %collective-permute-start.4 = (bf16[24,480]{1,0:T(8,128)(2,1)S(1)}, bf16[24,480]{1,0:T(8,128)(2,1)S(1)}, u32[]{:S(2)}, u32[]{:S(2)}) collective-permute-start(bf16[24,480]{1,0:T(8,128)(2,1)S(1)} %get-tuple-element.24), channel_id=1, source_target_pairs={{0,504},{16,8},{32,24},{48,40},{64,56},{80,72},{96,88},{112,104},{... | collective-permute-start | bytes 69128 | tf_op jit(solution)/shard_map/ppermute | solution.py:29
  31.8 4.4 %collective-permute-start.3 = (bf16[24,2272]{1,0:T(8,128)(2,1)S(1)}, bf16[24,2272]{1,0:T(8,128)(2,1)S(1)}, u32[]{:S(2)}, u32[]{:S(2)}) collective-permute-start(bf16[24,2272]{1,0:T(8,128)(2,1)S(1)} %get-tuple-element.23), channel_id=1, source_target_pairs={{0,504},{8,0},{16,8},{24,16},{32,24},{40,32},{48,40},{56,48},{64,5... | collective-permute-start | bytes 327176 | tf_op jit(solution)/shard_map/ppermute | solution.py:17
  33.9 10.9 %collective-permute-start.5 = (bf16[24,1728]{1,0:T(8,128)(2,1)S(1)}, bf16[24,1728]{1,0:T(8,128)(2,1)S(1)}, u32[]{:S(2)}, u32[]{:S(2)}) collective-permute-start(bf16[24,1728]{1,0:T(8,128)(2,1)S(1)} %get-tuple-element.31), channel_id=1, source_target_pairs={{8,16},{24,32},{40,48},{56,64},{72,80},{88,96},{104,112},{120,128}... | collective-permute-start | bytes 248840 | tf_op jit(solution)/shard_map/ppermute | solution.py:29
  36.6 8.2 %collective-permute-start.6 = (bf16[24,1728]{1,0:T(8,128)(2,1)S(1)}, bf16[24,1728]{1,0:T(8,128)(2,1)S(1)}, u32[]{:S(2)}, u32[]{:S(2)}) collective-permute-start(bf16[24,1728]{1,0:T(8,128)(2,1)S(1)} %get-tuple-element.32), channel_id=1, source_target_pairs={{0,8},{16,24},{32,40},{48,56},{64,72},{80,88},{96,104},{112,120},{... | collective-permute-start | bytes 248840 | tf_op jit(solution)/shard_map/ppermute | solution.py:29
